TPU v7x, 32 devices: a whole 2x2x4 slice. The times are simulated.
32 devices in a mesh: wide: 8 (over z, x), narrow: 4 (over y, core).
Axes of the slice: x: 2, y: 2, z: 4, core: 2. Of those that a mesh axis runs over, the one named last changes fastest.
Arguments:
- inputs: bfloat16 [16384, 768], P(('wide', 'narrow')), may hold values from -6 to 6
- segment_ids: int32 [64, 256], P(('wide', 'narrow')), may hold values from 0 to 9, as said below
- pre_attn_gain: bfloat16 [768], P(('wide', 'narrow')), may hold values from 0.5 to 1.5
- pre_attn_bias: bfloat16 [768], P(('wide', 'narrow')), may hold values from -2 to 2
- w_qkv: bfloat16 [768, 2304], P(('wide', 'narrow')), may hold values from -0.21875 to 0.21875
- b_query: bfloat16 [768], P(('wide', 'narrow')), may hold values from -2 to 2
- b_value: bfloat16 [768], P(('wide', 'narrow')), may hold values from -2 to 2
- w_out: bfloat16 [768, 768], P(('wide', 'narrow')), may hold values from -0.875 to 0.875
- b_out: bfloat16 [768], P(('wide', 'narrow')), may hold values from -2 to 2
- pre_mlp_gain: bfloat16 [768], P(('wide', 'narrow')), may hold values from 0.5 to 1.5
- pre_mlp_bias: bfloat16 [768], P(('wide', 'narrow')), may hold values from -2 to 2
- w_up: bfloat16 [768, 3072], P(('wide', 'narrow')), may hold values from -0.21875 to 0.21875
- b_up: bfloat16 [3072], P(('wide', 'narrow')), may hold values from -2 to 2
- w_down: bfloat16 [3072, 768], P(('wide', 'narrow')), may hold values from -0.109375 to 0.109375
- b_down: bfloat16 [768], P(('wide', 'narrow')), may hold values from -2 to 2
- cotangent: bfloat16 [16384, 768], P(('wide', 'narrow')), may hold values from -6 to 6
Outputs:
- layer_out: bfloat16 [16384, 768], P(('wide', 'narrow'))
- input_grad: bfloat16 [16384, 768], P(('wide', 'narrow'))
- grad_attn_gain: float32 [768], P(('wide', 'narrow'))
- grad_attn_shift: float32 [768], P(('wide', 'narrow'))
- grad_w_qkv: float32 [768, 2304], P(('wide', 'narrow'))
- grad_b_query: float32 [768], P(('wide', 'narrow'))
- grad_b_value: float32 [768], P(('wide', 'narrow'))
- grad_w_out: float32 [768, 768], P(('wide', 'narrow'))
- grad_b_out: float32 [768], P(('wide', 'narrow'))
- grad_mlp_gain: float32 [768], P(('wide', 'narrow'))
- grad_mlp_shift: float32 [768], P(('wide', 'narrow'))
- grad_w_up: float32 [768, 3072], P(('wide', 'narrow'))
- grad_b_up: float32 [3072], P(('wide', 'narrow'))
- grad_w_down: float32 [3072, 768], P(('wide', 'narrow'))
- grad_b_down: float32 [768], P(('wide', 'narrow'))
Inputs may be any that keep to these rules, and one draw needn't show every extreme that they name: `segment_ids`: in every row of 256 positions the ids count up from 1 without falling, one id for each caption of 1 to 64 positions, the first caption of each row has exactly 64; the last 1 to 8 positions of every row are 0 (padding). Ids are compared only within a row.
All inputs are finite; a program needn't handle non-finite values.
Results may differ from a plain program's by a relative error of at most 0.012.
The roundings to bfloat16 on the way count: a program that leaves them out, or rounds other values in their place, can miss the bound.
Values may be sent and summed in bfloat16 or wider, within the bound.
No kernel may reach another device: no remote copies, remote signals or barrier semaphores. Data moves between devices by JAX's collectives and lax.ppermute only.
A program may use at most 128 MiB of HBM per device.

v0:
```python
import functools
import math

import jax
import jax.numpy as jnp
from jax import lax
from jax.experimental import pallas as pl
from jax.experimental.pallas import tpu as pltpu
from jax.sharding import PartitionSpec as P

HEADS = 12
HEAD_DIM = 64
D = 768
FF = 3072
ROW_LEN = 256
HALF = 384
CHIPS = 16
BLK = 48
PAIRS = HEADS // 2
AXES = ("wide", "narrow")

EPS = 1e-06
MASKED = -1e30
F32 = jnp.float32
BF16 = jnp.bfloat16

BIT_Y, BIT_X, BIT_Z0, BIT_Z1 = 1, 2, 4, 8
Z_OFFSETS = (0, 4, 8, 12)

GATHER = tuple((o + z, o + z + BIT_Z1) for o in (0, BIT_Y, BIT_X, BIT_X + BIT_Y) for z in (0, BIT_Z0))
PIECES = 2 * len(GATHER)

SCATTER = (0, 8, 4, 12, 1, 9, 6, 14, 5, 13, 7, 15, 2, 10, 3, 11)


def nt(a, b):
    return lax.dot_general(a, b, (((1,), (1,)), ((), ())), preferred_element_type=F32)


def tn(a, b):
    return lax.dot_general(a, b, (((0,), (0,)), ((), ())), preferred_element_type=F32)


def nn(a, b):
    return lax.dot_general(a, b, (((1,), (0,)), ((), ())), preferred_element_type=F32)


def chunks(tokens, step, body):
    def one(i, carry):
        body(pl.ds(pl.multiple_of(i * step, step), step))
        return carry

    lax.fori_loop(0, tokens // step, one, 0)


def norm_parts(v):
    centre = jnp.mean(v, axis=-1, keepdims=True)
    centred = v - centre
    scale = lax.rsqrt(jnp.mean(centred * centred, axis=-1, keepdims=True) + EPS)
    return centred * scale, scale


def start(src, dst, sem):
    copy = pltpu.make_async_copy(src, dst, sem)
    copy.start()
    return copy


def whole_wait(ref, sem):
    pltpu.make_async_copy(ref, ref, sem).wait()


def each_block(pos_ref, pieces):
    for other in range(2):
        for ref, offsets in zip(pieces[other * len(GATHER) :], GATHER):
            for b, offset in enumerate(offsets):
                yield ref, b, pos_ref[0] ^ offset, other, offset


def chip_rows(chip, size):
    return pl.ds(pl.multiple_of(chip * size, 16), size)


def half_cols(pos_ref, other):
    return pl.ds(pl.multiple_of((pos_ref[1] ^ other) * HALF, 128), HALF)


def fetch_qkv(pos_ref, pieces, w_qkv, sems):
    for t in range(3):
        for ref, b, chip, other, _ in each_block(pos_ref, pieces):
            dst = w_qkv.at[t, chip_rows(chip, BLK), half_cols(pos_ref, other)]
            start(ref.at[b, pl.ds(t * BLK, BLK)], dst, sems.at[t])


def fetch_out(pos_ref, pieces, w_out, sem):
    for ref, b, chip, other, _ in each_block(pos_ref, pieces):
        dst = w_out.at[chip_rows(chip, BLK), half_cols(pos_ref, other)]
        start(ref.at[b, 4], dst, sem)


def fetch_small(pos_ref, pieces, small, sem):
    for ref, b, chip, other, _ in each_block(pos_ref, pieces):
        start(ref.at[b, pl.ds(3 * BLK, 16)], small.at[pos_ref[1] ^ other, chip], sem)


def fetch_up(pos_ref, pieces, w_up, sems):
    for ref, b, chip, other, _ in each_block(pos_ref, pieces):
        for u in range(2):
            dst = w_up.at[other, pl.ds(0, 2), chip_rows(chip, BLK), pl.ds(u * HALF, HALF)]
            start(ref.at[b, pl.ds(2 * u, 2)], dst, sems.at[other])


def fetch_down(pos_ref, pieces, w_down, sems):
    for q in range(4):
        for ref, b, chip, other, offset in each_block(pos_ref, pieces):
            if offset // 4 == q:
                dst = w_down.at[chip_rows(chip, 4 * BLK), half_cols(pos_ref, other)]
                start(ref.at[b], dst, sems.at[q])


def scatter_place(pos_ref, chip):
    offset = pos_ref[0] ^ chip
    xy, z = offset & 3, ((offset >> 2) & 1) * 2 + (offset >> 3)
    near = jnp.where(xy == 1, 4, jnp.where(xy == 2, 12, 14)) + z
    far = jnp.where(xy == 1, 6, jnp.where(xy == 2, 4, 8)) + z
    return jnp.where(xy == 0, z, jnp.where(z < 2, near, far))


def head_masks():
    lane = lax.broadcasted_iota(jnp.int32, (1, 2 * HEAD_DIM), 1)
    return [(lane // HEAD_DIM == hh).astype(F32).astype(BF16) for hh in range(2)]


def pair_cols(t, i):
    return pl.ds(pl.multiple_of(t * D + i * 128, 128), 128)


def attn_forward_kernel(pos_ref, segr_ref, segc_ref, x_any, *refs):
    pieces, refs = refs[:PIECES], refs[PIECES:]
    vec_ref, n1_ref, qkv_ref, soft_ref, mixed_ref, w_qkv, x_ref, small, bias, sems = refs
    tokens = x_ref.shape[0]
    n_rows = tokens // ROW_LEN
    load_x = start(x_any, x_ref, sems.at[4])
    fetch_small(pos_ref, pieces, small, sems.at[0])
    fetch_qkv(pos_ref, pieces, w_qkv, sems.at[pl.ds(1, 3)])
    for r in range(n_rows):
        same = segc_ref[r * ROW_LEN : (r + 1) * ROW_LEN] == segr_ref[r]
        bias[r] = jnp.where(same, 0.0, MASKED)
    whole_wait(small, sems.at[0])
    for h in range(2):
        vec_ref[:, h * HALF : (h + 1) * HALF] = jnp.sum(small[h].astype(F32), axis=0)
    load_x.wait()

    def norm_one(rows):
        xhat, _ = norm_parts(x_ref[rows, :].astype(F32))
        n1_ref[rows, :] = (xhat * vec_ref[0:1, :] + vec_ref[1:2, :]).astype(BF16)

    chunks(tokens, 128, norm_one)
    for t in range(3):
        whole_wait(w_qkv.at[t], sems.at[1 + t])
        y = (nn(n1_ref[...], w_qkv[t]) + vec_ref[2 + t : 3 + t, :]).astype(BF16)
        if t == 0:
            y = y * BF16(HEAD_DIM**-0.5)
        qkv_ref[:, t * D : (t + 1) * D] = y
    masks = head_masks()
    for r in range(n_rows):
        rows = slice(r * ROW_LEN, (r + 1) * ROW_LEN)

        def pair(i, carry):
            q, k, v = (qkv_ref[rows, pair_cols(t, i)] for t in range(3))
            mixed = jnp.zeros((ROW_LEN, 128), F32)
            for hh, keep in enumerate(masks):
                s = nt(q, k * keep) + bias[r]
                e = jnp.exp(s - jnp.max(s, axis=-1, keepdims=True))
                p = (e * (1.0 / jnp.sum(e, axis=-1, keepdims=True))).astype(BF16)
                soft_ref[r * HEADS + 2 * i + hh] = p
                mixed = mixed + nn(p, v * keep)
            mixed_ref[rows, pair_cols(0, i)] = mixed.astype(BF16)
            return carry

        lax.fori_loop(0, PAIRS, pair, 0)


GELU_A = 0.7978845608028654
GELU_B = 0.044715


def quarter(pos_ref, other, s):
    return (pos_ref[1] ^ other) * 2 + s


def quarter_cols(z):
    return pl.ds(pl.multiple_of(z * D, 128), D)


QUARTERS = ((0, 0), (0, 1), (1, 0), (1, 1))


def mlp_up_kernel(pos_ref, segc_ref, vec_ref, mixed_ref, x_any, cot_any, *refs):
    pieces, refs = refs[:PIECES], refs[PIECES:]
    gb_ref, n2_ref, mid_ref, act_ref, slope_ref, gout_ref, w_out, w_up, x_ref, cot_ref, sems = refs
    tokens = n2_ref.shape[0]
    load_cot = start(cot_any, cot_ref, sems.at[3])
    load_x = start(x_any, x_ref, sems.at[4])
    fetch_out(pos_ref, pieces, w_out, sems.at[2])
    fetch_up(pos_ref, pieces, w_up, sems)
    load_cot.wait()
    valid = segc_ref[...] > 0
    gout = jnp.where(valid, cot_ref[...].astype(F32), 0.0)
    gout_ref[...] = gout.astype(BF16)
    gb_ref[...] = jnp.broadcast_to(jnp.sum(gout, axis=0, keepdims=True), gb_ref.shape)
    load_x.wait()
    whole_wait(w_out, sems.at[2])
    mid_ref[...] = x_ref[...].astype(F32) + nn(mixed_ref[...], w_out[...]) + vec_ref[5:6, :]

    def norm_two(rows):
        xhat, _ = norm_parts(mid_ref[rows, :])
        n2_ref[rows, :] = (xhat * vec_ref[6:7, :] + vec_ref[7:8, :]).astype(BF16)

    chunks(tokens, 128, norm_two)
    for other, s in QUARTERS:
        if s == 0:
            whole_wait(w_up.at[other], sems.at[other])
        z = quarter(pos_ref, other, s)
        b_up = vec_ref[pl.ds(8 + z, 1), :]
        cols = quarter_cols(z)

        def part(rows):
            u = nn(n2_ref[rows, :], w_up[other, s]) + b_up
            sq = u * u
            t = jnp.tanh(u * (GELU_A + GELU_A * GELU_B * sq))
            half_up = 0.5 + 0.5 * t
            act_ref[rows, cols] = (u * half_up).astype(BF16)
            slope_ref[rows, cols] = (
                half_up + u * (0.5 - 0.5 * t * t) * (GELU_A + 3.0 * GELU_A * GELU_B * sq)
            ).astype(BF16)

        chunks(tokens, 256, part)


def down_grad_kernel(pos_ref, act_ref, gout_ref, mine, theirs, grad, sem):
    for z in range(4):
        grad[z] = tn(act_ref[:, z * D : (z + 1) * D], gout_ref[...]).astype(BF16)
        for j in range(4):
            place = scatter_place(pos_ref, 4 * z + j)
            for other, out in enumerate((mine, theirs)):
                src = grad.at[z, pl.ds(j * 4 * BLK, 4 * BLK), half_cols(pos_ref, other)]
                start(src, out.at[place], sem.at[0])
    whole_wait(grad, sem.at[0])


def mlp_down_kernel(pos_ref, gout_ref, slope_ref, n2_ref, *refs):
    pieces, refs = refs[:PIECES], refs[PIECES:]
    gb_ref, gpre_ref, w_down, mine, theirs, n2t, grad, sems = refs
    fetch_down(pos_ref, pieces, w_down, sems)
    gb_ref[...] = jnp.zeros(gb_ref.shape, F32)
    n2t[...] = n2_ref[...].T
    for other, s in QUARTERS:
        z = quarter(pos_ref, other, s)
        cols = quarter_cols(z)
        whole_wait(w_down.at[cols], sems.at[z ^ (pos_ref[0] >> 2)])
        ga = nt(gout_ref[...], w_down[cols, :])
        gp = (ga * slope_ref[:, cols].astype(F32)).astype(BF16)
        gpre_ref[:, cols] = gp
        gb_ref[pl.ds(z, 1), :] = jnp.sum(gp.astype(F32), axis=0, keepdims=True)
        grad[other, s] = nn(n2t[...], gp).astype(BF16)
        if s == 1:
            for chip in range(CHIPS):
                place = scatter_place(pos_ref, chip)
                for u in range(2):
                    src = grad.at[other, pl.ds(0, 2), pl.ds(chip * BLK, BLK), pl.ds(u * HALF, HALF)]
                    start(src, (mine, theirs)[other].at[place, pl.ds(2 * u, 2)], sems.at[4])
    whole_wait(grad, sems.at[4])


def norm_back(grad, xhat, scale, gain):
    gn = grad * gain
    mean_gn = jnp.mean(gn, axis=-1, keepdims=True)
    mean_gx = jnp.mean(gn * xhat, axis=-1, keepdims=True)
    return scale * (gn - mean_gn - xhat * mean_gx)


def mid_backward_kernel(
    pos_ref, vec_ref, gbd_ref, gbu_ref, gpre_ref, gout_ref, mid_ref, mixed_ref, w_out, w_up, _, __,
    sums, gmid, gmixed, mine, theirs, acc, gbr, mixt, grad, sem,
):
    tokens = mid_ref.shape[0]
    sums[...] = jnp.zeros(sums.shape, F32)
    sums[8:12, :] = gbu_ref[0:4, :]
    sums[12:13, :] = gbd_ref[0:1, :]
    mixt[...] = mixed_ref[...].T
    for other, s in QUARTERS:
        part = nt(gpre_ref[:, quarter_cols(quarter(pos_ref, other, s))], w_up[other, s])
        acc[...] = part if other + s == 0 else acc[...] + part

    def back_two(rows):
        xhat, scale = norm_parts(mid_ref[rows, :])
        g = acc[rows, :]
        sums[6:7, :] += jnp.sum(g * xhat, axis=0, keepdims=True)
        sums[7:8, :] += jnp.sum(g, axis=0, keepdims=True)
        gm = gout_ref[rows, :].astype(F32) + norm_back(g, xhat, scale, vec_ref[6:7, :])
        gmid[rows, :] = gm
        low = gm.astype(BF16)
        gbr[rows, :] = low
        sums[5:6, :] += jnp.sum(low.astype(F32), axis=0, keepdims=True)

    chunks(tokens, 128, back_two)
    grad[...] = nn(mixt[...], gbr[...]).astype(BF16)
    for chip in range(CHIPS):
        place = scatter_place(pos_ref, chip)
        for other, out in enumerate((mine, theirs)):
            src = grad.at[pl.ds(chip * BLK, BLK), half_cols(pos_ref, other)]
            start(src, out.at[place, 4], sem.at[0])
    gmixed[...] = nt(gbr[...], w_out[...]).astype(BF16)
    whole_wait(grad, sem.at[0])


def attn_backward_kernel(pos_ref, gmixed, qkv_ref, soft_ref, gb_ref, gqkv, give):
    masks = head_masks()
    for r in range(gmixed.shape[0] // ROW_LEN):
        rows = slice(r * ROW_LEN, (r + 1) * ROW_LEN)

        def pair(i, carry):
            q, k, v = (qkv_ref[rows, pair_cols(t, i)] for t in range(3))
            gm = gmixed[rows, pair_cols(0, i)]
            dq = jnp.zeros((ROW_LEN, 128), F32)
            dk = jnp.zeros((ROW_LEN, 128), F32)
            dv = jnp.zeros((ROW_LEN, 128), F32)
            for hh, keep in enumerate(masks):
                p_low = soft_ref[r * HEADS + 2 * i + hh]
                p = p_low.astype(F32)
                gmk = gm * keep
                gs = nt(gmk, v)
                inner = jnp.sum(p * gs, axis=-1, keepdims=True)
                ds = (p * (gs - inner)).astype(BF16)
                dq = dq + nn(ds, k * keep)
                dk = dk + tn(ds, q * keep)
                dv = dv + tn(p_low, gmk)
            gqkv[rows, pair_cols(0, i)] = (dq * (HEAD_DIM**-0.5)).astype(BF16)
            gqkv[rows, pair_cols(1, i)] = dk.astype(BF16)
            gqkv[rows, pair_cols(2, i)] = dv.astype(BF16)
            return carry

        lax.fori_loop(0, PAIRS, pair, 0)
    for t in range(3):
        cols = pl.ds(pl.multiple_of(t * D + (1 - pos_ref[1]) * HALF, 128), HALF)
        give[:, t * HALF : (t + 1) * HALF] = gqkv[:, cols]
    gb_ref[...] = jnp.zeros(gb_ref.shape, F32)
    gb_ref[0:1, :] = jnp.sum(gqkv[:, :D].astype(F32), axis=0, keepdims=True)
    gb_ref[2:3, :] = jnp.sum(gqkv[:, 2 * D :].astype(F32), axis=0, keepdims=True)


def qkv_grad_kernel(
    pos_ref, vec_ref, sums_ref, gbq_ref, gmid, gqkv, n1_ref, w_qkv, n1_got, g_got, x_any,
    igrad, mine, x_ref, acc, n1t, both, grad, sums, small, sems,
):
    tokens = x_ref.shape[0]
    load_x = start(x_any, x_ref, sems.at[0])
    sums[...] = sums_ref[...]
    sums[2:3, :] = gbq_ref[0:1, :]
    sums[4:5, :] = gbq_ref[2:3, :]
    n1t[:, :tokens] = n1_ref[...].T
    n1t[:, tokens:] = n1_got[...].T
    for t in range(3):
        cols = pl.ds(pl.multiple_of(t * D + pos_ref[1] * HALF, 128), HALF)
        both[:tokens, t * HALF : (t + 1) * HALF] = gqkv[:, cols]
    both[tokens:, :] = g_got[...]
    for z in range(4):
        rows = slice(z * 4 * BLK, (z + 1) * 4 * BLK)
        grad[rows, :] = nn(n1t[rows, :], both[...]).astype(BF16)
        for chip in range(4 * z, 4 * z + 4):
            place = scatter_place(pos_ref, chip)
            for t in range(3):
                src = grad.at[pl.ds(chip * BLK, BLK), pl.ds(t * HALF, HALF)]
                start(src, mine.at[place, pl.ds(t * BLK, BLK)], sems.at[1])
    for t in range(3):
        part = nt(gqkv[:, t * D : (t + 1) * D], w_qkv[t])
        acc[...] = part if t == 0 else acc[...] + part
    load_x.wait()

    def back_one(rows):
        xhat, scale = norm_parts(x_ref[rows, :].astype(F32))
        g = acc[rows, :]
        sums[0:1, :] += jnp.sum(g * xhat, axis=0, keepdims=True)
        sums[1:2, :] += jnp.sum(g, axis=0, keepdims=True)
        igrad[rows, :] = (gmid[rows, :] + norm_back(g, xhat, scale, vec_ref[0:1, :])).astype(BF16)

    chunks(tokens, 128, back_one)
    for p in range(CHIPS):
        small[p, 0:16] = sums[:, :HALF].astype(BF16)
        small[p, 16:32] = sums[:, HALF:].astype(BF16)
        start(small.at[p], mine.at[p, pl.ds(3 * BLK, 32)], sems.at[2])
    whole_wait(small, sems.at[2])
    whole_wait(grad, sems.at[1])


def layer_out_kernel(pos_ref, vec_ref, act_ref, mid_ref, w_down, out_ref):
    out_ref[...] = (
        mid_ref[...] + nn(act_ref[...], w_down[...]) + vec_ref[12:13, :]
    ).astype(BF16)


PER = D // (2 * CHIPS)
SEND_ROWS = (3 * PER, 16, 5 * PER, 4 * PER)


def pack_kernel(pos_ref, w_qkv, w_out, w_up, w_down, bu_ref, *refs):
    values, (mine, theirs, rows, last, wide) = refs[:8], refs[8:]
    place = pos_ref[0] * 2 + pos_ref[1]
    rows[...] = jnp.zeros(rows.shape, F32)
    last[...] = jnp.zeros(last.shape, F32)
    for r, value in zip((0, 1, 2, 4, 5, 6, 7, 12), values):
        rows[r : r + 1, 0:PER] = value[...].astype(F32)
    last[0:1, 0 : 4 * PER] = bu_ref[...].astype(F32)
    at = place * (4 * PER)
    up = pltpu.roll(last[...], at % D, 1)[0:1]
    here = lax.broadcasted_iota(jnp.int32, (16, 1), 0) == 8 + at // D
    rows[...] = pltpu.roll(rows[...], place * PER, 1) + jnp.where(here, up, 0.0)
    for out, other in ((mine, 0), (theirs, 1)):
        half = pos_ref[1] ^ other

        def cols(first):
            return pl.ds(pl.multiple_of(first + half * HALF, 128), HALF)

        at = 0
        for t in range(3):
            wide[at : at + PER, :] = w_qkv[:, cols(t * D)].astype(F32)
            at += PER
        wide[at : at + 16, :] = rows[:, cols(0)]
        at += 16
        for n in range(4):
            u, s = n // 2, n % 2
            first = pl.multiple_of(half * (2 * D) + s * D + u * HALF, 128)
            wide[at : at + PER, :] = w_up[:, pl.ds(first, HALF)].astype(F32)
            at += PER
        wide[at : at + PER, :] = w_out[:, cols(0)].astype(F32)
        at += PER
        wide[at : at + 4 * PER, :] = w_down[:, cols(0)].astype(F32)
        out[...] = wide[...].astype(BF16)


def combine_kernel(pos_ref, mine, got, one, two, upper, lower, wide):
    first = pos_ref[1] == 0
    m, g = mine[...].astype(F32), got[...].astype(F32)
    upper[...] = jnp.where(first, m, g)
    lower[...] = jnp.where(first, g, m)

    def pair(at, size):
        wide[0:size, :] = upper[at : at + size, :]
        wide[size : 2 * size, :] = lower[at : at + size, :]
        return wide[0 : 2 * size, :].astype(BF16)

    for t in range(3):
        one[t * BLK : (t + 1) * BLK, :] = pair(t * PER, PER)
    at = 3 * PER
    one[3 * BLK :, :] = (upper[at : at + 16, :] + lower[at : at + 16, :]).astype(BF16)
    at += 16
    for n in range(5):
        two[n] = pair(at + n * PER, PER)
    low = pair(at + 5 * PER, 4 * PER)
    for n in range(4):
        two[5 + n] = low[n * BLK : (n + 1) * BLK]


def finish_kernel(pos_ref, last, *refs):
    terms, (keep, send, held, sems) = refs[:4], refs[4:]
    for i, term in enumerate(terms):
        start(term.at[0], held.at[i], sems.at[i])
    total = last[...].astype(F32)
    for i in range(4):
        whole_wait(held.at[i], sems.at[i])
        total = total + held[i].astype(F32)
    first = pos_ref[1] == 0
    for t in range(3):
        upper, lower = total[t * BLK : t * BLK + PER], total[t * BLK + PER : (t + 1) * BLK]
        keep[t * PER : (t + 1) * PER, :] = jnp.where(first, upper, lower)
        send[t * PER : (t + 1) * PER, :] = jnp.where(first, lower, upper)
    keep[3 * PER :, :] = total[3 * BLK :]
    send[3 * PER :, :] = total[3 * BLK :]


def spread_kernel(pos_ref, keep, got, w_ref, eight_ref, up_ref, down_ref, rows):
    place = pos_ref[0] * 2 + pos_ref[1]
    for ref, other in ((keep, 0), (got, 1)):
        half = pos_ref[1] ^ other
        for t in range(3):
            cols = pl.ds(pl.multiple_of(t * D + half * HALF, 128), HALF)
            w_ref[:, cols] = ref[t * PER : (t + 1) * PER, :]
    for h in range(2):
        at = 3 * PER + 16 * h
        rows[:, h * HALF : (h + 1) * HALF] = keep[at : at + 16, :] + got[at : at + 16, :]
    mine = pltpu.roll(rows[...], lax.rem(D - place * PER, D), 1)
    eight_ref[...] = mine[0:8, 0:PER]
    down_ref[...] = mine[12:13, 0:PER]
    at = place * (4 * PER)
    here = lax.broadcasted_iota(jnp.int32, (16, 1), 0) == 8 + at // D
    row = jnp.sum(jnp.where(here, rows[...], 0.0), axis=0, keepdims=True)
    turned = pltpu.roll(jnp.broadcast_to(row, (8, D)), lax.rem(D - at % D, D), 1)
    up_ref[...] = turned[0:1, 0 : 4 * PER]


def spread_up_kernel(pos_ref, keep, got, up_ref, out_ref):
    for ref, other in ((keep, 0), (got, 1)):
        half = pos_ref[1] ^ other
        for n in range(4):
            first = half * (2 * D) + (n % 2) * D + (n // 2) * HALF
            up_ref[:, pl.ds(pl.multiple_of(first, 128), HALF)] = ref[n]
        out_ref[:, pl.ds(pl.multiple_of(half * HALF, 128), HALF)] = ref[4]


def call(kernel, name, near, far, near_outs, far_outs, scratch, flops, aliases=None, limit=18):
    far = [in_hbm(a) for a in far]
    space = pl.BlockSpec(memory_space=pltpu.VMEM)
    anyspec = pl.BlockSpec(memory_space=pl.ANY)
    outs = tuple(near_outs) + tuple(far_outs)
    moved = sum(math.prod(a.shape) * a.dtype.itemsize for a in (*near, *far, *outs))
    return pl.pallas_call(
        kernel,
        out_shape=outs,
        in_specs=[pl.BlockSpec(memory_space=pltpu.SMEM)]
        + [space] * (len(near) - 1)
        + [anyspec] * len(far),
        out_specs=[space] * len(near_outs) + [anyspec] * len(far_outs),
        scratch_shapes=scratch,
        input_output_aliases=aliases or {},
        compiler_params=pltpu.CompilerParams(vmem_limit_bytes=limit << 20),
        cost_estimate=pl.CostEstimate(flops=flops, bytes_accessed=moved, transcendentals=0),
        name=name,
    )(*near, *far)


def in_hbm(array):
    return pltpu.with_memory_space_constraint(array, pltpu.HBM)


def keep(*arrays):
    return [pltpu.with_memory_space_constraint(a, pltpu.VMEM) for a in arrays]


def swap(value, chip_bit):
    flip = chip_bit * 2 if chip_bit else 1
    return lax.ppermute(value, AXES, [(i, i ^ flip) for i in range(2 * CHIPS)])


def tie(value, *after):
    return lax.optimization_barrier((value,) + after)[0]


def gathered(*own_half):
    return list(own_half) + [swap(piece, 0) for piece in own_half]


def hold(pieces, *after):
    return lax.optimization_barrier((*pieces, *after))[: len(pieces)] if after else pieces


def rounded_sum(*terms):
    total = terms[0].astype(F32)
    for term in terms[1:]:
        total = total + term.astype(F32)
    return total.astype(BF16)


def small_grads(sums, place, per, per_up):
    eight = lax.dynamic_slice(sums, (0, place * per), (8, per))
    at = place * per_up
    up = lax.dynamic_slice(sums, (8 + at // D, at % D), (1, per_up))[0]
    down = lax.dynamic_slice(sums, (12, place * per), (1, per))[0]
    return eight, up, down


def halves(w_qkv, w_out, w_up, w_down):
    rows = w_qkv.shape[0]
    qkv = w_qkv.reshape(rows, 3, 2, HALF)
    up = w_up.reshape(rows, 2, 4, HALF)
    for h in range(2):
        cols = slice(h * HALF, (h + 1) * HALF)
        up_h = up[:, h].reshape(rows, 2, 2, HALF).transpose(2, 1, 0, 3).reshape(4, rows, HALF)
        yield (
            qkv[:, :, h].transpose(1, 0, 2),
            jnp.concatenate([up_h, w_out[None, :, cols]]),
            w_down[:, cols],
        )


def gather_plain(weights, values):
    def whole(w):
        return lax.all_gather(w, AXES, axis=0, tiled=True)

    gain1, bias1, bq, bv, bo, gain2, bias2, bu, bd = [whole(v) for v in values]
    rest = jnp.zeros((3, D), BF16)
    small = jnp.stack([gain1, bias1, bq, jnp.zeros_like(bq), bv, bo, gain2, bias2])
    small = jnp.concatenate([small, bu.reshape(4, D), bd[None], rest])
    groups = ([], [], [])
    for h, (attn, up, down) in enumerate(halves(*[whole(w) for w in weights])):
        attn = attn.reshape(3, CHIPS, BLK, HALF).transpose(1, 0, 2, 3).reshape(CHIPS, 3 * BLK, HALF)
        up = up.reshape(5, CHIPS, BLK, HALF).transpose(1, 0, 2, 3)
        down = down.reshape(CHIPS, 4 * BLK, HALF)
        extra = jnp.zeros((CHIPS, 16, HALF), BF16).at[0].set(small[:, h * HALF : (h + 1) * HALF])
        for group, blocks in zip(groups, (jnp.concatenate([attn, extra], axis=1), up, down)):
            group.extend(jnp.stack([blocks[o] for o in piece]) for piece in GATHER)
    return groups


def scatter_plain(pair, group):
    both = [jnp.stack([part[SCATTER.index(chip)] for chip in range(CHIPS)]) for part in pair]

    def scatter(v):
        return lax.psum_scatter(v.astype(F32), AXES, scatter_dimension=0, tiled=True)

    def matrix(units):
        return jnp.stack(units, axis=3).transpose(0, 2, 1, 3, 4).reshape(D, -1, 2, HALF)

    if group == "attn":
        sums = jnp.concatenate([both[0][0, 3 * BLK + 16 * h :][:16] for h in range(2)], axis=1)
        qkv = matrix([b[:, : 3 * BLK].reshape(CHIPS, 3, BLK, HALF) for b in both])
        return scatter(qkv.reshape(D, 3 * D)), lax.psum(sums.astype(F32), AXES)
    if group == "up":
        up = matrix(both)
        order = up[:, :4].reshape(D, 2, 2, 2, HALF).transpose(0, 3, 2, 1, 4)
        return scatter(order.reshape(D, FF)), scatter(up[:, 4].reshape(D, D))
    return scatter(jnp.concatenate([b.reshape(FF, HALF) for b in both], axis=1))


def shape(dims, kind=BF16):
    return jax.ShapeDtypeStruct(dims, kind)


def far_shape(*dims):
    return pltpu.HBM(dims, BF16)


def dma(n):
    return pltpu.SemaphoreType.DMA((n,))


def vmem(*dims, kind=BF16):
    return pltpu.VMEM(dims, kind)


class Layer:
    def __init__(self, tokens):
        self.tokens = tokens
        self.rows = tokens // ROW_LEN
        self.out = shape((tokens, D))
        self.wide = vmem(tokens, FF)
        self.one = vmem(tokens, D)
        self.one_f32 = vmem(tokens, D, kind=F32)
        self.qkv = vmem(tokens, 3 * D)
        self.soft = vmem(self.rows * HEADS, ROW_LEN, ROW_LEN)
        self.turned = vmem(D, tokens)
        self.square = vmem(D, D)
        self.three = vmem(3, D, D)
        self.four = vmem(2, 2, D, D)
        self.sums = vmem(8, D, kind=F32)
        self.vec = vmem(16, D, kind=F32)

    def chip_blocks(self, pos, weights, values):
        *rest, bu, bd = [in_hbm(v.reshape(1, -1)) for v in values]
        weights = [in_hbm(w) for w in weights]
        sent = shape((sum(SEND_ROWS), HALF))
        wide = vmem(sum(SEND_ROWS), HALF, kind=F32)
        mine, theirs = call(
            pack_kernel, "pack", (pos, *weights, bu, *rest, bd), (), (sent, sent), (),
            [vmem(16, D, kind=F32), vmem(8, D, kind=F32), wide], 0,
        )
        return call(
            combine_kernel, "combine", (pos, mine, swap(theirs, 0)), (),
            (shape((3 * BLK + 16, HALF)), shape((9, BLK, HALF))), (),
            [wide, wide, vmem(4 * BLK, HALF, kind=F32)], 0,
        )

    def finish(self, pos, last, low):
        sent = shape((3 * PER + 32, HALF), F32)
        keep, send = call(
            finish_kernel, "finish", (pos, last), low, (sent, sent), (),
            [vmem(4, 3 * BLK + 32, HALF), dma(4)], 0,
        )
        return call(
            spread_kernel, "spread", (pos, keep, swap(send, 0)), (),
            (shape((PER, 3 * D), F32), shape((8, PER), F32), shape((1, 4 * PER), F32), shape((1, PER), F32)),
            (), [vmem(16, D, kind=F32)], 0,
        )

    def spread_up(self, pos, keep, got):
        return call(
            spread_up_kernel, "spread_up", (pos, keep, got), (),
            (shape((PER, FF), F32), shape((PER, D), F32)), (), [], 0,
        )

    def attn_forward(self, pos, segr, segc, inputs, attn):
        return call(
            attn_forward_kernel, "attn_forward", (pos, segr, segc), [in_hbm(inputs)] + attn,
            (self.vec, self.one, self.qkv, self.soft, self.one, self.three), (),
            [
                self.one, vmem(2, CHIPS, 16, HALF),
                vmem(self.rows, ROW_LEN, ROW_LEN, kind=F32), dma(5),
            ],
            2 * self.tokens * D * D * 3 + 8 * self.tokens * D * ROW_LEN,
        )

    def mlp_up(self, pos, segc, vec, inputs, mixed, cotangent, up):
        vec, mixed = keep(vec, mixed)
        return call(
            mlp_up_kernel, "mlp_up", (pos, segc, vec, mixed), [inputs, cotangent] + up,
            (self.sums, self.one, self.one_f32, self.wide, self.wide, self.one, self.square, self.four), (),
            [self.one, self.one, dma(5)],
            2 * self.tokens * D * (FF + D),
        )

    def down_grad(self, pos, act, gout):
        buffer = far_shape(CHIPS, 4 * BLK, HALF)
        return call(
            down_grad_kernel, "down_grad", (pos, *keep(act, gout)), [], (), (buffer, buffer),
            [vmem(4, D, D), dma(1)],
            2 * self.tokens * D * FF,
        )

    def mlp_down(self, pos, gout, slope, n2, down):
        buffer = far_shape(CHIPS, 5, BLK, HALF)
        return call(
            mlp_down_kernel, "mlp_down", (pos, *keep(gout, slope, n2)), down,
            (self.sums, self.wide, vmem(FF, D)), (buffer, buffer),
            [self.turned, self.four, dma(5)],
            4 * self.tokens * D * FF,
        )

    def mid_backward(self, pos, vec, gbd, gbu, gpre, gout, mid, mixed, w_out, w_up, mine, theirs):
        buffer = far_shape(*mine.shape)
        near = (pos, *keep(vec, gbd, gbu, gpre, gout, mid, mixed, w_out, w_up))
        return call(
            mid_backward_kernel, "mid_backward", near, [mine, theirs],
            (self.vec, self.one_f32, self.one), (buffer, buffer),
            [self.one_f32, self.one, self.turned, self.square, dma(1)],
            2 * self.tokens * D * (FF + 2 * D),
            {len(near): 3, len(near) + 1: 4},
        )

    def attn_backward(self, pos, gmixed, qkv, soft):
        return call(
            attn_backward_kernel, "attn_backward", (pos, *keep(gmixed, qkv, soft)), [],
            (self.sums, self.qkv, vmem(self.tokens, 3 * HALF)), (), [], 20 * self.tokens * D * ROW_LEN,
        )

    def qkv_grad(self, pos, vec, sums, gbq, gmid, gqkv, n1, w_qkv, n1_got, g_got, inputs):
        return call(
            qkv_grad_kernel, "qkv_grad", (pos, *keep(vec, sums, gbq, gmid, gqkv, n1, w_qkv, n1_got, g_got)),
            [inputs], (self.out,), (far_shape(CHIPS, 3 * BLK + 32, HALF),),
            [
                self.one, self.one_f32, vmem(D, 2 * self.tokens), vmem(2 * self.tokens, 3 * HALF),
                vmem(D, 3 * HALF), vmem(16, D, kind=F32), vmem(CHIPS, 32, HALF), dma(3),
            ],
            2 * self.tokens * D * 6 * D,
        )

    def layer_out(self, pos, vec, act, mid, w_down):
        (out,) = call(
            layer_out_kernel, "layer_out", (pos, *keep(vec, act, mid, w_down)), [], (self.out,), (), [],
            2 * self.tokens * D * FF,
        )
        return out


class Scatter:
    def __init__(self, mine, theirs=None, *after):
        self.both = [mine] if theirs is None else [mine, swap(tie(theirs, *after), 0)]

    def part(self, first, last):
        return [ref[first:last] for ref in self.both]

    def hold_back(self, *after):
        self.both[-1] = hold((self.both[-1],), *after)[0]

    def first(self, *after):
        self.hold_back(*after)
        self.out = (rounded_sum(*self.part(8, 12)), rounded_sum(*self.part(12, 16)))
        self.in_y, self.in_x = swap(self.out[0], BIT_Y), swap(self.out[1], BIT_X)

    def second(self, *after):
        in_y, in_x = hold((self.in_y, self.in_x), *after)
        self.out = (
            rounded_sum(*self.part(4, 6), in_x[2:]),
            rounded_sum(*self.part(6, 8), in_y[2:]),
        )
        self.in_y, self.in_x = in_y, in_x
        self.in_y2, self.in_x2 = swap(self.out[0], BIT_Y), swap(self.out[1], BIT_X)

    def third(self, *after):
        in_y2, in_x2 = hold((self.in_y2, self.in_x2), *after)
        self.near = (*self.part(0, 2), self.in_x[:2], in_y2)
        self.out = (rounded_sum(*self.part(2, 4), self.in_y[:2], in_x2),)
        self.in_z = swap(self.out[0], BIT_Z0)

    def diagonal(self, *after):
        self.hold_back(*after)
        self.out = (rounded_sum(*self.part(10, 12)), rounded_sum(*self.part(14, 16)))
        self.in_y, self.in_x = swap(self.out[0], BIT_Y), swap(self.out[1], BIT_X)

    def hi(self, *after):
        in_y, self.in_x = hold((self.in_y, self.in_x), *after)
        self.out = (rounded_sum(*self.part(8, 10)), rounded_sum(*self.part(6, 8), in_y))
        self.in_y2, self.in_x2 = swap(self.out[0], BIT_Y), swap(self.out[1], BIT_X)

    def lo(self, *after):
        in_y2, in_x2 = hold((self.in_y2, self.in_x2), *after)
        far = rounded_sum(*self.part(2, 4), in_y2, in_x2)
        self.in_z = swap(far, BIT_Z0)
        low_y, low_x = rounded_sum(*self.part(4, 6), self.in_x), rounded_sum(*self.part(12, 14))
        low_y, low_x = hold((low_y, low_x), far)
        self.out = (far, low_y, low_x)
        self.near = (*self.part(0, 2), swap(low_y, BIT_Y), swap(low_x, BIT_X))

    def fourth(self, *after):
        self.near = (*self.near, *hold((self.in_z,), *after))
        self.out = (rounded_sum(*[t[1] for t in self.near]),)
        self.in_z = swap(self.out[0], BIT_Z1)

    def result(self, *after):
        total = hold((self.in_z,), *after)[0].astype(F32)
        for term in self.near:
            total = total + term[0].astype(F32)
        return total


def per_device(tuned, *args):
    (
        inputs, segment_ids, pre_attn_gain, pre_attn_bias, w_qkv, b_query, b_value, w_out, b_out,
        pre_mlp_gain, pre_mlp_bias, w_up, b_up, w_down, b_down, cotangent,
    ) = args
    tokens = inputs.shape[0]
    n_rows = tokens // ROW_LEN
    wide, narrow = lax.axis_index("wide"), lax.axis_index("narrow")
    weights = (w_qkv, w_out, w_up, w_down)
    values = (
        pre_attn_gain, pre_attn_bias, b_query, b_value, b_out, pre_mlp_gain, pre_mlp_bias, b_up, b_down,
    )
    per, per_up = pre_attn_gain.shape[0], b_up.shape[0]
    position = jnp.arange(ROW_LEN, dtype=jnp.int32)[None]
    own_id = jnp.where(segment_ids != 0, segment_ids, -1 - position)
    segr = own_id.reshape(n_rows, 1, ROW_LEN)
    segc = own_id.reshape(tokens, 1)
    layer = Layer(tokens)

    if not tuned:
        place = wide * lax.axis_size("narrow") + narrow
        pos = jnp.zeros((2,), jnp.int32)
        attn, up, down = gather_plain(weights, values)
        vec, n1, qkv, soft, mixed, w_qkv_all = layer.attn_forward(pos, segr, segc, inputs, attn)
        gbd, n2, mid, act, slope, gout, *w_mid = layer.mlp_up(pos, segc, vec, inputs, mixed, cotangent, up)
        pair_down = layer.down_grad(pos, act, gout)
        gbu, gpre, w_down_all, *pair_up = layer.mlp_down(pos, gout, slope, n2, down)
        sums, gmid, gmixed, *pair_up = layer.mid_backward(
            pos, vec, gbd, gbu, gpre, gout, mid, mixed, *w_mid, *pair_up
        )
        gbq, gqkv, give = layer.attn_backward(pos, gmixed, qkv, soft)
        pair_attn = []
        for half in range(2):
            input_grad, blocks = layer.qkv_grad(
                jnp.array([0, half], jnp.int32), vec, sums, gbq, gmid, gqkv, n1, w_qkv_all,
                jnp.zeros_like(n1), jnp.zeros_like(give), inputs,
            )
            pair_attn.append(blocks)
        layer_out = layer.layer_out(pos, vec, act, mid, w_down_all)
        grad_w_down = scatter_plain(pair_down, "down")
        grad_w_up, grad_w_out = scatter_plain(pair_up, "up")
        grad_w_qkv, sums = scatter_plain(pair_attn, "attn")
        eight, grad_b_up, grad_b_down = small_grads(sums, place, per, per_up)
    else:
        core = (narrow & 1).astype(jnp.int32)
        pos = jnp.stack([wide * 2 + (narrow >> 1), core]).astype(jnp.int32)
        block1, block23 = layer.chip_blocks(pos, weights, values)
        flat = (4 * BLK, HALF)

        near1 = swap(block1, BIT_Z1)
        lo1 = jnp.stack([block1, near1])
        hi1 = swap(lo1, BIT_Z0)
        y_lo1, x_lo1 = swap(lo1, BIT_Y), swap(lo1, BIT_X)
        near23 = swap(tie(block23, near1), BIT_Z1)
        d_lo1 = swap(y_lo1, BIT_X)
        y_hi1, x_hi1 = swap(hi1, BIT_Y), swap(hi1, BIT_X)
        lo2 = jnp.stack([block23[:5], near23[:5]])
        lo3 = jnp.stack([block23[5:].reshape(flat), near23[5:].reshape(flat)])
        hi2 = swap(tie(lo2, hi1), BIT_Z0)
        d_hi1 = swap(tie(x_hi1, y_hi1), BIT_Y)
        lo2b = tie(lo2, d_lo1, x_hi1, y_hi1)
        y_lo2, x_lo2 = swap(lo2b, BIT_Y), swap(lo2b, BIT_X)
        attn = gathered(lo1, hi1, y_lo1, y_hi1, x_lo1, x_hi1, d_lo1, d_hi1)
        hi3 = swap(tie(lo3, hi2), BIT_Z0)
        y_hi2, x_hi2 = swap(hi2, BIT_Y), swap(hi2, BIT_X)
        d_lo2, d_hi2 = swap(y_lo2, BIT_X), swap(tie(x_hi2, y_hi2), BIT_Y)
        lo3b = tie(lo3, y_lo2, x_lo2, y_hi2)
        y_lo3, x_lo3 = swap(lo3b, BIT_Y), swap(lo3b, BIT_X)
        vec, n1, qkv, soft, mixed, w_qkv_all = layer.attn_forward(
            tie(pos, y_hi2, x_hi2, lo3b, d_lo2), segr, segc, inputs, attn
        )

        d_hi2, y_lo3, x_lo3, hi3 = hold((d_hi2, y_lo3, x_lo3, hi3), mixed)
        d_lo3 = swap(y_lo3, BIT_X)
        y_hi3, x_hi3 = swap(hi3, BIT_Y), swap(hi3, BIT_X)
        lo2, hi2, y_lo2, y_hi2, x_lo2, x_hi2, d_lo2 = hold(
            (lo2, hi2, y_lo2, y_hi2, x_lo2, x_hi2, d_lo2), x_lo3, hi3
        )
        up = gathered(lo2, hi2, y_lo2, y_hi2, x_lo2, x_hi2, d_lo2, d_hi2)
        gbd, n2, mid, act, slope, gout, *w_mid = layer.mlp_up(
            tie(pos, hi3, y_lo3, x_lo3), segc, vec, inputs, mixed, cotangent, up
        )
        y_hi3, x_hi3, d_lo3 = hold((y_hi3, x_hi3, d_lo3), gbd)
        d_hi3 = swap(x_hi3, BIT_Y)
        pair_down = layer.down_grad(tie(pos, y_hi3, x_hi3, d_lo3), act, gout)
        d_hi3 = tie(d_hi3, pair_down[0])
        down = gathered(lo3, hi3, y_lo3, y_hi3, x_lo3, x_hi3, d_lo3, d_hi3)
        scatter1 = Scatter(*pair_down, *down)
        gbu, gpre, w_down_all, *pair_up = layer.mlp_down(pos, gout, slope, n2, down)
        scatter1.first(gbu)
        sums, gmid, gmixed, *pair_up = layer.mid_backward(
            tie(pos, *scatter1.out), vec, gbd, gbu, gpre, gout, mid, mixed, *w_mid, *pair_up
        )
        scatter1.second(sums)
        scatter2 = Scatter(*pair_up, scatter1.in_y, scatter1.in_x)
        gbq, gqkv, give = layer.attn_backward(tie(pos, *scatter1.out), gmixed, qkv, soft)
        scatter1.third(gbq)
        n1, give = hold((n1, give), *scatter1.out)
        n1_got, g_got = swap(n1, 0), swap(give, 0)
        scatter2.diagonal(gbq)
        input_grad, sums_attn = layer.qkv_grad(
            tie(pos, *scatter2.out, *scatter1.out),
            vec, sums, gbq, gmid, gqkv, n1, w_qkv_all, n1_got, g_got, inputs,
        )
        scatter2.hi(input_grad)
        scatter1.fourth(input_grad)
        scatter3 = Scatter(tie(sums_attn, *scatter2.out))
        scatter3.diagonal()
        layer_out = layer.layer_out(
            tie(pos, *scatter3.out, *scatter1.out), vec, act, mid, w_down_all
        )
        scatter1.in_z = tie(scatter1.in_z, layer_out)
        scatter3.hi(layer_out, scatter1.in_z)
        scatter2.lo(*scatter3.out)
        scatter3.lo(*scatter2.out)
        scatter2.fourth(*scatter3.out)
        scatter3.fourth(*scatter2.out)

        def exchange(blocks, axis):
            first, second = jnp.split(blocks, 2, axis=axis)
            keep = jnp.where(core == 0, first, second)
            got = swap(jnp.where(core == 0, second, first), 0)
            return jnp.where(core == 0, keep, got), jnp.where(core == 0, got, keep)

        grad_w_down = jnp.concatenate(exchange(scatter1.result(*scatter3.out), 0), axis=1)
        total = scatter2.result(*scatter3.out)
        upper, lower = total[:, :PER], total[:, PER:]
        got = swap(jnp.where(core == 0, lower, upper), 0)
        grad_w_up, grad_w_out = layer.spread_up(pos, jnp.where(core == 0, upper, lower), got)
        grad_w_qkv, eight, grad_b_up, grad_b_down = layer.finish(
            pos, scatter3.in_z, [*scatter3.both, *scatter3.near[1:]]
        )
        grad_b_up, grad_b_down = grad_b_up[0], grad_b_down[0]
    return (
        layer_out, input_grad, eight[0], eight[1], grad_w_qkv, eight[2], eight[4], grad_w_out, eight[5],
        eight[6], eight[7], grad_w_up, grad_b_up, grad_w_down, grad_b_down,
    )


def solution(mesh):
    both = P(AXES, None)
    one = P(AXES)
    tuned = dict(mesh.shape) == {"wide": 8, "narrow": 4}
    in_specs = (both, both, one, one, both, one, one, both, one, one, one, both, one, both, one, both)
    out_specs = (both, both, one, one, both, one, one, both, one, one, one, both, one, both, one)
    return jax.shard_map(
        functools.partial(per_device, tuned),
        mesh=mesh,
        in_specs=in_specs,
        out_specs=out_specs,
        check_vma=False,
    )
```

profile of v0, /device:TPU:0, one launch (start us, length us, event | category | flops | bytes accessed | tf_op | source)
XLA Modules:
  0.0 220.3 jit_solution(15071076448440500595)
XLA Ops:
  4.3 4.0 %collective-permute-start.1 = (bf16[160,384]{1,0:T(8,128)(2,1)S(1)}, bf16[160,384]{1,0:T(8,128)(2,1)S(1)}, u32[]{:S(2)}, u32[]{:S(2)}) collective-permute-start(bf16[160,384]{1,0:T(8,128)(2,1)S(1)} %get-tuple-element.119), channel_id=1, source_target_pairs={{0,16},{1,17},{2,18},{3,19},{4,20},{5,21},{6,22},{7,23},{8,24},{9,... | collective-permute-start | bytes 368648 | tf_op jit(solution)/shard_map/ppermute | solution.py:542
  8.3 6.3 %collective-permute-done.1 = bf16[160,384]{1,0:T(8,128)(2,1)S(1)} collective-permute-done((bf16[160,384]{1,0:T(8,128)(2,1)S(1)}, bf16[160,384]{1,0:T(8,128)(2,1)S(1)}, u32[]{:S(2)}, u32[]{:S(2)}) %collective-permute-start.1) | collective-permute-done | bytes 122912 | tf_op jit(solution)/shard_map/ppermute | solution.py:542
  14.7 1.6 collective-permute-start.8
  16.3 4.0 %collective-permute-start.3 = (bf16[2,160,384]{2,1,0:T(8,128)(2,1)S(1)}, bf16[2,160,384]{2,1,0:T(8,128)(2,1)S(1)}, u32[]{:S(2)}, u32[]{:S(2)}) collective-permute-start(bf16[2,160,384]{2,1,0:T(8,128)(2,1)S(1)} %pad_maximum_fusion.3.refs_0_), channel_id=1, source_target_pairs={{0,8},{1,9},{2,10},{3,11},{4,12},{5,13},{6,14},{7,15},{8,0},{9,1},... | collective-permute-start | bytes 737288 | tf_op jit(solution)/shard_map/ppermute | solution.py:542
  20.3 1.6 collective-permute-start.18
  23.4 3.6 %collective-permute-done.3.refs_1_ = bf16[2,160,384]{2,1,0:T(8,128)(2,1)S(1)} collective-permute-done((bf16[2,160,384]{2,1,0:T(8,128)(2,1)S(1)}, bf16[2,160,384]{2,1,0:T(8,128)(2,1)S(1)}, u32[]{:S(2)}, u32[]{:S(2)}) %collective-permute-start.3) | collective-permute-done | bytes 245792 | tf_op jit(solution)/shard_map/ppermute | solution.py:542
  28.2 3.6 %collective-permute-done.2 = bf16[9,48,384]{2,1,0:T(8,128)(2,1)S(1)} collective-permute-done((bf16[9,48,384]{2,1,0:T(8,128)(2,1)S(1)}, bf16[9,48,384]{2,1,0:T(8,128)(2,1)S(1)}, u32[]{:S(2)}, u32[]{:S(2)}) %collective-permute-start.2) | collective-permute-done | bytes 331808 | tf_op jit(solution)/shard_map/ppermute | solution.py:542
  32.1 1.3 collective-permute-start.10
  34.0 4.8 %collective-permute-done.10.refs_5_ = bf16[2,160,384]{2,1,0:T(8,128)(2,1)S(1)} collective-permute-done((bf16[2,160,384]{2,1,0:T(8,128)(2,1)S(1)}, bf16[2,160,384]{2,1,0:T(8,128)(2,1)S(1)}, u32[]{:S(2)}, u32[]{:S(2)}) %collective-permute-start.10) | collective-permute-done | bytes 245792 | tf_op jit(solution)/shard_map/ppermute | solution.py:542
  39.7 1.6 collective-permute-start.13
  44.2 5.8 %collective-permute-done.12.refs_2_ = bf16[2,5,48,384]{3,2,1,0:T(8,128)(2,1)S(1)} collective-permute-done((bf16[2,5,48,384]{3,2,1,0:T(8,128)(2,1)S(1)}, bf16[2,5,48,384]{3,2,1,0:T(8,128)(2,1)S(1)}, u32[]{:S(2)}, u32[]{:S(2)}) %collective-permute-start.12) | collective-permute-done | bytes 368672 | tf_op jit(solution)/shard_map/ppermute | solution.py:542
  50.6 9.7 %collective-permute-done.19.refs_7_ = bf16[2,160,384]{2,1,0:T(8,128)(2,1)} collective-permute-done((bf16[2,160,384]{2,1,0:T(8,128)(2,1)S(1)}, bf16[2,160,384]{2,1,0:T(8,128)(2,1)}, u32[]{:S(2)}, u32[]{:S(2)}) %collective-permute-start.19) | collective-permute-done | bytes 245792 | tf_op jit(solution)/shard_map/ppermute | solution.py:542
  61.8 1.4 collective-permute-start.16
  64.1 1.5 collective-permute-start.14
  65.6 1.4 collective-permute-done.17.refs_6_
  68.3 12.1 %attn_forward.1 = (f32[16,768]{1,0:T(8,128)S(1)}, bf16[512,768]{1,0:T(8,128)(2,1)S(1)}, bf16[512,2304]{1,0:T(8,128)(2,1)S(1)}, bf16[24,256,256]{2,1,0:T(8,128)(2...) custom-call(s32[2]{0:T(128)S(1)} %pad_add_fusion.pos_ref, s32[2,1,256]{2,1,0:T(1,128)S(1)} %reshape.123.segr_ref, ...), custom_call_target="tpu_custom_call" | custom-call | flops 2617245696 | bytes 15388680 | tf_op jit(solution)/shard_map/attn_forward/pallas_call | solution.py:517
  85.9 1.5 collective-permute-start.28
  88.2 10.0 %mlp_up.1 = (f32[8,768]{1,0:T(8,128)S(1)}, bf16[512,768]{1,0:T(8,128)(2,1)S(1)}, f32[512,768]{1,0:T(8,128)S(1)}, bf16[512,3072]{1,0:T(8,128)(2,1)S(1)}, bf16[512...) custom-call(s32[2]{0:T(128)S(1)} %pad_add_fusion.pos_ref, ...), custom_call_target="tpu_custom_call" | custom-call | flops 3019898880 | bytes 23668744 | tf_op jit(solution)/shard_map/mlp_up/pallas_call | solution.py:517
  99.4 1.6 collective-permute-start.39
  102.0 4.3 %down_grad.1 = (bf16[16,192,384]{2,1,0:T(8,128)(2,1)}, bf16[16,192,384]{2,1,0:T(8,128)(2,1)}) custom-call(s32[2]{0:T(128)S(1)} %pad_add_fusion.pos_ref, bf16[512,3072]{1,0:T(8,128)(2,1)S(1)} %get-tuple-element.147.act_ref, bf16[512,768]{1,0:T(8,128)(2,1)S(1)} %get-tuple-element.148.gout_ref), custom_call_target="tpu_custom_call" | custom-call | flops 2415919104 | bytes 8650760 | tf_op jit(solution)/shard_map/down_grad/pallas_call | solution.py:517
  106.4 1.3 collective-permute-done.39.refs_7_
  111.3 9.7 %mlp_down.1 = (f32[8,768]{1,0:T(8,128)S(1)}, bf16[512,3072]{1,0:T(8,128)(2,1)S(1)}, bf16[3072,768]{1,0:T(8,128)(2,1)S(1)}, bf16[16,5,48,384]{3,2,1,0:T(8,128)(2,1)}, bf16[16,5,48,384]{3,2,1,0:T(8,128)(2,1)}) custom-call(s32[2]{0:T(128)S(1)} %pad_add_fusion.pos_ref, bf16[512,768]{1,0:T(8,128)(2,1)S(1)} %get-tuple-element.148.gout_ref, ...), custom_call_target="tpu_custom_call" | custom-call | flops 4831838208 | bytes 23224328 | tf_op jit(solution)/shard_map/mlp_down/pallas_call | solution.py:517
  121.3 1.3 collective-permute-start.50
  123.8 8.8 %mid_backward.1 = (f32[16,768]{1,0:T(8,128)S(1)}, f32[512,768]{1,0:T(8,128)S(1)}, bf16[512,768]{1,0:T(8,128)(2,1)S(1)}, bf16[16,5,48,384]{3,2,1,0:T(8,128)(2,1)}, bf16[16,5,48,384]{3,2,1,0:T(8,128)(2,1)}) custom-call(s32[2]{0:T(128)S(1)} %pad_add_fusion.pos_ref, ...), custom_call_target="tpu_custom_call", output_to_operand_aliasing={{3}: (10, {}), {4}: (11, {})} | custom-call | flops 3623878656 | bytes 26492936 | tf_op jit(solution)/shard_map/mid_backward/pallas_call | solution.py:517
  132.6 4.9 %collective-permute-done.50 = bf16[4,192,384]{2,1,0:T(8,128)(2,1)S(1)} collective-permute-done((bf16[4,192,384]{2,1,0:T(8,128)(2,1)S(1)}, bf16[4,192,384]{2,1,0:T(8,128)(2,1)S(1)}, u32[]{:S(2)}, u32[]{:S(2)}) %collective-permute-start.50) | collective-permute-done | bytes 589856 | tf_op jit(solution)/shard_map/ppermute | solution.py:542
  139.5 1.5 collective-permute-start.52
  141.1 8.9 %attn_backward.1 = (f32[8,768]{1,0:T(8,128)S(1)}, bf16[512,2304]{1,0:T(8,128)(2,1)S(1)}, bf16[512,1152]{1,0:T(8,128)(2,1)S(1)}) custom-call(s32[2]{0:T(128)S(1)} %pad_add_fusion.pos_ref, bf16[512,768]{1,0:T(8,128)(2,1)S(1)} %get-tuple-element.171.gmixed, bf16[512,2304]{1,0:T(8,128)(2,1)S(1)} %get-tuple-element.172.qkv_ref, ...), custom_call_target="tpu_custom_call" | custom-call | flops 2013265920 | bytes 9854984 | tf_op jit(solution)/shard_map/attn_backward/pallas_call | solution.py:517
  152.7 1.9 collective-permute-start.58
  154.6 8.1 %qkv_grad.1 = (bf16[512,768]{1,0:T(8,128)(2,1)}, bf16[16,176,384]{2,1,0:T(8,128)(2,1)}) custom-call(s32[2]{0:T(128)S(1)} %pad_add_fusion.pos_ref, f32[16,768]{1,0:T(8,128)S(1)} %get-tuple-element.133.vec_ref, f32[16,768]{1,0:T(8,128)S(1)} %get-tuple-element.166.sums_ref, f32[8,768]{1,0:T(8,128)S(1)} %get-tuple-element.174.gbq_ref, ...), custom_call_target="tpu_custom_call" | custom-call | flops 3623878656 | bytes 14082056 | tf_op jit(solution)/shard_map/qkv_grad/pallas_call | solution.py:517
  163.0 1.4 copy-done.1
  167.4 2.9 %collective-permute-start.61 = (bf16[192,384]{1,0:T(8,128)(2,1)S(1)}, bf16[192,384]{1,0:T(8,128)(2,1)S(1)}, u32[]{:S(2)}, u32[]{:S(2)}) collective-permute-start(bf16[192,384]{1,0:T(8,128)(2,1)S(1)} %fusion.1), channel_id=1, source_target_pairs={{0,16},{1,17},{2,18},{3,19},{4,20},{5,21},{6,22},{7,23},{8,24},{9,... | collective-permute-start | bytes 442376 | tf_op jit(solution)/shard_map/ppermute | solution.py:542
  170.4 1.5 collective-permute-start.65
  172.3 4.0 %layer_out.1 = bf16[512,768]{1,0:T(8,128)(2,1)} custom-call(s32[2]{0:T(128)S(1)} %pad_add_fusion.pos_ref, f32[16,768]{1,0:T(8,128)S(1)} %get-tuple-element.133.vec_ref, bf16[512,3072]{1,0:T(8,128)(2,1)S(1)} %get-tuple-element.147.act_ref, f32[512,768]{1,0:T(8,128)S(1)} %get-tuple-element.159.mid_ref, bf16[3072,768]{1,0:T(8,128)(2,1)S(1)} %get-tuple-element.192.w_down), custom_call_target="tpu_custom_call" | custom-call | flops 2415919104 | bytes 10272776 | tf_op jit(solution)/shard_map/layer_out/pallas_call | solution.py:517
  179.1 3.3 %collective-permute-done.65 = bf16[2,5,48,384]{3,2,1,0:T(8,128)(2,1)S(1)} collective-permute-done((bf16[2,5,48,384]{3,2,1,0:T(8,128)(2,1)S(1)}, bf16[2,5,48,384]{3,2,1,0:T(8,128)(2,1)S(1)}, u32[]{:S(2)}, u32[]{:S(2)}) %collective-permute-start.65) | collective-permute-done | bytes 368672 | tf_op jit(solution)/shard_map/ppermute | solution.py:542
  183.4 1.3 add_convert_fusion.2
  184.7 1.8 collective-permute-start.71
  189.3 2.7 %collective-permute-start.68 = (bf16[2,176,384]{2,1,0:T(8,128)(2,1)}, bf16[2,176,384]{2,1,0:T(8,128)(2,1)S(1)}, u32[]{:S(2)}, u32[]{:S(2)}) collective-permute-start(bf16[2,176,384]{2,1,0:T(8,128)(2,1)} %get-tuple-element.228), channel_id=1, source_target_pairs={{0,8},{1,9},{2,10},{3,11},{4,12},{5,13},{6,14},{7,15},{8,0},{9,1},... | collective-permute-start | bytes 811016 | tf_op jit(solution)/shard_map/ppermute | solution.py:542
  192.5 3.0 %collective-permute-done.71 = bf16[2,5,48,384]{3,2,1,0:T(8,128)(2,1)} collective-permute-done((bf16[2,5,48,384]{3,2,1,0:T(8,128)(2,1)S(1)}, bf16[2,5,48,384]{3,2,1,0:T(8,128)(2,1)}, u32[]{:S(2)}, u32[]{:S(2)}) %collective-permute-start.71) | collective-permute-done | bytes 368672 | tf_op jit(solution)/shard_map/ppermute | solution.py:542
  196.2 2.2 collective-permute-done.69
  198.4 1.3 fusion
  199.7 2.7 %collective-permute-start.74 = (bf16[5,48,384]{2,1,0:T(8,128)(2,1)S(1)}, bf16[5,48,384]{2,1,0:T(8,128)(2,1)S(1)}, u32[]{:S(2)}, u32[]{:S(2)}) collective-permute-start(bf16[5,48,384]{2,1,0:T(8,128)(2,1)S(1)} %fusion), channel_id=1, source_target_pairs={{0,16},{1,17},{2,18},{3,19},{4,20},{5,21},{6,22},{7,23},{8,24},{9,... | collective-permute-start | bytes 552968 | tf_op jit(solution)/shard_map/ppermute | solution.py:542
  203.7 2.4 %collective-permute-start.72 = (bf16[176,384]{1,0:T(8,128)(2,1)S(1)}, bf16[176,384]{1,0:T(8,128)(2,1)S(1)}, u32[]{:S(2)}, u32[]{:S(2)}) collective-permute-start(bf16[176,384]{1,0:T(8,128)(2,1)S(1)} %fusion.2), channel_id=1, source_target_pairs={{0,16},{1,17},{2,18},{3,19},{4,20},{5,21},{6,22},{7,23},{8,24},{9,... | collective-permute-start | bytes 405512 | tf_op jit(solution)/shard_map/ppermute | solution.py:542
  206.1 1.4 convert_add_fusion.5
  207.6 4.9 %collective-permute-done.74 = bf16[5,48,384]{2,1,0:T(8,128)(2,1)S(1)} collective-permute-done((bf16[5,48,384]{2,1,0:T(8,128)(2,1)S(1)}, bf16[5,48,384]{2,1,0:T(8,128)(2,1)S(1)}, u32[]{:S(2)}, u32[]{:S(2)}) %collective-permute-start.74) | collective-permute-done | bytes 184352 | tf_op jit(solution)/shard_map/ppermute | solution.py:542
  212.4 1.3 convert_add_fusion
  213.9 1.7 finish.1
  217.2 1.3 spread.1
  219.0 1.3 spread_up.1
  (260 shorter events, 48.5 us)
Async XLA Ops:
  4.3 10.3 %collective-permute-start.1 = (bf16[160,384]{1,0:T(8,128)(2,1)S(1)}, bf16[160,384]{1,0:T(8,128)(2,1)S(1)}, u32[]{:S(2)}, u32[]{:S(2)}) collective-permute-start(bf16[160,384]{1,0:T(8,128)(2,1)S(1)} %get-tuple-element.119), channel_id=1, source_target_pairs={{0,16},{1,17},{2,18},{3,19},{4,20},{5,21},{6,22},{7,23},{8,24},{9,... | collective-permute-start | bytes 368648 | tf_op jit(solution)/shard_map/ppermute | solution.py:542
  14.6 17.3 %collective-permute-start.2 = (bf16[9,48,384]{2,1,0:T(8,128)(2,1)S(1)}, bf16[9,48,384]{2,1,0:T(8,128)(2,1)S(1)}, u32[]{:S(2)}, u32[]{:S(2)}) collective-permute-start(bf16[9,48,384]{2,1,0:T(8,128)(2,1)S(1)} %get-tuple-element.120), channel_id=1, source_target_pairs={{0,16},{1,17},{2,18},{3,19},{4,20},{5,21},{6,22},{7,23},{8,24},{9,... | collective-permute-start | bytes 995336 | tf_op jit(solution)/shard_map/ppermute | solution.py:542
  14.7 7.5 %collective-permute-start.8 = (bf16[2,160,384]{2,1,0:T(8,128)(2,1)S(1)}, bf16[2,160,384]{2,1,0:T(8,128)(2,1)S(1)}, u32[]{:S(2)}, u32[]{:S(2)}) collective-permute-start(bf16[2,160,384]{2,1,0:T(8,128)(2,1)S(1)} %pad_maximum_fusion.3.refs_0_), channel_id=1, source_target_pairs={{0,2},{1,3},{2,0},{3,1},{4,6},{5,7},{6,4},{7,5},{8,10},{9,11},{10,... | collective-permute-start | bytes 737288 | tf_op jit(solution)/shard_map/ppermute | solution.py:542
  16.3 10.7 %collective-permute-start.3 = (bf16[2,160,384]{2,1,0:T(8,128)(2,1)S(1)}, bf16[2,160,384]{2,1,0:T(8,128)(2,1)S(1)}, u32[]{:S(2)}, u32[]{:S(2)}) collective-permute-start(bf16[2,160,384]{2,1,0:T(8,128)(2,1)S(1)} %pad_maximum_fusion.3.refs_0_), channel_id=1, source_target_pairs={{0,8},{1,9},{2,10},{3,11},{4,12},{5,13},{6,14},{7,15},{8,0},{9,1},... | collective-permute-start | bytes 737288 | tf_op jit(solution)/shard_map/ppermute | solution.py:542
  20.3 13.0 %collective-permute-start.18 = (bf16[2,160,384]{2,1,0:T(8,128)(2,1)S(1)}, bf16[2,160,384]{2,1,0:T(8,128)(2,1)S(1)}, u32[]{:S(2)}, u32[]{:S(2)}) collective-permute-start(bf16[2,160,384]{2,1,0:T(8,128)(2,1)S(1)} %pad_maximum_fusion.3.refs_0_), channel_id=1, source_target_pairs={{0,4},{1,5},{2,6},{3,7},{4,0},{5,1},{6,2},{7,3},{8,12},{9,13},{10,... | collective-permute-start | bytes 737288 | tf_op jit(solution)/shard_map/ppermute | solution.py:542
  22.2 11.2 %collective-permute-start.9 = (bf16[2,160,384]{2,1,0:T(8,128)(2,1)S(1)}, bf16[2,160,384]{2,1,0:T(8,128)(2,1)S(1)}, u32[]{:S(2)}, u32[]{:S(2)}) collective-permute-start(bf16[2,160,384]{2,1,0:T(8,128)(2,1)S(1)} %collective-permute-done.8.refs_2_), channel_id=1, source_target_pairs={{0,4},{1,5},{2,6},{3,7},{4,0},{5,1},{6,2},{7,3},{8,12},{9,13},{10,... | collective-permute-start | bytes 737288 | tf_op jit(solution)/shard_map/ppermute | solution.py:542
  32.0 9.3 %collective-permute-start.4 = (bf16[2,5,48,384]{3,2,1,0:T(8,128)(2,1)S(1)}, bf16[2,5,48,384]{3,2,1,0:T(8,128)(2,1)S(1)}, u32[]{:S(2)}, u32[]{:S(2)}) collective-permute-start(bf16[2,5,48,384]{3,2,1,0:T(8,128)(2,1)S(1)} %pad_maximum_fusion.refs_0_), channel_id=1, source_target_pairs={{0,8},{1,9},{2,10},{3,11},{4,12},{5,13},{6,14},{7,15},{8,0},{9,1},... | collective-permute-start | bytes 1105928 | tf_op jit(solution)/shard_map/ppermute | solution.py:542
  33.9 8.3 %collective-permute-start.22 = (bf16[2,160,384]{2,1,0:T(8,128)(2,1)S(1)}, bf16[2,160,384]{2,1,0:T(8,128)(2,1)S(1)}, u32[]{:S(2)}, u32[]{:S(2)}) collective-permute-start(bf16[2,160,384]{2,1,0:T(8,128)(2,1)S(1)} %collective-permute-done.8.refs_2_), channel_id=1, source_target_pairs={{0,1},{1,0},{2,3},{3,2},{4,5},{5,4},{6,7},{7,6},{8,9},{9,8},{10,11... | collective-permute-start | bytes 737288 | tf_op jit(solution)/shard_map/ppermute | solution.py:542
  38.7 11.3 %collective-permute-start.12 = (bf16[2,5,48,384]{3,2,1,0:T(8,128)(2,1)S(1)}, bf16[2,5,48,384]{3,2,1,0:T(8,128)(2,1)S(1)}, u32[]{:S(2)}, u32[]{:S(2)}) collective-permute-start(bf16[2,5,48,384]{3,2,1,0:T(8,128)(2,1)S(1)} %pad_maximum_fusion.refs_0_), channel_id=1, source_target_pairs={{0,2},{1,3},{2,0},{3,1},{4,6},{5,7},{6,4},{7,5},{8,10},{9,11},{10,... | collective-permute-start | bytes 1105928 | tf_op jit(solution)/shard_map/ppermute | solution.py:542
  39.7 20.6 %collective-permute-start.13 = (bf16[2,5,48,384]{3,2,1,0:T(8,128)(2,1)S(1)}, bf16[2,5,48,384]{3,2,1,0:T(8,128)(2,1)S(1)}, u32[]{:S(2)}, u32[]{:S(2)}) collective-permute-start(bf16[2,5,48,384]{3,2,1,0:T(8,128)(2,1)S(1)} %pad_maximum_fusion.refs_0_), channel_id=1, source_target_pairs={{0,4},{1,5},{2,6},{3,7},{4,0},{5,1},{6,2},{7,3},{8,12},{9,13},{10,... | collective-permute-start | bytes 1105928 | tf_op jit(solution)/shard_map/ppermute | solution.py:542
  41.3 19.5 %collective-permute-start.6 = (bf16[2,5,48,384]{3,2,1,0:T(8,128)(2,1)S(1)}, bf16[2,5,48,384]{3,2,1,0:T(8,128)(2,1)S(1)}, u32[]{:S(2)}, u32[]{:S(2)}) collective-permute-start(bf16[2,5,48,384]{3,2,1,0:T(8,128)(2,1)S(1)} %collective-permute-done.4.refs_1_), channel_id=1, source_target_pairs={{0,2},{1,3},{2,0},{3,1},{4,6},{5,7},{6,4},{7,5},{8,10},{9,11},{10,... | collective-permute-start | bytes 1105928 | tf_op jit(solution)/shard_map/ppermute | solution.py:542
  42.2 18.1 %collective-permute-start.19 = (bf16[2,160,384]{2,1,0:T(8,128)(2,1)S(1)}, bf16[2,160,384]{2,1,0:T(8,128)(2,1)}, u32[]{:S(2)}, u32[]{:S(2)}) collective-permute-start(bf16[2,160,384]{2,1,0:T(8,128)(2,1)S(1)} %collective-permute-done.10.refs_5_), channel_id=1, source_target_pairs={{0,2},{1,3},{2,0},{3,1},{4,6},{5,7},{6,4},{7,5},{8,10},{9,11},{10,... | collective-permute-start | bytes 737288 | tf_op jit(solution)/shard_map/ppermute | solution.py:542
  43.3 17.7 %collective-permute-start.5 = (bf16[2,5,48,384]{3,2,1,0:T(8,128)(2,1)S(1)}, bf16[2,5,48,384]{3,2,1,0:T(8,128)(2,1)S(1)}, u32[]{:S(2)}, u32[]{:S(2)}) collective-permute-start(bf16[2,5,48,384]{3,2,1,0:T(8,128)(2,1)S(1)} %collective-permute-done.4.refs_1_), channel_id=1, source_target_pairs={{0,4},{1,5},{2,6},{3,7},{4,0},{5,1},{6,2},{7,3},{8,12},{9,13},{10,... | collective-permute-start | bytes 1105928 | tf_op jit(solution)/shard_map/ppermute | solution.py:542
  50.0 16.9 %collective-permute-start.17 = (bf16[2,5,48,384]{3,2,1,0:T(8,128)(2,1)S(1)}, bf16[2,5,48,384]{3,2,1,0:T(8,128)(2,1)S(1)}, u32[]{:S(2)}, u32[]{:S(2)}) collective-permute-start(bf16[2,5,48,384]{3,2,1,0:T(8,128)(2,1)S(1)} %collective-permute-done.12.refs_2_), channel_id=1, source_target_pairs={{0,4},{1,5},{2,6},{3,7},{4,0},{5,1},{6,2},{7,3},{8,12},{9,13},{10,... | collective-permute-start | bytes 1105928 | tf_op jit(solution)/shard_map/ppermute | solution.py:542
  61.0 7.3 %collective-permute-start.27 = (bf16[2,160,384]{2,1,0:T(8,128)(2,1)}, bf16[2,160,384]{2,1,0:T(8,128)(2,1)}, u32[]{:S(2)}, u32[]{:S(2)}) collective-permute-start(bf16[2,160,384]{2,1,0:T(8,128)(2,1)} %collective-permute-done.19.refs_7_), channel_id=1, source_target_pairs={{0,1},{1,0},{2,3},{3,2},{4,5},{5,4},{6,7},{7,6},{8,9},{9,8},{10,11... | collective-permute-start | bytes 737288 | tf_op jit(solution)/shard_map/ppermute | solution.py:542
  61.8 18.6 %collective-permute-start.16 = (bf16[2,192,384]{2,1,0:T(8,128)(2,1)S(1)}, bf16[2,192,384]{2,1,0:T(8,128)(2,1)}, u32[]{:S(2)}, u32[]{:S(2)}) collective-permute-start(bf16[2,192,384]{2,1,0:T(8,128)(2,1)S(1)} %pad_maximum_fusion.1.refs_0_), channel_id=1, source_target_pairs={{0,8},{1,9},{2,10},{3,11},{4,12},{5,13},{6,14},{7,15},{8,0},{9,1},... | collective-permute-start | bytes 884744 | tf_op jit(solution)/shard_map/ppermute | solution.py:542
  63.2 17.2 %collective-permute-start.15 = (bf16[2,192,384]{2,1,0:T(8,128)(2,1)S(1)}, bf16[2,192,384]{2,1,0:T(8,128)(2,1)}, u32[]{:S(2)}, u32[]{:S(2)}) collective-permute-start(bf16[2,192,384]{2,1,0:T(8,128)(2,1)S(1)} %pad_maximum_fusion.1.refs_0_), channel_id=1, source_target_pairs={{0,4},{1,5},{2,6},{3,7},{4,0},{5,1},{6,2},{7,3},{8,12},{9,13},{10,... | collective-permute-start | bytes 884744 | tf_op jit(solution)/shard_map/ppermute | solution.py:542
  64.1 16.4 %collective-permute-start.14 = (bf16[2,192,384]{2,1,0:T(8,128)(2,1)S(1)}, bf16[2,192,384]{2,1,0:T(8,128)(2,1)}, u32[]{:S(2)}, u32[]{:S(2)}) collective-permute-start(bf16[2,192,384]{2,1,0:T(8,128)(2,1)S(1)} %pad_maximum_fusion.1.refs_0_), channel_id=1, source_target_pairs={{0,2},{1,3},{2,0},{3,1},{4,6},{5,7},{6,4},{7,5},{8,10},{9,11},{10,... | collective-permute-start | bytes 884744 | tf_op jit(solution)/shard_map/ppermute | solution.py:542
  66.9 13.6 %collective-permute-start.7 = (bf16[2,5,48,384]{3,2,1,0:T(8,128)(2,1)S(1)}, bf16[2,5,48,384]{3,2,1,0:T(8,128)(2,1)}, u32[]{:S(2)}, u32[]{:S(2)}) collective-permute-start(bf16[2,5,48,384]{3,2,1,0:T(8,128)(2,1)S(1)} %collective-permute-done.5.refs_5_), channel_id=1, source_target_pairs={{0,2},{1,3},{2,0},{3,1},{4,6},{5,7},{6,4},{7,5},{8,10},{9,11},{10,... | collective-permute-start | bytes 1105928 | tf_op jit(solution)/shard_map/ppermute | solution.py:542
  83.8 15.6 %collective-permute-start.29 = (bf16[2,192,384]{2,1,0:T(8,128)(2,1)}, bf16[2,192,384]{2,1,0:T(8,128)(2,1)S(1)}, u32[]{:S(2)}, u32[]{:S(2)}) collective-permute-start(bf16[2,192,384]{2,1,0:T(8,128)(2,1)} %collective-permute-done.16.refs_1_), channel_id=1, source_target_pairs={{0,4},{1,5},{2,6},{3,7},{4,0},{5,1},{6,2},{7,3},{8,12},{9,13},{10,... | collective-permute-start | bytes 884744 | tf_op jit(solution)/shard_map/ppermute | solution.py:542
  85.0 14.4 %collective-permute-start.30 = (bf16[2,192,384]{2,1,0:T(8,128)(2,1)}, bf16[2,192,384]{2,1,0:T(8,128)(2,1)S(1)}, u32[]{:S(2)}, u32[]{:S(2)}) collective-permute-start(bf16[2,192,384]{2,1,0:T(8,128)(2,1)} %collective-permute-done.14.refs_2_), channel_id=1, source_target_pairs={{0,4},{1,5},{2,6},{3,7},{4,0},{5,1},{6,2},{7,3},{8,12},{9,13},{10,... | collective-permute-start | bytes 884744 | tf_op jit(solution)/shard_map/ppermute | solution.py:542
  85.9 13.6 %collective-permute-start.28 = (bf16[2,192,384]{2,1,0:T(8,128)(2,1)}, bf16[2,192,384]{2,1,0:T(8,128)(2,1)S(1)}, u32[]{:S(2)}, u32[]{:S(2)}) collective-permute-start(bf16[2,192,384]{2,1,0:T(8,128)(2,1)} %collective-permute-done.16.refs_1_), channel_id=1, source_target_pairs={{0,2},{1,3},{2,0},{3,1},{4,6},{5,7},{6,4},{7,5},{8,10},{9,11},{10,... | collective-permute-start | bytes 884744 | tf_op jit(solution)/shard_map/ppermute | solution.py:542
  99.4 8.3 %collective-permute-start.39 = (bf16[2,192,384]{2,1,0:T(8,128)(2,1)S(1)}, bf16[2,192,384]{2,1,0:T(8,128)(2,1)S(1)}, u32[]{:S(2)}, u32[]{:S(2)}) collective-permute-start(bf16[2,192,384]{2,1,0:T(8,128)(2,1)S(1)} %collective-permute-done.29.refs_5_), channel_id=1, source_target_pairs={{0,2},{1,3},{2,0},{3,1},{4,6},{5,7},{6,4},{7,5},{8,10},{9,11},{10,... | collective-permute-start | bytes 884744 | tf_op jit(solution)/shard_map/ppermute | solution.py:542
  101.5 7.4 %collective-permute-start.41 = (bf16[2,192,384]{2,1,0:T(8,128)(2,1)}, bf16[2,192,384]{2,1,0:T(8,128)(2,1)S(1)}, u32[]{:S(2)}, u32[]{:S(2)}) collective-permute-start(bf16[2,192,384]{2,1,0:T(8,128)(2,1)} %collective-permute-done.16.refs_1_), channel_id=1, source_target_pairs={{0,1},{1,0},{2,3},{3,2},{4,5},{5,4},{6,7},{7,6},{8,9},{9,8},{10,11... | collective-permute-start | bytes 884744 | tf_op jit(solution)/shard_map/ppermute | solution.py:542
  110.6 10.4 %collective-permute-start.48 = (bf16[16,192,384]{2,1,0:T(8,128)(2,1)}, bf16[16,192,384]{2,1,0:T(8,128)(2,1)S(1)}, u32[]{:S(2)}, u32[]{:S(2)}) collective-permute-start(bf16[16,192,384]{2,1,0:T(8,128)(2,1)} %get-tuple-element.152), channel_id=1, source_target_pairs={{0,1},{1,0},{2,3},{3,2},{4,5},{5,4},{6,7},{7,6},{8,9},{9,8},{10,11... | collective-permute-start | bytes 7077896 | tf_op jit(solution)/shard_map/ppermute | solution.py:542
  121.3 16.2 %collective-permute-start.50 = (bf16[4,192,384]{2,1,0:T(8,128)(2,1)S(1)}, bf16[4,192,384]{2,1,0:T(8,128)(2,1)S(1)}, u32[]{:S(2)}, u32[]{:S(2)}) collective-permute-start(bf16[4,192,384]{2,1,0:T(8,128)(2,1)S(1)} %get-tuple-element.226), channel_id=1, source_target_pairs={{0,4},{1,5},{2,6},{3,7},{4,0},{5,1},{6,2},{7,3},{8,12},{9,13},{10,... | collective-permute-start | bytes 1769480 | tf_op jit(solution)/shard_map/ppermute | solution.py:542
  122.6 15.8 %collective-permute-start.49 = (bf16[4,192,384]{2,1,0:T(8,128)(2,1)S(1)}, bf16[4,192,384]{2,1,0:T(8,128)(2,1)S(1)}, u32[]{:S(2)}, u32[]{:S(2)}) collective-permute-start(bf16[4,192,384]{2,1,0:T(8,128)(2,1)S(1)} %get-tuple-element.227), channel_id=1, source_target_pairs={{0,2},{1,3},{2,0},{3,1},{4,6},{5,7},{6,4},{7,5},{8,10},{9,11},{10,... | collective-permute-start | bytes 1769480 | tf_op jit(solution)/shard_map/ppermute | solution.py:542
  138.4 12.4 %collective-permute-start.51 = (bf16[16,5,48,384]{3,2,1,0:T(8,128)(2,1)}, bf16[16,5,48,384]{3,2,1,0:T(8,128)(2,1)S(1)}, u32[]{:S(2)}, u32[]{:S(2)}) collective-permute-start(bf16[16,5,48,384]{3,2,1,0:T(8,128)(2,1)} %get-tuple-element.169), channel_id=1, source_target_pairs={{0,1},{1,0},{2,3},{3,2},{4,5},{5,4},{6,7},{7,6},{8,9},{9,8},{10,11... | collective-permute-start | bytes 8847368 | tf_op jit(solution)/shard_map/ppermute | solution.py:542
  138.6 11.4 %collective-permute-start.53 = (bf16[2,192,384]{2,1,0:T(8,128)(2,1)S(1)}, bf16[2,192,384]{2,1,0:T(8,128)(2,1)S(1)}, u32[]{:S(2)}, u32[]{:S(2)}) collective-permute-start(bf16[2,192,384]{2,1,0:T(8,128)(2,1)S(1)} %get-tuple-element.224), channel_id=1, source_target_pairs={{0,4},{1,5},{2,6},{3,7},{4,0},{5,1},{6,2},{7,3},{8,12},{9,13},{10,... | collective-permute-start | bytes 884744 | tf_op jit(solution)/shard_map/ppermute | solution.py:542
  139.5 10.5 %collective-permute-start.52 = (bf16[2,192,384]{2,1,0:T(8,128)(2,1)S(1)}, bf16[2,192,384]{2,1,0:T(8,128)(2,1)S(1)}, u32[]{:S(2)}, u32[]{:S(2)}) collective-permute-start(bf16[2,192,384]{2,1,0:T(8,128)(2,1)S(1)} %get-tuple-element.225), channel_id=1, source_target_pairs={{0,2},{1,3},{2,0},{3,1},{4,6},{5,7},{6,4},{7,5},{8,10},{9,11},{10,... | collective-permute-start | bytes 884744 | tf_op jit(solution)/shard_map/ppermute | solution.py:542
  151.0 11.8 %collective-permute-start.57 = (bf16[2,5,48,384]{3,2,1,0:T(8,128)(2,1)S(1)}, bf16[2,5,48,384]{3,2,1,0:T(8,128)(2,1)S(1)}, u32[]{:S(2)}, u32[]{:S(2)}) collective-permute-start(bf16[2,5,48,384]{3,2,1,0:T(8,128)(2,1)S(1)} %get-tuple-element.222), channel_id=1, source_target_pairs={{0,4},{1,5},{2,6},{3,7},{4,0},{5,1},{6,2},{7,3},{8,12},{9,13},{10,... | collective-permute-start | bytes 1105928 | tf_op jit(solution)/shard_map/ppermute | solution.py:542
  151.9 10.9 %collective-permute-start.56 = (bf16[2,5,48,384]{3,2,1,0:T(8,128)(2,1)S(1)}, bf16[2,5,48,384]{3,2,1,0:T(8,128)(2,1)S(1)}, u32[]{:S(2)}, u32[]{:S(2)}) collective-permute-start(bf16[2,5,48,384]{3,2,1,0:T(8,128)(2,1)S(1)} %get-tuple-element.223), channel_id=1, source_target_pairs={{0,2},{1,3},{2,0},{3,1},{4,6},{5,7},{6,4},{7,5},{8,10},{9,11},{10,... | collective-permute-start | bytes 1105928 | tf_op jit(solution)/shard_map/ppermute | solution.py:542
  152.7 10.0 %collective-permute-start.58 = (bf16[2,192,384]{2,1,0:T(8,128)(2,1)S(1)}, bf16[2,192,384]{2,1,0:T(8,128)(2,1)S(1)}, u32[]{:S(2)}, u32[]{:S(2)}) collective-permute-start(bf16[2,192,384]{2,1,0:T(8,128)(2,1)S(1)} %add_convert_fusion.9), channel_id=1, source_target_pairs={{0,8},{1,9},{2,10},{3,11},{4,12},{5,13},{6,14},{7,15},{8,0},{9,1},... | collective-permute-start | bytes 884744 | tf_op jit(solution)/shard_map/ppermute | solution.py:542
  165.3 12.7 %collective-permute-start.60 = (bf16[2,176,384]{2,1,0:T(8,128)(2,1)S(1)}, bf16[2,176,384]{2,1,0:T(8,128)(2,1)S(1)}, u32[]{:S(2)}, u32[]{:S(2)}) collective-permute-start(bf16[2,176,384]{2,1,0:T(8,128)(2,1)S(1)} %get-tuple-element.232), channel_id=1, source_target_pairs={{0,4},{1,5},{2,6},{3,7},{4,0},{5,1},{6,2},{7,3},{8,12},{9,13},{10,... | collective-permute-start | bytes 811016 | tf_op jit(solution)/shard_map/ppermute | solution.py:542
  166.2 11.7 %collective-permute-start.59 = (bf16[2,176,384]{2,1,0:T(8,128)(2,1)S(1)}, bf16[2,176,384]{2,1,0:T(8,128)(2,1)S(1)}, u32[]{:S(2)}, u32[]{:S(2)}) collective-permute-start(bf16[2,176,384]{2,1,0:T(8,128)(2,1)S(1)} %get-tuple-element.233), channel_id=1, source_target_pairs={{0,2},{1,3},{2,0},{3,1},{4,6},{5,7},{6,4},{7,5},{8,10},{9,11},{10,... | collective-permute-start | bytes 811016 | tf_op jit(solution)/shard_map/ppermute | solution.py:542
  167.4 9.7 %collective-permute-start.61 = (bf16[192,384]{1,0:T(8,128)(2,1)S(1)}, bf16[192,384]{1,0:T(8,128)(2,1)S(1)}, u32[]{:S(2)}, u32[]{:S(2)}) collective-permute-start(bf16[192,384]{1,0:T(8,128)(2,1)S(1)} %fusion.1), channel_id=1, source_target_pairs={{0,16},{1,17},{2,18},{3,19},{4,20},{5,21},{6,22},{7,23},{8,24},{9,... | collective-permute-start | bytes 442376 | tf_op jit(solution)/shard_map/ppermute | solution.py:542
  170.4 12.0 %collective-permute-start.65 = (bf16[2,5,48,384]{3,2,1,0:T(8,128)(2,1)S(1)}, bf16[2,5,48,384]{3,2,1,0:T(8,128)(2,1)S(1)}, u32[]{:S(2)}, u32[]{:S(2)}) collective-permute-start(bf16[2,5,48,384]{3,2,1,0:T(8,128)(2,1)S(1)} %get-tuple-element.220), channel_id=1, source_target_pairs={{0,4},{1,5},{2,6},{3,7},{4,0},{5,1},{6,2},{7,3},{8,12},{9,13},{10,... | collective-permute-start | bytes 1105928 | tf_op jit(solution)/shard_map/ppermute | solution.py:542
  171.9 11.5 %collective-permute-start.64 = (bf16[2,5,48,384]{3,2,1,0:T(8,128)(2,1)S(1)}, bf16[2,5,48,384]{3,2,1,0:T(8,128)(2,1)S(1)}, u32[]{:S(2)}, u32[]{:S(2)}) collective-permute-start(bf16[2,5,48,384]{3,2,1,0:T(8,128)(2,1)S(1)} %get-tuple-element.221), channel_id=1, source_target_pairs={{0,2},{1,3},{2,0},{3,1},{4,6},{5,7},{6,4},{7,5},{8,10},{9,11},{10,... | collective-permute-start | bytes 1105928 | tf_op jit(solution)/shard_map/ppermute | solution.py:542
  177.2 11.1 %collective-permute-start.62 = (bf16[2,176,384]{2,1,0:T(8,128)(2,1)S(1)}, bf16[2,176,384]{2,1,0:T(8,128)(2,1)S(1)}, u32[]{:S(2)}, u32[]{:S(2)}) collective-permute-start(bf16[2,176,384]{2,1,0:T(8,128)(2,1)S(1)} %get-tuple-element.230), channel_id=1, source_target_pairs={{0,2},{1,3},{2,0},{3,1},{4,6},{5,7},{6,4},{7,5},{8,10},{9,11},{10,... | collective-permute-start | bytes 811016 | tf_op jit(solution)/shard_map/ppermute | solution.py:542
  178.0 10.3 %collective-permute-start.63 = (bf16[2,176,384]{2,1,0:T(8,128)(2,1)S(1)}, bf16[2,176,384]{2,1,0:T(8,128)(2,1)S(1)}, u32[]{:S(2)}, u32[]{:S(2)}) collective-permute-start(bf16[2,176,384]{2,1,0:T(8,128)(2,1)S(1)} %add_convert_fusion.13), channel_id=1, source_target_pairs={{0,4},{1,5},{2,6},{3,7},{4,0},{5,1},{6,2},{7,3},{8,12},{9,13},{10,... | collective-permute-start | bytes 811016 | tf_op jit(solution)/shard_map/ppermute | solution.py:542
  184.7 10.8 %collective-permute-start.71 = (bf16[2,5,48,384]{3,2,1,0:T(8,128)(2,1)S(1)}, bf16[2,5,48,384]{3,2,1,0:T(8,128)(2,1)}, u32[]{:S(2)}, u32[]{:S(2)}) collective-permute-start(bf16[2,5,48,384]{3,2,1,0:T(8,128)(2,1)S(1)} %get-tuple-element.219), channel_id=1, source_target_pairs={{0,8},{1,9},{2,10},{3,11},{4,12},{5,13},{6,14},{7,15},{8,0},{9,1},... | collective-permute-start | bytes 1105928 | tf_op jit(solution)/shard_map/ppermute | solution.py:542
  186.6 11.8 %collective-permute-start.69 = (bf16[2,5,48,384]{3,2,1,0:T(8,128)(2,1)}, bf16[2,5,48,384]{3,2,1,0:T(8,128)(2,1)}, u32[]{:S(2)}, u32[]{:S(2)}) collective-permute-start(bf16[2,5,48,384]{3,2,1,0:T(8,128)(2,1)} %get-tuple-element.199), channel_id=1, source_target_pairs={{0,2},{1,3},{2,0},{3,1},{4,6},{5,7},{6,4},{7,5},{8,10},{9,11},{10,... | collective-permute-start | bytes 1105928 | tf_op jit(solution)/shard_map/ppermute | solution.py:542
  187.0 11.4 %collective-permute-start.70 = (bf16[2,5,48,384]{3,2,1,0:T(8,128)(2,1)}, bf16[2,5,48,384]{3,2,1,0:T(8,128)(2,1)}, u32[]{:S(2)}, u32[]{:S(2)}) collective-permute-start(bf16[2,5,48,384]{3,2,1,0:T(8,128)(2,1)} %get-tuple-element.200), channel_id=1, source_target_pairs={{0,4},{1,5},{2,6},{3,7},{4,0},{5,1},{6,2},{7,3},{8,12},{9,13},{10,... | collective-permute-start | bytes 1105928 | tf_op jit(solution)/shard_map/ppermute | solution.py:542
  189.3 13.1 %collective-permute-start.68 = (bf16[2,176,384]{2,1,0:T(8,128)(2,1)}, bf16[2,176,384]{2,1,0:T(8,128)(2,1)S(1)}, u32[]{:S(2)}, u32[]{:S(2)}) collective-permute-start(bf16[2,176,384]{2,1,0:T(8,128)(2,1)} %get-tuple-element.228), channel_id=1, source_target_pairs={{0,8},{1,9},{2,10},{3,11},{4,12},{5,13},{6,14},{7,15},{8,0},{9,1},... | collective-permute-start | bytes 811016 | tf_op jit(solution)/shard_map/ppermute | solution.py:542
  192.0 10.4 %collective-permute-start.66 = (bf16[2,176,384]{2,1,0:T(8,128)(2,1)}, bf16[2,176,384]{2,1,0:T(8,128)(2,1)S(1)}, u32[]{:S(2)}, u32[]{:S(2)}) collective-permute-start(bf16[2,176,384]{2,1,0:T(8,128)(2,1)} %get-tuple-element.203), channel_id=1, source_target_pairs={{0,2},{1,3},{2,0},{3,1},{4,6},{5,7},{6,4},{7,5},{8,10},{9,11},{10,... | collective-permute-start | bytes 811016 | tf_op jit(solution)/shard_map/ppermute | solution.py:542
  199.7 12.7 %collective-permute-start.74 = (bf16[5,48,384]{2,1,0:T(8,128)(2,1)S(1)}, bf16[5,48,384]{2,1,0:T(8,128)(2,1)S(1)}, u32[]{:S(2)}, u32[]{:S(2)}) collective-permute-start(bf16[5,48,384]{2,1,0:T(8,128)(2,1)S(1)} %fusion), channel_id=1, source_target_pairs={{0,16},{1,17},{2,18},{3,19},{4,20},{5,21},{6,22},{7,23},{8,24},{9,... | collective-permute-start | bytes 552968 | tf_op jit(solution)/shard_map/ppermute | solution.py:542
  203.7 10.2 %collective-permute-start.72 = (bf16[176,384]{1,0:T(8,128)(2,1)S(1)}, bf16[176,384]{1,0:T(8,128)(2,1)S(1)}, u32[]{:S(2)}, u32[]{:S(2)}) collective-permute-start(bf16[176,384]{1,0:T(8,128)(2,1)S(1)} %fusion.2), channel_id=1, source_target_pairs={{0,16},{1,17},{2,18},{3,19},{4,20},{5,21},{6,22},{7,23},{8,24},{9,... | collective-permute-start | bytes 405512 | tf_op jit(solution)/shard_map/ppermute | solution.py:542
  207.5 8.7 %collective-permute-start.76 = (f32[96,384]{1,0:T(8,128)S(1)}, f32[96,384]{1,0:T(8,128)S(1)}, u32[]{:S(2)}, u32[]{:S(2)}) collective-permute-start(f32[96,384]{1,0:T(8,128)S(1)} %slice_select_fusion.2), channel_id=1, source_target_pairs={{0,1},{1,0},{2,3},{3,2},{4,5},{5,4},{6,7},{7,6},{8,9},{9,8},{10,11... | collective-permute-start | bytes 442376 | tf_op jit(solution)/shard_map/ppermute | solution.py:542
  (83 other events, 1046.0 us)
where the time goes:
time: 221 us; the launch traced here: 220 us
  Pallas kernels  72 us (33%)
  starting transfers between devices  67.9 us (31%)
  waiting for transfers between devices  64.5 us (29%)
  other arithmetic  9.86 us (4%)
  local copies, waits for them, and re-layouts  4.48 us (2%)
    pallas_call x13, Pallas kernels, call(): pl.pallas_call(kernel, out_shape=outs, in_specs=[pl.BlockSpec(memory_spac...  72 us
    ppermute x77, starting transfers between devices, swap(): return lax.ppermute(value, AXES, [(i, i ^ flip) for i in range(2 * CHIPS)])  67.9 us
    ppermute x77, waiting for transfers between devices, swap(): return lax.ppermute(value, AXES, [(i, i ^ flip) for i in range(2 * CHIPS)])  64.5 us
    convert_element_type x10, other arithmetic, rounded_sum(): return total.astype(BF16)  4.93 us
  transfers between devices with their start and end apart: 77, of which 32 were waited for; matrix products, arithmetic and copies ran while one was open for 5% of the time, Pallas kernels for 31%

commit v1 on v0

--- a/solution.py
+++ b/solution.py
@@ -911,14 +911,14 @@
         down = gathered(lo3, hi3, y_lo3, y_hi3, x_lo3, x_hi3, d_lo3, d_hi3)
         scatter1 = Scatter(*pair_down, *down)
         gbu, gpre, w_down_all, *pair_up = layer.mlp_down(pos, gout, slope, n2, down)
-        scatter1.first(gbu)
+        scatter1.diagonal(gbu)
         sums, gmid, gmixed, *pair_up = layer.mid_backward(
             tie(pos, *scatter1.out), vec, gbd, gbu, gpre, gout, mid, mixed, *w_mid, *pair_up
         )
-        scatter1.second(sums)
-        scatter2 = Scatter(*pair_up, scatter1.in_y, scatter1.in_x)
+        scatter1.hi(sums)
+        scatter2 = Scatter(*pair_up, scatter1.in_x)
         gbq, gqkv, give = layer.attn_backward(tie(pos, *scatter1.out), gmixed, qkv, soft)
-        scatter1.third(gbq)
+        scatter1.lo(gbq)
         n1, give = hold((n1, give), *scatter1.out)
         n1_got, g_got = swap(n1, 0), swap(give, 0)
         scatter2.diagonal(gbq)

time: 221 us -> 219 us (level)
  waiting for transfers between devices: 64.5 us -> 58.1 us
  starting transfers between devices: 67.9 us -> 71.2 us
    ppermute x77 -> x79, waiting for transfers between devices: 64.5 us -> 58.1 us  [swap(): return lax.ppermute(value, AXES, [(i, i ^ flip) for i in range(2 * CHIPS)])]
    ppermute x77 -> x79, starting transfers between devices: 67.9 us -> 71.2 us  [swap(): return lax.ppermute(value, AXES, [(i, i ^ flip) for i in range(2 * CHIPS)])]
  transfers between devices with their start and end apart: 77 -> 79, of which waited for: 32 -> 29; matrix products, arithmetic and copies ran while one was open for 5% -> 5% of each run, Pallas kernels for 31% -> 32%
where the time goes in v1:
time: 219 us; the launch traced here: 218 us
  Pallas kernels  72.2 us (33%)
  starting transfers between devices  71.2 us (33%)
  waiting for transfers between devices  58.1 us (27%)
  other arithmetic  9.87 us (5%)
  local copies, waits for them, and re-layouts  5.35 us (2%)
    pallas_call x13, Pallas kernels, call(): pl.pallas_call(kernel, out_shape=outs, in_specs=[pl.BlockSpec(memory_spac...  72.2 us
    ppermute x79, starting transfers between devices, swap(): return lax.ppermute(value, AXES, [(i, i ^ flip) for i in range(2 * CHIPS)])  71.2 us
    ppermute x79, waiting for transfers between devices, swap(): return lax.ppermute(value, AXES, [(i, i ^ flip) for i in range(2 * CHIPS)])  58.1 us
    convert_element_type x10, other arithmetic, rounded_sum(): return total.astype(BF16)  4.94 us
  transfers between devices with their start and end apart: 79, of which 29 were waited for; matrix products, arithmetic and copies ran while one was open for 5% of the time, Pallas kernels for 32%

profile of v1, /device:TPU:0, one launch (start us, length us, event | category | flops | bytes accessed | tf_op | source)
XLA Modules:
  0.0 218.3 jit_solution(1700692777375233555)
XLA Ops:
  4.3 4.0 %collective-permute-start.1 = (bf16[160,384]{1,0:T(8,128)(2,1)S(1)}, bf16[160,384]{1,0:T(8,128)(2,1)S(1)}, u32[]{:S(2)}, u32[]{:S(2)}) collective-permute-start(bf16[160,384]{1,0:T(8,128)(2,1)S(1)} %get-tuple-element.121), channel_id=1, source_target_pairs={{0,16},{1,17},{2,18},{3,19},{4,20},{5,21},{6,22},{7,23},{8,24},{9,... | collective-permute-start | bytes 368648 | tf_op jit(solution)/shard_map/ppermute | solution.py:542
  8.3 6.3 %collective-permute-done.1 = bf16[160,384]{1,0:T(8,128)(2,1)S(1)} collective-permute-done((bf16[160,384]{1,0:T(8,128)(2,1)S(1)}, bf16[160,384]{1,0:T(8,128)(2,1)S(1)}, u32[]{:S(2)}, u32[]{:S(2)}) %collective-permute-start.1) | collective-permute-done | bytes 122912 | tf_op jit(solution)/shard_map/ppermute | solution.py:542
  14.7 1.6 collective-permute-start.8
  16.3 4.0 %collective-permute-start.3 = (bf16[2,160,384]{2,1,0:T(8,128)(2,1)S(1)}, bf16[2,160,384]{2,1,0:T(8,128)(2,1)S(1)}, u32[]{:S(2)}, u32[]{:S(2)}) collective-permute-start(bf16[2,160,384]{2,1,0:T(8,128)(2,1)S(1)} %pad_maximum_fusion.3.refs_0_), channel_id=1, source_target_pairs={{0,8},{1,9},{2,10},{3,11},{4,12},{5,13},{6,14},{7,15},{8,0},{9,1},... | collective-permute-start | bytes 737288 | tf_op jit(solution)/shard_map/ppermute | solution.py:542
  20.3 1.6 collective-permute-start.18
  23.4 3.6 %collective-permute-done.3.refs_1_ = bf16[2,160,384]{2,1,0:T(8,128)(2,1)S(1)} collective-permute-done((bf16[2,160,384]{2,1,0:T(8,128)(2,1)S(1)}, bf16[2,160,384]{2,1,0:T(8,128)(2,1)S(1)}, u32[]{:S(2)}, u32[]{:S(2)}) %collective-permute-start.3) | collective-permute-done | bytes 245792 | tf_op jit(solution)/shard_map/ppermute | solution.py:542
  28.2 3.6 %collective-permute-done.2 = bf16[9,48,384]{2,1,0:T(8,128)(2,1)S(1)} collective-permute-done((bf16[9,48,384]{2,1,0:T(8,128)(2,1)S(1)}, bf16[9,48,384]{2,1,0:T(8,128)(2,1)S(1)}, u32[]{:S(2)}, u32[]{:S(2)}) %collective-permute-start.2) | collective-permute-done | bytes 331808 | tf_op jit(solution)/shard_map/ppermute | solution.py:542
  32.1 1.3 collective-permute-start.10
  34.0 4.8 %collective-permute-done.10.refs_5_ = bf16[2,160,384]{2,1,0:T(8,128)(2,1)S(1)} collective-permute-done((bf16[2,160,384]{2,1,0:T(8,128)(2,1)S(1)}, bf16[2,160,384]{2,1,0:T(8,128)(2,1)S(1)}, u32[]{:S(2)}, u32[]{:S(2)}) %collective-permute-start.10) | collective-permute-done | bytes 245792 | tf_op jit(solution)/shard_map/ppermute | solution.py:542
  39.7 1.6 collective-permute-start.13
  44.2 5.8 %collective-permute-done.12.refs_2_ = bf16[2,5,48,384]{3,2,1,0:T(8,128)(2,1)S(1)} collective-permute-done((bf16[2,5,48,384]{3,2,1,0:T(8,128)(2,1)S(1)}, bf16[2,5,48,384]{3,2,1,0:T(8,128)(2,1)S(1)}, u32[]{:S(2)}, u32[]{:S(2)}) %collective-permute-start.12) | collective-permute-done | bytes 368672 | tf_op jit(solution)/shard_map/ppermute | solution.py:542
  50.6 9.7 %collective-permute-done.19.refs_7_ = bf16[2,160,384]{2,1,0:T(8,128)(2,1)} collective-permute-done((bf16[2,160,384]{2,1,0:T(8,128)(2,1)S(1)}, bf16[2,160,384]{2,1,0:T(8,128)(2,1)}, u32[]{:S(2)}, u32[]{:S(2)}) %collective-permute-start.19) | collective-permute-done | bytes 245792 | tf_op jit(solution)/shard_map/ppermute | solution.py:542
  61.8 1.4 collective-permute-start.16
  64.1 1.5 collective-permute-start.14
  65.6 1.4 collective-permute-done.17.refs_6_
  68.3 12.1 %attn_forward.1 = (f32[16,768]{1,0:T(8,128)S(1)}, bf16[512,768]{1,0:T(8,128)(2,1)S(1)}, bf16[512,2304]{1,0:T(8,128)(2,1)S(1)}, bf16[24,256,256]{2,1,0:T(8,128)(2...) custom-call(s32[2]{0:T(128)S(1)} %pad_add_fusion.pos_ref, s32[2,1,256]{2,1,0:T(1,128)S(1)} %reshape.123.segr_ref, ...), custom_call_target="tpu_custom_call" | custom-call | flops 2617245696 | bytes 15388680 | tf_op jit(solution)/shard_map/attn_forward/pallas_call | solution.py:517
  85.9 1.5 collective-permute-start.28
  88.3 9.9 %mlp_up.1 = (f32[8,768]{1,0:T(8,128)S(1)}, bf16[512,768]{1,0:T(8,128)(2,1)S(1)}, f32[512,768]{1,0:T(8,128)S(1)}, bf16[512,3072]{1,0:T(8,128)(2,1)S(1)}, bf16[512...) custom-call(s32[2]{0:T(128)S(1)} %pad_add_fusion.pos_ref, ...), custom_call_target="tpu_custom_call" | custom-call | flops 3019898880 | bytes 23668744 | tf_op jit(solution)/shard_map/mlp_up/pallas_call | solution.py:517
  99.4 1.6 collective-permute-start.39
  102.0 4.4 %down_grad.1 = (bf16[16,192,384]{2,1,0:T(8,128)(2,1)}, bf16[16,192,384]{2,1,0:T(8,128)(2,1)}) custom-call(s32[2]{0:T(128)S(1)} %pad_add_fusion.pos_ref, bf16[512,3072]{1,0:T(8,128)(2,1)S(1)} %get-tuple-element.149.act_ref, bf16[512,768]{1,0:T(8,128)(2,1)S(1)} %get-tuple-element.150.gout_ref), custom_call_target="tpu_custom_call" | custom-call | flops 2415919104 | bytes 8650760 | tf_op jit(solution)/shard_map/down_grad/pallas_call | solution.py:517
  106.4 1.3 collective-permute-done.39.refs_7_
  111.3 9.7 %mlp_down.1 = (f32[8,768]{1,0:T(8,128)S(1)}, bf16[512,3072]{1,0:T(8,128)(2,1)S(1)}, bf16[3072,768]{1,0:T(8,128)(2,1)S(1)}, bf16[16,5,48,384]{3,2,1,0:T(8,128)(2,1)}, bf16[16,5,48,384]{3,2,1,0:T(8,128)(2,1)}) custom-call(s32[2]{0:T(128)S(1)} %pad_add_fusion.pos_ref, bf16[512,768]{1,0:T(8,128)(2,1)S(1)} %get-tuple-element.150.gout_ref, ...), custom_call_target="tpu_custom_call" | custom-call | flops 4831838208 | bytes 23224328 | tf_op jit(solution)/shard_map/mlp_down/pallas_call | solution.py:517
  123.7 8.8 %mid_backward.1 = (f32[16,768]{1,0:T(8,128)S(1)}, f32[512,768]{1,0:T(8,128)S(1)}, bf16[512,768]{1,0:T(8,128)(2,1)S(1)}, bf16[16,5,48,384]{3,2,1,0:T(8,128)(2,1)}, bf16[16,5,48,384]{3,2,1,0:T(8,128)(2,1)}) custom-call(s32[2]{0:T(128)S(1)} %pad_add_fusion.pos_ref, ...), custom_call_target="tpu_custom_call", output_to_operand_aliasing={{3}: (10, {}), {4}: (11, {})} | custom-call | flops 3623878656 | bytes 26492936 | tf_op jit(solution)/shard_map/mid_backward/pallas_call | solution.py:517
  134.8 9.0 %attn_backward.1 = (f32[8,768]{1,0:T(8,128)S(1)}, bf16[512,2304]{1,0:T(8,128)(2,1)S(1)}, bf16[512,1152]{1,0:T(8,128)(2,1)S(1)}) custom-call(s32[2]{0:T(128)S(1)} %pad_add_fusion.pos_ref, bf16[512,768]{1,0:T(8,128)(2,1)S(1)} %get-tuple-element.173.gmixed, bf16[512,2304]{1,0:T(8,128)(2,1)S(1)} %get-tuple-element.174.qkv_ref, ...), custom_call_target="tpu_custom_call" | custom-call | flops 2013265920 | bytes 9854984 | tf_op jit(solution)/shard_map/attn_backward/pallas_call | solution.py:517
  145.8 1.3 collective-permute-start.57
  149.9 2.0 collective-permute-start.60
  152.0 8.1 %qkv_grad.1 = (bf16[512,768]{1,0:T(8,128)(2,1)}, bf16[16,176,384]{2,1,0:T(8,128)(2,1)}) custom-call(s32[2]{0:T(128)S(1)} %pad_add_fusion.pos_ref, f32[16,768]{1,0:T(8,128)S(1)} %get-tuple-element.135.vec_ref, f32[16,768]{1,0:T(8,128)S(1)} %get-tuple-element.168.sums_ref, f32[8,768]{1,0:T(8,128)S(1)} %get-tuple-element.176.gbq_ref, ...), custom_call_target="tpu_custom_call" | custom-call | flops 3623878656 | bytes 14082056 | tf_op jit(solution)/shard_map/qkv_grad/pallas_call | solution.py:517
  160.4 1.4 copy-done.1
  163.8 1.5 collective-permute-start.61
  165.4 3.2 %collective-permute-start.63 = (bf16[192,384]{1,0:T(8,128)(2,1)S(1)}, bf16[192,384]{1,0:T(8,128)(2,1)S(1)}, u32[]{:S(2)}, u32[]{:S(2)}) collective-permute-start(bf16[192,384]{1,0:T(8,128)(2,1)S(1)} %fusion.1), channel_id=1, source_target_pairs={{0,16},{1,17},{2,18},{3,19},{4,20},{5,21},{6,22},{7,23},{8,24},{9,... | collective-permute-start | bytes 442376 | tf_op jit(solution)/shard_map/ppermute | solution.py:542
  168.6 1.5 collective-permute-start.67
  170.1 1.4 collective-permute-start.66
  171.4 4.0 %layer_out.1 = bf16[512,768]{1,0:T(8,128)(2,1)} custom-call(s32[2]{0:T(128)S(1)} %pad_add_fusion.pos_ref, f32[16,768]{1,0:T(8,128)S(1)} %get-tuple-element.135.vec_ref, bf16[512,3072]{1,0:T(8,128)(2,1)S(1)} %get-tuple-element.149.act_ref, f32[512,768]{1,0:T(8,128)S(1)} %get-tuple-element.161.mid_ref, bf16[3072,768]{1,0:T(8,128)(2,1)S(1)} %get-tuple-element.196.w_down), custom_call_target="tpu_custom_call" | custom-call | flops 2415919104 | bytes 10272776 | tf_op jit(solution)/shard_map/layer_out/pallas_call | solution.py:517
  177.9 2.9 %collective-permute-done.66 = bf16[2,5,48,384]{3,2,1,0:T(8,128)(2,1)S(1)} collective-permute-done((bf16[2,5,48,384]{3,2,1,0:T(8,128)(2,1)S(1)}, bf16[2,5,48,384]{3,2,1,0:T(8,128)(2,1)S(1)}, u32[]{:S(2)}, u32[]{:S(2)}) %collective-permute-start.66) | collective-permute-done | bytes 368672 | tf_op jit(solution)/shard_map/ppermute | solution.py:542
  180.8 1.3 add_convert_fusion
  182.2 1.8 collective-permute-start.73
  184.0 1.8 collective-permute-start.72
  187.6 1.8 collective-permute-start.70
  189.4 3.3 %collective-permute-done.73 = bf16[2,5,48,384]{3,2,1,0:T(8,128)(2,1)} collective-permute-done((bf16[2,5,48,384]{3,2,1,0:T(8,128)(2,1)S(1)}, bf16[2,5,48,384]{3,2,1,0:T(8,128)(2,1)}, u32[]{:S(2)}, u32[]{:S(2)}) %collective-permute-start.73) | collective-permute-done | bytes 368672 | tf_op jit(solution)/shard_map/ppermute | solution.py:542
  192.7 2.7 %collective-permute-done.71 = bf16[2,5,48,384]{3,2,1,0:T(8,128)(2,1)} collective-permute-done((bf16[2,5,48,384]{3,2,1,0:T(8,128)(2,1)}, bf16[2,5,48,384]{3,2,1,0:T(8,128)(2,1)}, u32[]{:S(2)}, u32[]{:S(2)}) %collective-permute-start.71) | collective-permute-done | bytes 368672 | tf_op jit(solution)/shard_map/ppermute | solution.py:542
  195.4 1.3 fusion
  196.8 3.8 %collective-permute-start.76 = (bf16[5,48,384]{2,1,0:T(8,128)(2,1)S(1)}, bf16[5,48,384]{2,1,0:T(8,128)(2,1)S(1)}, u32[]{:S(2)}, u32[]{:S(2)}) collective-permute-start(bf16[5,48,384]{2,1,0:T(8,128)(2,1)S(1)} %fusion), channel_id=1, source_target_pairs={{0,16},{1,17},{2,18},{3,19},{4,20},{5,21},{6,22},{7,23},{8,24},{9,... | collective-permute-start | bytes 552968 | tf_op jit(solution)/shard_map/ppermute | solution.py:542
  201.8 3.0 %collective-permute-start.74 = (bf16[176,384]{1,0:T(8,128)(2,1)S(1)}, bf16[176,384]{1,0:T(8,128)(2,1)S(1)}, u32[]{:S(2)}, u32[]{:S(2)}) collective-permute-start(bf16[176,384]{1,0:T(8,128)(2,1)S(1)} %fusion.2), channel_id=1, source_target_pairs={{0,16},{1,17},{2,18},{3,19},{4,20},{5,21},{6,22},{7,23},{8,24},{9,... | collective-permute-start | bytes 405512 | tf_op jit(solution)/shard_map/ppermute | solution.py:542
  204.8 1.4 convert_add_fusion.5
  206.3 4.1 %collective-permute-done.76 = bf16[5,48,384]{2,1,0:T(8,128)(2,1)S(1)} collective-permute-done((bf16[5,48,384]{2,1,0:T(8,128)(2,1)S(1)}, bf16[5,48,384]{2,1,0:T(8,128)(2,1)S(1)}, u32[]{:S(2)}, u32[]{:S(2)}) %collective-permute-start.76) | collective-permute-done | bytes 184352 | tf_op jit(solution)/shard_map/ppermute | solution.py:542
  210.4 1.3 convert_add_fusion
  211.9 1.7 finish.1
  217.0 1.3 spread_up.1
  (264 shorter events, 48.3 us)
Async XLA Ops:
  4.3 10.3 %collective-permute-start.1 = (bf16[160,384]{1,0:T(8,128)(2,1)S(1)}, bf16[160,384]{1,0:T(8,128)(2,1)S(1)}, u32[]{:S(2)}, u32[]{:S(2)}) collective-permute-start(bf16[160,384]{1,0:T(8,128)(2,1)S(1)} %get-tuple-element.121), channel_id=1, source_target_pairs={{0,16},{1,17},{2,18},{3,19},{4,20},{5,21},{6,22},{7,23},{8,24},{9,... | collective-permute-start | bytes 368648 | tf_op jit(solution)/shard_map/ppermute | solution.py:542
  14.6 17.3 %collective-permute-start.2 = (bf16[9,48,384]{2,1,0:T(8,128)(2,1)S(1)}, bf16[9,48,384]{2,1,0:T(8,128)(2,1)S(1)}, u32[]{:S(2)}, u32[]{:S(2)}) collective-permute-start(bf16[9,48,384]{2,1,0:T(8,128)(2,1)S(1)} %get-tuple-element.122), channel_id=1, source_target_pairs={{0,16},{1,17},{2,18},{3,19},{4,20},{5,21},{6,22},{7,23},{8,24},{9,... | collective-permute-start | bytes 995336 | tf_op jit(solution)/shard_map/ppermute | solution.py:542
  16.3 10.7 %collective-permute-start.3 = (bf16[2,160,384]{2,1,0:T(8,128)(2,1)S(1)}, bf16[2,160,384]{2,1,0:T(8,128)(2,1)S(1)}, u32[]{:S(2)}, u32[]{:S(2)}) collective-permute-start(bf16[2,160,384]{2,1,0:T(8,128)(2,1)S(1)} %pad_maximum_fusion.3.refs_0_), channel_id=1, source_target_pairs={{0,8},{1,9},{2,10},{3,11},{4,12},{5,13},{6,14},{7,15},{8,0},{9,1},... | collective-permute-start | bytes 737288 | tf_op jit(solution)/shard_map/ppermute | solution.py:542
  20.3 13.0 %collective-permute-start.18 = (bf16[2,160,384]{2,1,0:T(8,128)(2,1)S(1)}, bf16[2,160,384]{2,1,0:T(8,128)(2,1)S(1)}, u32[]{:S(2)}, u32[]{:S(2)}) collective-permute-start(bf16[2,160,384]{2,1,0:T(8,128)(2,1)S(1)} %pad_maximum_fusion.3.refs_0_), channel_id=1, source_target_pairs={{0,4},{1,5},{2,6},{3,7},{4,0},{5,1},{6,2},{7,3},{8,12},{9,13},{10,... | collective-permute-start | bytes 737288 | tf_op jit(solution)/shard_map/ppermute | solution.py:542
  22.2 11.2 %collective-permute-start.9 = (bf16[2,160,384]{2,1,0:T(8,128)(2,1)S(1)}, bf16[2,160,384]{2,1,0:T(8,128)(2,1)S(1)}, u32[]{:S(2)}, u32[]{:S(2)}) collective-permute-start(bf16[2,160,384]{2,1,0:T(8,128)(2,1)S(1)} %collective-permute-done.8.refs_2_), channel_id=1, source_target_pairs={{0,4},{1,5},{2,6},{3,7},{4,0},{5,1},{6,2},{7,3},{8,12},{9,13},{10,... | collective-permute-start | bytes 737288 | tf_op jit(solution)/shard_map/ppermute | solution.py:542
  32.0 9.3 %collective-permute-start.4 = (bf16[2,5,48,384]{3,2,1,0:T(8,128)(2,1)S(1)}, bf16[2,5,48,384]{3,2,1,0:T(8,128)(2,1)S(1)}, u32[]{:S(2)}, u32[]{:S(2)}) collective-permute-start(bf16[2,5,48,384]{3,2,1,0:T(8,128)(2,1)S(1)} %pad_maximum_fusion.refs_0_), channel_id=1, source_target_pairs={{0,8},{1,9},{2,10},{3,11},{4,12},{5,13},{6,14},{7,15},{8,0},{9,1},... | collective-permute-start | bytes 1105928 | tf_op jit(solution)/shard_map/ppermute | solution.py:542
  33.9 8.3 %collective-permute-start.22 = (bf16[2,160,384]{2,1,0:T(8,128)(2,1)S(1)}, bf16[2,160,384]{2,1,0:T(8,128)(2,1)S(1)}, u32[]{:S(2)}, u32[]{:S(2)}) collective-permute-start(bf16[2,160,384]{2,1,0:T(8,128)(2,1)S(1)} %collective-permute-done.8.refs_2_), channel_id=1, source_target_pairs={{0,1},{1,0},{2,3},{3,2},{4,5},{5,4},{6,7},{7,6},{8,9},{9,8},{10,11... | collective-permute-start | bytes 737288 | tf_op jit(solution)/shard_map/ppermute | solution.py:542
  38.7 11.3 %collective-permute-start.12 = (bf16[2,5,48,384]{3,2,1,0:T(8,128)(2,1)S(1)}, bf16[2,5,48,384]{3,2,1,0:T(8,128)(2,1)S(1)}, u32[]{:S(2)}, u32[]{:S(2)}) collective-permute-start(bf16[2,5,48,384]{3,2,1,0:T(8,128)(2,1)S(1)} %pad_maximum_fusion.refs_0_), channel_id=1, source_target_pairs={{0,2},{1,3},{2,0},{3,1},{4,6},{5,7},{6,4},{7,5},{8,10},{9,11},{10,... | collective-permute-start | bytes 1105928 | tf_op jit(solution)/shard_map/ppermute | solution.py:542
  39.7 20.6 %collective-permute-start.13 = (bf16[2,5,48,384]{3,2,1,0:T(8,128)(2,1)S(1)}, bf16[2,5,48,384]{3,2,1,0:T(8,128)(2,1)S(1)}, u32[]{:S(2)}, u32[]{:S(2)}) collective-permute-start(bf16[2,5,48,384]{3,2,1,0:T(8,128)(2,1)S(1)} %pad_maximum_fusion.refs_0_), channel_id=1, source_target_pairs={{0,4},{1,5},{2,6},{3,7},{4,0},{5,1},{6,2},{7,3},{8,12},{9,13},{10,... | collective-permute-start | bytes 1105928 | tf_op jit(solution)/shard_map/ppermute | solution.py:542
  41.3 19.5 %collective-permute-start.6 = (bf16[2,5,48,384]{3,2,1,0:T(8,128)(2,1)S(1)}, bf16[2,5,48,384]{3,2,1,0:T(8,128)(2,1)S(1)}, u32[]{:S(2)}, u32[]{:S(2)}) collective-permute-start(bf16[2,5,48,384]{3,2,1,0:T(8,128)(2,1)S(1)} %collective-permute-done.4.refs_1_), channel_id=1, source_target_pairs={{0,2},{1,3},{2,0},{3,1},{4,6},{5,7},{6,4},{7,5},{8,10},{9,11},{10,... | collective-permute-start | bytes 1105928 | tf_op jit(solution)/shard_map/ppermute | solution.py:542
  42.2 18.1 %collective-permute-start.19 = (bf16[2,160,384]{2,1,0:T(8,128)(2,1)S(1)}, bf16[2,160,384]{2,1,0:T(8,128)(2,1)}, u32[]{:S(2)}, u32[]{:S(2)}) collective-permute-start(bf16[2,160,384]{2,1,0:T(8,128)(2,1)S(1)} %collective-permute-done.10.refs_5_), channel_id=1, source_target_pairs={{0,2},{1,3},{2,0},{3,1},{4,6},{5,7},{6,4},{7,5},{8,10},{9,11},{10,... | collective-permute-start | bytes 737288 | tf_op jit(solution)/shard_map/ppermute | solution.py:542
  43.3 17.7 %collective-permute-start.5 = (bf16[2,5,48,384]{3,2,1,0:T(8,128)(2,1)S(1)}, bf16[2,5,48,384]{3,2,1,0:T(8,128)(2,1)S(1)}, u32[]{:S(2)}, u32[]{:S(2)}) collective-permute-start(bf16[2,5,48,384]{3,2,1,0:T(8,128)(2,1)S(1)} %collective-permute-done.4.refs_1_), channel_id=1, source_target_pairs={{0,4},{1,5},{2,6},{3,7},{4,0},{5,1},{6,2},{7,3},{8,12},{9,13},{10,... | collective-permute-start | bytes 1105928 | tf_op jit(solution)/shard_map/ppermute | solution.py:542
  50.0 16.9 %collective-permute-start.17 = (bf16[2,5,48,384]{3,2,1,0:T(8,128)(2,1)S(1)}, bf16[2,5,48,384]{3,2,1,0:T(8,128)(2,1)S(1)}, u32[]{:S(2)}, u32[]{:S(2)}) collective-permute-start(bf16[2,5,48,384]{3,2,1,0:T(8,128)(2,1)S(1)} %collective-permute-done.12.refs_2_), channel_id=1, source_target_pairs={{0,4},{1,5},{2,6},{3,7},{4,0},{5,1},{6,2},{7,3},{8,12},{9,13},{10,... | collective-permute-start | bytes 1105928 | tf_op jit(solution)/shard_map/ppermute | solution.py:542
  61.8 18.6 %collective-permute-start.16 = (bf16[2,192,384]{2,1,0:T(8,128)(2,1)S(1)}, bf16[2,192,384]{2,1,0:T(8,128)(2,1)}, u32[]{:S(2)}, u32[]{:S(2)}) collective-permute-start(bf16[2,192,384]{2,1,0:T(8,128)(2,1)S(1)} %pad_maximum_fusion.1.refs_0_), channel_id=1, source_target_pairs={{0,8},{1,9},{2,10},{3,11},{4,12},{5,13},{6,14},{7,15},{8,0},{9,1},... | collective-permute-start | bytes 884744 | tf_op jit(solution)/shard_map/ppermute | solution.py:542
  63.2 17.2 %collective-permute-start.15 = (bf16[2,192,384]{2,1,0:T(8,128)(2,1)S(1)}, bf16[2,192,384]{2,1,0:T(8,128)(2,1)}, u32[]{:S(2)}, u32[]{:S(2)}) collective-permute-start(bf16[2,192,384]{2,1,0:T(8,128)(2,1)S(1)} %pad_maximum_fusion.1.refs_0_), channel_id=1, source_target_pairs={{0,4},{1,5},{2,6},{3,7},{4,0},{5,1},{6,2},{7,3},{8,12},{9,13},{10,... | collective-permute-start | bytes 884744 | tf_op jit(solution)/shard_map/ppermute | solution.py:542
  64.1 16.4 %collective-permute-start.14 = (bf16[2,192,384]{2,1,0:T(8,128)(2,1)S(1)}, bf16[2,192,384]{2,1,0:T(8,128)(2,1)}, u32[]{:S(2)}, u32[]{:S(2)}) collective-permute-start(bf16[2,192,384]{2,1,0:T(8,128)(2,1)S(1)} %pad_maximum_fusion.1.refs_0_), channel_id=1, source_target_pairs={{0,2},{1,3},{2,0},{3,1},{4,6},{5,7},{6,4},{7,5},{8,10},{9,11},{10,... | collective-permute-start | bytes 884744 | tf_op jit(solution)/shard_map/ppermute | solution.py:542
  66.9 13.6 %collective-permute-start.7 = (bf16[2,5,48,384]{3,2,1,0:T(8,128)(2,1)S(1)}, bf16[2,5,48,384]{3,2,1,0:T(8,128)(2,1)}, u32[]{:S(2)}, u32[]{:S(2)}) collective-permute-start(bf16[2,5,48,384]{3,2,1,0:T(8,128)(2,1)S(1)} %collective-permute-done.5.refs_5_), channel_id=1, source_target_pairs={{0,2},{1,3},{2,0},{3,1},{4,6},{5,7},{6,4},{7,5},{8,10},{9,11},{10,... | collective-permute-start | bytes 1105928 | tf_op jit(solution)/shard_map/ppermute | solution.py:542
  83.8 15.6 %collective-permute-start.29 = (bf16[2,192,384]{2,1,0:T(8,128)(2,1)}, bf16[2,192,384]{2,1,0:T(8,128)(2,1)S(1)}, u32[]{:S(2)}, u32[]{:S(2)}) collective-permute-start(bf16[2,192,384]{2,1,0:T(8,128)(2,1)} %collective-permute-done.16.refs_1_), channel_id=1, source_target_pairs={{0,4},{1,5},{2,6},{3,7},{4,0},{5,1},{6,2},{7,3},{8,12},{9,13},{10,... | collective-permute-start | bytes 884744 | tf_op jit(solution)/shard_map/ppermute | solution.py:542
  85.0 14.4 %collective-permute-start.30 = (bf16[2,192,384]{2,1,0:T(8,128)(2,1)}, bf16[2,192,384]{2,1,0:T(8,128)(2,1)S(1)}, u32[]{:S(2)}, u32[]{:S(2)}) collective-permute-start(bf16[2,192,384]{2,1,0:T(8,128)(2,1)} %collective-permute-done.14.refs_2_), channel_id=1, source_target_pairs={{0,4},{1,5},{2,6},{3,7},{4,0},{5,1},{6,2},{7,3},{8,12},{9,13},{10,... | collective-permute-start | bytes 884744 | tf_op jit(solution)/shard_map/ppermute | solution.py:542
  85.9 13.6 %collective-permute-start.28 = (bf16[2,192,384]{2,1,0:T(8,128)(2,1)}, bf16[2,192,384]{2,1,0:T(8,128)(2,1)S(1)}, u32[]{:S(2)}, u32[]{:S(2)}) collective-permute-start(bf16[2,192,384]{2,1,0:T(8,128)(2,1)} %collective-permute-done.16.refs_1_), channel_id=1, source_target_pairs={{0,2},{1,3},{2,0},{3,1},{4,6},{5,7},{6,4},{7,5},{8,10},{9,11},{10,... | collective-permute-start | bytes 884744 | tf_op jit(solution)/shard_map/ppermute | solution.py:542
  99.4 8.3 %collective-permute-start.39 = (bf16[2,192,384]{2,1,0:T(8,128)(2,1)S(1)}, bf16[2,192,384]{2,1,0:T(8,128)(2,1)S(1)}, u32[]{:S(2)}, u32[]{:S(2)}) collective-permute-start(bf16[2,192,384]{2,1,0:T(8,128)(2,1)S(1)} %collective-permute-done.29.refs_5_), channel_id=1, source_target_pairs={{0,2},{1,3},{2,0},{3,1},{4,6},{5,7},{6,4},{7,5},{8,10},{9,11},{10,... | collective-permute-start | bytes 884744 | tf_op jit(solution)/shard_map/ppermute | solution.py:542
  110.6 10.4 %collective-permute-start.48 = (bf16[16,192,384]{2,1,0:T(8,128)(2,1)}, bf16[16,192,384]{2,1,0:T(8,128)(2,1)S(1)}, u32[]{:S(2)}, u32[]{:S(2)}) collective-permute-start(bf16[16,192,384]{2,1,0:T(8,128)(2,1)} %get-tuple-element.154), channel_id=1, source_target_pairs={{0,1},{1,0},{2,3},{3,2},{4,5},{5,4},{6,7},{7,6},{8,9},{9,8},{10,11... | collective-permute-start | bytes 7077896 | tf_op jit(solution)/shard_map/ppermute | solution.py:542
  121.2 11.3 %collective-permute-start.50 = (bf16[2,192,384]{2,1,0:T(8,128)(2,1)S(1)}, bf16[2,192,384]{2,1,0:T(8,128)(2,1)S(1)}, u32[]{:S(2)}, u32[]{:S(2)}) collective-permute-start(bf16[2,192,384]{2,1,0:T(8,128)(2,1)S(1)} %get-tuple-element.233), channel_id=1, source_target_pairs={{0,4},{1,5},{2,6},{3,7},{4,0},{5,1},{6,2},{7,3},{8,12},{9,13},{10,... | collective-permute-start | bytes 884744 | tf_op jit(solution)/shard_map/ppermute | solution.py:542
  122.4 10.1 %collective-permute-start.49 = (bf16[2,192,384]{2,1,0:T(8,128)(2,1)S(1)}, bf16[2,192,384]{2,1,0:T(8,128)(2,1)S(1)}, u32[]{:S(2)}, u32[]{:S(2)}) collective-permute-start(bf16[2,192,384]{2,1,0:T(8,128)(2,1)S(1)} %get-tuple-element.234), channel_id=1, source_target_pairs={{0,2},{1,3},{2,0},{3,1},{4,6},{5,7},{6,4},{7,5},{8,10},{9,11},{10,... | collective-permute-start | bytes 884744 | tf_op jit(solution)/shard_map/ppermute | solution.py:542
  132.5 12.2 %collective-permute-start.51 = (bf16[16,5,48,384]{3,2,1,0:T(8,128)(2,1)}, bf16[16,5,48,384]{3,2,1,0:T(8,128)(2,1)S(1)}, u32[]{:S(2)}, u32[]{:S(2)}) collective-permute-start(bf16[16,5,48,384]{3,2,1,0:T(8,128)(2,1)} %get-tuple-element.170), channel_id=1, source_target_pairs={{0,1},{1,0},{2,3},{3,2},{4,5},{5,4},{6,7},{7,6},{8,9},{9,8},{10,11... | collective-permute-start | bytes 8847368 | tf_op jit(solution)/shard_map/ppermute | solution.py:542
  133.1 10.7 %collective-permute-start.53 = (bf16[2,192,384]{2,1,0:T(8,128)(2,1)S(1)}, bf16[2,192,384]{2,1,0:T(8,128)(2,1)S(1)}, u32[]{:S(2)}, u32[]{:S(2)}) collective-permute-start(bf16[2,192,384]{2,1,0:T(8,128)(2,1)S(1)} %get-tuple-element.231), channel_id=1, source_target_pairs={{0,4},{1,5},{2,6},{3,7},{4,0},{5,1},{6,2},{7,3},{8,12},{9,13},{10,... | collective-permute-start | bytes 884744 | tf_op jit(solution)/shard_map/ppermute | solution.py:542
  134.3 9.5 %collective-permute-start.52 = (bf16[2,192,384]{2,1,0:T(8,128)(2,1)S(1)}, bf16[2,192,384]{2,1,0:T(8,128)(2,1)S(1)}, u32[]{:S(2)}, u32[]{:S(2)}) collective-permute-start(bf16[2,192,384]{2,1,0:T(8,128)(2,1)S(1)} %get-tuple-element.232), channel_id=1, source_target_pairs={{0,2},{1,3},{2,0},{3,1},{4,6},{5,7},{6,4},{7,5},{8,10},{9,11},{10,... | collective-permute-start | bytes 884744 | tf_op jit(solution)/shard_map/ppermute | solution.py:542
  145.8 14.3 %collective-permute-start.57 = (bf16[2,5,48,384]{3,2,1,0:T(8,128)(2,1)S(1)}, bf16[2,5,48,384]{3,2,1,0:T(8,128)(2,1)S(1)}, u32[]{:S(2)}, u32[]{:S(2)}) collective-permute-start(bf16[2,5,48,384]{3,2,1,0:T(8,128)(2,1)S(1)} %get-tuple-element.226), channel_id=1, source_target_pairs={{0,4},{1,5},{2,6},{3,7},{4,0},{5,1},{6,2},{7,3},{8,12},{9,13},{10,... | collective-permute-start | bytes 1105928 | tf_op jit(solution)/shard_map/ppermute | solution.py:542
  147.1 13.0 %collective-permute-start.56 = (bf16[2,5,48,384]{3,2,1,0:T(8,128)(2,1)S(1)}, bf16[2,5,48,384]{3,2,1,0:T(8,128)(2,1)S(1)}, u32[]{:S(2)}, u32[]{:S(2)}) collective-permute-start(bf16[2,5,48,384]{3,2,1,0:T(8,128)(2,1)S(1)} %get-tuple-element.227), channel_id=1, source_target_pairs={{0,2},{1,3},{2,0},{3,1},{4,6},{5,7},{6,4},{7,5},{8,10},{9,11},{10,... | collective-permute-start | bytes 1105928 | tf_op jit(solution)/shard_map/ppermute | solution.py:542
  148.3 16.9 %collective-permute-start.58 = (bf16[2,192,384]{2,1,0:T(8,128)(2,1)S(1)}, bf16[2,192,384]{2,1,0:T(8,128)(2,1)S(1)}, u32[]{:S(2)}, u32[]{:S(2)}) collective-permute-start(bf16[2,192,384]{2,1,0:T(8,128)(2,1)S(1)} %get-tuple-element.180), channel_id=1, source_target_pairs={{0,2},{1,3},{2,0},{3,1},{4,6},{5,7},{6,4},{7,5},{8,10},{9,11},{10,... | collective-permute-start | bytes 884744 | tf_op jit(solution)/shard_map/ppermute | solution.py:542
  149.2 16.1 %collective-permute-start.59 = (bf16[2,192,384]{2,1,0:T(8,128)(2,1)S(1)}, bf16[2,192,384]{2,1,0:T(8,128)(2,1)S(1)}, u32[]{:S(2)}, u32[]{:S(2)}) collective-permute-start(bf16[2,192,384]{2,1,0:T(8,128)(2,1)S(1)} %get-tuple-element.181), channel_id=1, source_target_pairs={{0,4},{1,5},{2,6},{3,7},{4,0},{5,1},{6,2},{7,3},{8,12},{9,13},{10,... | collective-permute-start | bytes 884744 | tf_op jit(solution)/shard_map/ppermute | solution.py:542
  149.9 10.2 %collective-permute-start.60 = (bf16[2,192,384]{2,1,0:T(8,128)(2,1)S(1)}, bf16[2,192,384]{2,1,0:T(8,128)(2,1)S(1)}, u32[]{:S(2)}, u32[]{:S(2)}) collective-permute-start(bf16[2,192,384]{2,1,0:T(8,128)(2,1)S(1)} %get-tuple-element.230), channel_id=1, source_target_pairs={{0,8},{1,9},{2,10},{3,11},{4,12},{5,13},{6,14},{7,15},{8,0},{9,1},... | collective-permute-start | bytes 884744 | tf_op jit(solution)/shard_map/ppermute | solution.py:542
  162.7 13.6 %collective-permute-start.62 = (bf16[2,176,384]{2,1,0:T(8,128)(2,1)S(1)}, bf16[2,176,384]{2,1,0:T(8,128)(2,1)S(1)}, u32[]{:S(2)}, u32[]{:S(2)}) collective-permute-start(bf16[2,176,384]{2,1,0:T(8,128)(2,1)S(1)} %get-tuple-element.239), channel_id=1, source_target_pairs={{0,4},{1,5},{2,6},{3,7},{4,0},{5,1},{6,2},{7,3},{8,12},{9,13},{10,... | collective-permute-start | bytes 811016 | tf_op jit(solution)/shard_map/ppermute | solution.py:542
  163.8 12.5 %collective-permute-start.61 = (bf16[2,176,384]{2,1,0:T(8,128)(2,1)S(1)}, bf16[2,176,384]{2,1,0:T(8,128)(2,1)S(1)}, u32[]{:S(2)}, u32[]{:S(2)}) collective-permute-start(bf16[2,176,384]{2,1,0:T(8,128)(2,1)S(1)} %get-tuple-element.240), channel_id=1, source_target_pairs={{0,2},{1,3},{2,0},{3,1},{4,6},{5,7},{6,4},{7,5},{8,10},{9,11},{10,... | collective-permute-start | bytes 811016 | tf_op jit(solution)/shard_map/ppermute | solution.py:542
  165.4 10.1 %collective-permute-start.63 = (bf16[192,384]{1,0:T(8,128)(2,1)S(1)}, bf16[192,384]{1,0:T(8,128)(2,1)S(1)}, u32[]{:S(2)}, u32[]{:S(2)}) collective-permute-start(bf16[192,384]{1,0:T(8,128)(2,1)S(1)} %fusion.1), channel_id=1, source_target_pairs={{0,16},{1,17},{2,18},{3,19},{4,20},{5,21},{6,22},{7,23},{8,24},{9,... | collective-permute-start | bytes 442376 | tf_op jit(solution)/shard_map/ppermute | solution.py:542
  168.6 9.3 %collective-permute-start.67 = (bf16[2,5,48,384]{3,2,1,0:T(8,128)(2,1)S(1)}, bf16[2,5,48,384]{3,2,1,0:T(8,128)(2,1)S(1)}, u32[]{:S(2)}, u32[]{:S(2)}) collective-permute-start(bf16[2,5,48,384]{3,2,1,0:T(8,128)(2,1)S(1)} %get-tuple-element.224), channel_id=1, source_target_pairs={{0,4},{1,5},{2,6},{3,7},{4,0},{5,1},{6,2},{7,3},{8,12},{9,13},{10,... | collective-permute-start | bytes 1105928 | tf_op jit(solution)/shard_map/ppermute | solution.py:542
  170.1 10.8 %collective-permute-start.66 = (bf16[2,5,48,384]{3,2,1,0:T(8,128)(2,1)S(1)}, bf16[2,5,48,384]{3,2,1,0:T(8,128)(2,1)S(1)}, u32[]{:S(2)}, u32[]{:S(2)}) collective-permute-start(bf16[2,5,48,384]{3,2,1,0:T(8,128)(2,1)S(1)} %get-tuple-element.225), channel_id=1, source_target_pairs={{0,2},{1,3},{2,0},{3,1},{4,6},{5,7},{6,4},{7,5},{8,10},{9,11},{10,... | collective-permute-start | bytes 1105928 | tf_op jit(solution)/shard_map/ppermute | solution.py:542
  175.5 11.1 %collective-permute-start.64 = (bf16[2,176,384]{2,1,0:T(8,128)(2,1)S(1)}, bf16[2,176,384]{2,1,0:T(8,128)(2,1)S(1)}, u32[]{:S(2)}, u32[]{:S(2)}) collective-permute-start(bf16[2,176,384]{2,1,0:T(8,128)(2,1)S(1)} %get-tuple-element.237), channel_id=1, source_target_pairs={{0,2},{1,3},{2,0},{3,1},{4,6},{5,7},{6,4},{7,5},{8,10},{9,11},{10,... | collective-permute-start | bytes 811016 | tf_op jit(solution)/shard_map/ppermute | solution.py:542
  176.3 10.3 %collective-permute-start.65 = (bf16[2,176,384]{2,1,0:T(8,128)(2,1)S(1)}, bf16[2,176,384]{2,1,0:T(8,128)(2,1)S(1)}, u32[]{:S(2)}, u32[]{:S(2)}) collective-permute-start(bf16[2,176,384]{2,1,0:T(8,128)(2,1)S(1)} %add_convert_fusion.15), channel_id=1, source_target_pairs={{0,4},{1,5},{2,6},{3,7},{4,0},{5,1},{6,2},{7,3},{8,12},{9,13},{10,... | collective-permute-start | bytes 811016 | tf_op jit(solution)/shard_map/ppermute | solution.py:542
  182.2 10.5 %collective-permute-start.73 = (bf16[2,5,48,384]{3,2,1,0:T(8,128)(2,1)S(1)}, bf16[2,5,48,384]{3,2,1,0:T(8,128)(2,1)}, u32[]{:S(2)}, u32[]{:S(2)}) collective-permute-start(bf16[2,5,48,384]{3,2,1,0:T(8,128)(2,1)S(1)} %get-tuple-element.223), channel_id=1, source_target_pairs={{0,8},{1,9},{2,10},{3,11},{4,12},{5,13},{6,14},{7,15},{8,0},{9,1},... | collective-permute-start | bytes 1105928 | tf_op jit(solution)/shard_map/ppermute | solution.py:542
  184.0 11.5 %collective-permute-start.71 = (bf16[2,5,48,384]{3,2,1,0:T(8,128)(2,1)}, bf16[2,5,48,384]{3,2,1,0:T(8,128)(2,1)}, u32[]{:S(2)}, u32[]{:S(2)}) collective-permute-start(bf16[2,5,48,384]{3,2,1,0:T(8,128)(2,1)} %get-tuple-element.203), channel_id=1, source_target_pairs={{0,2},{1,3},{2,0},{3,1},{4,6},{5,7},{6,4},{7,5},{8,10},{9,11},{10,... | collective-permute-start | bytes 1105928 | tf_op jit(solution)/shard_map/ppermute | solution.py:542
  184.0 11.5 %collective-permute-start.72 = (bf16[2,5,48,384]{3,2,1,0:T(8,128)(2,1)}, bf16[2,5,48,384]{3,2,1,0:T(8,128)(2,1)}, u32[]{:S(2)}, u32[]{:S(2)}) collective-permute-start(bf16[2,5,48,384]{3,2,1,0:T(8,128)(2,1)} %get-tuple-element.204), channel_id=1, source_target_pairs={{0,4},{1,5},{2,6},{3,7},{4,0},{5,1},{6,2},{7,3},{8,12},{9,13},{10,... | collective-permute-start | bytes 1105928 | tf_op jit(solution)/shard_map/ppermute | solution.py:542
  187.6 13.0 %collective-permute-start.70 = (bf16[2,176,384]{2,1,0:T(8,128)(2,1)}, bf16[2,176,384]{2,1,0:T(8,128)(2,1)S(1)}, u32[]{:S(2)}, u32[]{:S(2)}) collective-permute-start(bf16[2,176,384]{2,1,0:T(8,128)(2,1)} %get-tuple-element.235), channel_id=1, source_target_pairs={{0,8},{1,9},{2,10},{3,11},{4,12},{5,13},{6,14},{7,15},{8,0},{9,1},... | collective-permute-start | bytes 811016 | tf_op jit(solution)/shard_map/ppermute | solution.py:542
  189.4 11.2 %collective-permute-start.68 = (bf16[2,176,384]{2,1,0:T(8,128)(2,1)}, bf16[2,176,384]{2,1,0:T(8,128)(2,1)S(1)}, u32[]{:S(2)}, u32[]{:S(2)}) collective-permute-start(bf16[2,176,384]{2,1,0:T(8,128)(2,1)} %get-tuple-element.207), channel_id=1, source_target_pairs={{0,2},{1,3},{2,0},{3,1},{4,6},{5,7},{6,4},{7,5},{8,10},{9,11},{10,... | collective-permute-start | bytes 811016 | tf_op jit(solution)/shard_map/ppermute | solution.py:542
  192.7 7.9 %collective-permute-start.69 = (bf16[2,176,384]{2,1,0:T(8,128)(2,1)}, bf16[2,176,384]{2,1,0:T(8,128)(2,1)}, u32[]{:S(2)}, u32[]{:S(2)}) collective-permute-start(bf16[2,176,384]{2,1,0:T(8,128)(2,1)} %get-tuple-element.208), channel_id=1, source_target_pairs={{0,4},{1,5},{2,6},{3,7},{4,0},{5,1},{6,2},{7,3},{8,12},{9,13},{10,... | collective-permute-start | bytes 811016 | tf_op jit(solution)/shard_map/ppermute | solution.py:542
  196.8 13.7 %collective-permute-start.76 = (bf16[5,48,384]{2,1,0:T(8,128)(2,1)S(1)}, bf16[5,48,384]{2,1,0:T(8,128)(2,1)S(1)}, u32[]{:S(2)}, u32[]{:S(2)}) collective-permute-start(bf16[5,48,384]{2,1,0:T(8,128)(2,1)S(1)} %fusion), channel_id=1, source_target_pairs={{0,16},{1,17},{2,18},{3,19},{4,20},{5,21},{6,22},{7,23},{8,24},{9,... | collective-permute-start | bytes 552968 | tf_op jit(solution)/shard_map/ppermute | solution.py:542
  201.8 10.0 %collective-permute-start.74 = (bf16[176,384]{1,0:T(8,128)(2,1)S(1)}, bf16[176,384]{1,0:T(8,128)(2,1)S(1)}, u32[]{:S(2)}, u32[]{:S(2)}) collective-permute-start(bf16[176,384]{1,0:T(8,128)(2,1)S(1)} %fusion.2), channel_id=1, source_target_pairs={{0,16},{1,17},{2,18},{3,19},{4,20},{5,21},{6,22},{7,23},{8,24},{9,... | collective-permute-start | bytes 405512 | tf_op jit(solution)/shard_map/ppermute | solution.py:542
  206.2 7.9 %collective-permute-start.78 = (f32[96,384]{1,0:T(8,128)S(1)}, f32[96,384]{1,0:T(8,128)S(1)}, u32[]{:S(2)}, u32[]{:S(2)}) collective-permute-start(f32[96,384]{1,0:T(8,128)S(1)} %slice_select_fusion.2), channel_id=1, source_target_pairs={{0,1},{1,0},{2,3},{3,2},{4,5},{5,4},{6,7},{7,6},{8,9},{9,8},{10,11... | collective-permute-start | bytes 442376 | tf_op jit(solution)/shard_map/ppermute | solution.py:542
  (85 other events, 1031.6 us)

commit v2 on v1

--- a/solution.py
+++ b/solution.py
@@ -155,7 +155,7 @@
         xhat, _ = norm_parts(x_ref[rows, :].astype(F32))
         n1_ref[rows, :] = (xhat * vec_ref[0:1, :] + vec_ref[1:2, :]).astype(BF16)
 
-    chunks(tokens, 128, norm_one)
+    chunks(tokens, 256, norm_one)
     for t in range(3):
         whole_wait(w_qkv.at[t], sems.at[1 + t])
         y = (nn(n1_ref[...], w_qkv[t]) + vec_ref[2 + t : 3 + t, :]).astype(BF16)
@@ -178,7 +178,7 @@
             mixed_ref[rows, pair_cols(0, i)] = mixed.astype(BF16)
             return carry
 
-        lax.fori_loop(0, PAIRS, pair, 0)
+        lax.fori_loop(0, PAIRS, pair, 0, unroll=PAIRS)
 
 
 GELU_A = 0.7978845608028654
@@ -217,7 +217,7 @@
         xhat, _ = norm_parts(mid_ref[rows, :])
         n2_ref[rows, :] = (xhat * vec_ref[6:7, :] + vec_ref[7:8, :]).astype(BF16)
 
-    chunks(tokens, 128, norm_two)
+    chunks(tokens, 256, norm_two)
     for other, s in QUARTERS:
         if s == 0:
             whole_wait(w_up.at[other], sems.at[other])
@@ -235,7 +235,7 @@
                 half_up + u * (0.5 - 0.5 * t * t) * (GELU_A + 3.0 * GELU_A * GELU_B * sq)
             ).astype(BF16)
 
-        chunks(tokens, 256, part)
+        chunks(tokens, 512, part)
 
 
 def down_grad_kernel(pos_ref, act_ref, gout_ref, mine, theirs, grad, sem):
@@ -304,7 +304,7 @@
         gbr[rows, :] = low
         sums[5:6, :] += jnp.sum(low.astype(F32), axis=0, keepdims=True)
 
-    chunks(tokens, 128, back_two)
+    chunks(tokens, 256, back_two)
     grad[...] = nn(mixt[...], gbr[...]).astype(BF16)
     for chip in range(CHIPS):
         place = scatter_place(pos_ref, chip)
@@ -341,13 +341,18 @@
             gqkv[rows, pair_cols(2, i)] = dv.astype(BF16)
             return carry
 
-        lax.fori_loop(0, PAIRS, pair, 0)
+        lax.fori_loop(0, PAIRS, pair, 0, unroll=PAIRS)
     for t in range(3):
         cols = pl.ds(pl.multiple_of(t * D + (1 - pos_ref[1]) * HALF, 128), HALF)
         give[:, t * HALF : (t + 1) * HALF] = gqkv[:, cols]
     gb_ref[...] = jnp.zeros(gb_ref.shape, F32)
     gb_ref[0:1, :] = jnp.sum(gqkv[:, :D].astype(F32), axis=0, keepdims=True)
     gb_ref[2:3, :] = jnp.sum(gqkv[:, 2 * D :].astype(F32), axis=0, keepdims=True)
+
+
+def up_rows():
+    row = lax.broadcasted_iota(jnp.int32, (16, 1), 0)
+    return (row >= 8) & (row < 12)
 
 
 def qkv_grad_kernel(
@@ -385,11 +390,14 @@
         sums[1:2, :] += jnp.sum(g, axis=0, keepdims=True)
         igrad[rows, :] = (gmid[rows, :] + norm_back(g, xhat, scale, vec_ref[0:1, :])).astype(BF16)
 
-    chunks(tokens, 128, back_one)
-    for p in range(CHIPS):
-        small[p, 0:16] = sums[:, :HALF].astype(BF16)
-        small[p, 16:32] = sums[:, HALF:].astype(BF16)
-        start(small.at[p], mine.at[p, pl.ds(3 * BLK, 32)], sems.at[2])
+    chunks(tokens, 256, back_one)
+    is_up = up_rows()
+    for chip in range(CHIPS):
+        one, up = chip // 8 * HALF, chip % 4 // 2 * HALF
+        block = jnp.where(is_up, sums[:, up : up + HALF], sums[:, one : one + HALF])
+        place = scatter_place(pos_ref, chip)
+        small[place] = block.astype(BF16)
+        start(small.at[place], mine.at[place, pl.ds(3 * BLK, 16)], sems.at[2])
     whole_wait(small, sems.at[2])
     whole_wait(grad, sems.at[1])
 
@@ -486,16 +494,14 @@
         for t in range(3):
             cols = pl.ds(pl.multiple_of(t * D + half * HALF, 128), HALF)
             w_ref[:, cols] = ref[t * PER : (t + 1) * PER, :]
-    for h in range(2):
-        at = 3 * PER + 16 * h
-        rows[:, h * HALF : (h + 1) * HALF] = keep[at : at + 16, :] + got[at : at + 16, :]
-    mine = pltpu.roll(rows[...], lax.rem(D - place * PER, D), 1)
+    rows[...] = keep[3 * PER :, :] + got[3 * PER :, :]
+    mine = pltpu.roll(rows[...], (HALF - place * PER % HALF) % HALF, 1)
     eight_ref[...] = mine[0:8, 0:PER]
     down_ref[...] = mine[12:13, 0:PER]
     at = place * (4 * PER)
     here = lax.broadcasted_iota(jnp.int32, (16, 1), 0) == 8 + at // D
     row = jnp.sum(jnp.where(here, rows[...], 0.0), axis=0, keepdims=True)
-    turned = pltpu.roll(jnp.broadcast_to(row, (8, D)), lax.rem(D - at % D, D), 1)
+    turned = pltpu.roll(jnp.broadcast_to(row, (8, HALF)), (HALF - at % HALF) % HALF, 1)
     up_ref[...] = turned[0:1, 0 : 4 * PER]
 
 
@@ -612,7 +618,8 @@
         return jnp.stack(units, axis=3).transpose(0, 2, 1, 3, 4).reshape(D, -1, 2, HALF)
 
     if group == "attn":
-        sums = jnp.concatenate([both[0][0, 3 * BLK + 16 * h :][:16] for h in range(2)], axis=1)
+        near, far, far_up = (both[0][chip, 3 * BLK :] for chip in (0, 8, 2))
+        sums = jnp.concatenate([near, far.at[8:12].set(far_up[8:12])], axis=1)
         qkv = matrix([b[:, : 3 * BLK].reshape(CHIPS, 3, BLK, HALF) for b in both])
         return scatter(qkv.reshape(D, 3 * D)), lax.psum(sums.astype(F32), AXES)
     if group == "up":
@@ -671,15 +678,15 @@
         )
 
     def finish(self, pos, last, low):
-        sent = shape((3 * PER + 32, HALF), F32)
+        sent = shape((3 * PER + 16, HALF), F32)
         keep, send = call(
             finish_kernel, "finish", (pos, last), low, (sent, sent), (),
-            [vmem(4, 3 * BLK + 32, HALF), dma(4)], 0,
+            [vmem(4, 3 * BLK + 16, HALF), dma(4)], 0,
         )
         return call(
             spread_kernel, "spread", (pos, keep, swap(send, 0)), (),
             (shape((PER, 3 * D), F32), shape((8, PER), F32), shape((1, 4 * PER), F32), shape((1, PER), F32)),
-            (), [vmem(16, D, kind=F32)], 0,
+            (), [vmem(16, HALF, kind=F32)], 0,
         )
 
     def spread_up(self, pos, keep, got):
@@ -745,10 +752,10 @@
     def qkv_grad(self, pos, vec, sums, gbq, gmid, gqkv, n1, w_qkv, n1_got, g_got, inputs):
         return call(
             qkv_grad_kernel, "qkv_grad", (pos, *keep(vec, sums, gbq, gmid, gqkv, n1, w_qkv, n1_got, g_got)),
-            [inputs], (self.out,), (far_shape(CHIPS, 3 * BLK + 32, HALF),),
+            [inputs], (self.out,), (far_shape(CHIPS, 3 * BLK + 16, HALF),),
             [
                 self.one, self.one_f32, vmem(D, 2 * self.tokens), vmem(2 * self.tokens, 3 * HALF),
-                vmem(D, 3 * HALF), vmem(16, D, kind=F32), vmem(CHIPS, 32, HALF), dma(3),
+                vmem(D, 3 * HALF), vmem(16, D, kind=F32), vmem(CHIPS, 16, HALF), dma(3),
             ],
             2 * self.tokens * D * 6 * D,
         )
@@ -926,19 +933,17 @@
             tie(pos, *scatter2.out, *scatter1.out),
             vec, sums, gbq, gmid, gqkv, n1, w_qkv_all, n1_got, g_got, inputs,
         )
+        scatter1.fourth(input_grad)
         scatter2.hi(input_grad)
-        scatter1.fourth(input_grad)
         scatter3 = Scatter(tie(sums_attn, *scatter2.out))
         scatter3.diagonal()
-        layer_out = layer.layer_out(
-            tie(pos, *scatter3.out, *scatter1.out), vec, act, mid, w_down_all
-        )
+        layer_out = layer.layer_out(tie(pos, *scatter3.out, *scatter1.out), vec, act, mid, w_down_all)
         scatter1.in_z = tie(scatter1.in_z, layer_out)
         scatter3.hi(layer_out, scatter1.in_z)
         scatter2.lo(*scatter3.out)
         scatter3.lo(*scatter2.out)
-        scatter2.fourth(*scatter3.out)
-        scatter3.fourth(*scatter2.out)
+        scatter2.fourth(scatter3.in_z)
+        scatter3.fourth()
 
         def exchange(blocks, axis):
             first, second = jnp.split(blocks, 2, axis=axis)
@@ -946,13 +951,13 @@
             got = swap(jnp.where(core == 0, second, first), 0)
             return jnp.where(core == 0, keep, got), jnp.where(core == 0, got, keep)
 
-        grad_w_down = jnp.concatenate(exchange(scatter1.result(*scatter3.out), 0), axis=1)
+        grad_w_down = jnp.concatenate(exchange(scatter1.result(scatter2.in_z), 0), axis=1)
         total = scatter2.result(*scatter3.out)
         upper, lower = total[:, :PER], total[:, PER:]
         got = swap(jnp.where(core == 0, lower, upper), 0)
         grad_w_up, grad_w_out = layer.spread_up(pos, jnp.where(core == 0, upper, lower), got)
         grad_w_qkv, eight, grad_b_up, grad_b_down = layer.finish(
-            pos, scatter3.in_z, [*scatter3.both, *scatter3.near[1:]]
+            tie(pos, total), scatter3.in_z, [*scatter3.both, *scatter3.near[1:]]
         )
         grad_b_up, grad_b_down = grad_b_up[0], grad_b_down[0]
     return (

time: 219 us -> 220 us (level); the launches traced: 218 us -> 217 us
  Pallas kernels: 72.2 us -> 67.7 us
  starting transfers between devices: 71.2 us -> 74.6 us
    pallas_call x13, Pallas kernels: 72.2 us -> 67.7 us  [call(): pl.pallas_call(kernel, out_shape=outs, in_specs=[pl.BlockSpec(memory_spac...]
    ppermute x79, starting transfers between devices: 71.2 us -> 74.6 us  [swap(): return lax.ppermute(value, AXES, [(i, i ^ flip) for i in range(2 * CHIPS)])]
  transfers between devices with their start and end apart: 79 -> 79, of which waited for: 29 -> 32; matrix products, arithmetic and copies ran while one was open for 5% -> 5% of each run, Pallas kernels for 32% -> 29%
where the time goes in v2:
time: 220 us; the launch traced here: 217 us
  starting transfers between devices  74.6 us (34%)
  Pallas kernels  67.7 us (31%)
  waiting for transfers between devices  58 us (26%)
  other arithmetic  9.47 us (4%)
  local copies, waits for them, and re-layouts  5.1 us (2%)
    ppermute x79, starting transfers between devices, swap(): return lax.ppermute(value, AXES, [(i, i ^ flip) for i in range(2 * CHIPS)])  74.6 us
    pallas_call x13, Pallas kernels, call(): pl.pallas_call(kernel, out_shape=outs, in_specs=[pl.BlockSpec(memory_spac...  67.7 us
    ppermute x79, waiting for transfers between devices, swap(): return lax.ppermute(value, AXES, [(i, i ^ flip) for i in range(2 * CHIPS)])  58 us
    convert_element_type x10, other arithmetic, rounded_sum(): return total.astype(BF16)  4.9 us
  transfers between devices with their start and end apart: 79, of which 32 were waited for; matrix products, arithmetic and copies ran while one was open for 5% of the time, Pallas kernels for 29%

profile of v2, /device:TPU:0, one launch (start us, length us, event | category | flops | bytes accessed | tf_op | source)
XLA Modules:
  0.0 216.5 jit_solution(9579160471004939451)
XLA Ops:
  0.7 1.3 pack.1
  4.3 4.0 %collective-permute-start.1 = (bf16[160,384]{1,0:T(8,128)(2,1)S(1)}, bf16[160,384]{1,0:T(8,128)(2,1)S(1)}, u32[]{:S(2)}, u32[]{:S(2)}) collective-permute-start(bf16[160,384]{1,0:T(8,128)(2,1)S(1)} %get-tuple-element.121), channel_id=1, source_target_pairs={{0,16},{1,17},{2,18},{3,19},{4,20},{5,21},{6,22},{7,23},{8,24},{9,... | collective-permute-start | bytes 368648 | tf_op jit(solution)/shard_map/ppermute | solution.py:548
  8.3 6.3 %collective-permute-done.1 = bf16[160,384]{1,0:T(8,128)(2,1)S(1)} collective-permute-done((bf16[160,384]{1,0:T(8,128)(2,1)S(1)}, bf16[160,384]{1,0:T(8,128)(2,1)S(1)}, u32[]{:S(2)}, u32[]{:S(2)}) %collective-permute-start.1) | collective-permute-done | bytes 122912 | tf_op jit(solution)/shard_map/ppermute | solution.py:548
  14.7 1.6 collective-permute-start.8
  16.3 4.0 %collective-permute-start.3 = (bf16[2,160,384]{2,1,0:T(8,128)(2,1)S(1)}, bf16[2,160,384]{2,1,0:T(8,128)(2,1)S(1)}, u32[]{:S(2)}, u32[]{:S(2)}) collective-permute-start(bf16[2,160,384]{2,1,0:T(8,128)(2,1)S(1)} %pad_maximum_fusion.3.refs_0_), channel_id=1, source_target_pairs={{0,8},{1,9},{2,10},{3,11},{4,12},{5,13},{6,14},{7,15},{8,0},{9,1},... | collective-permute-start | bytes 737288 | tf_op jit(solution)/shard_map/ppermute | solution.py:548
  20.3 1.6 collective-permute-start.18
  23.4 3.6 %collective-permute-done.3.refs_1_ = bf16[2,160,384]{2,1,0:T(8,128)(2,1)S(1)} collective-permute-done((bf16[2,160,384]{2,1,0:T(8,128)(2,1)S(1)}, bf16[2,160,384]{2,1,0:T(8,128)(2,1)S(1)}, u32[]{:S(2)}, u32[]{:S(2)}) %collective-permute-start.3) | collective-permute-done | bytes 245792 | tf_op jit(solution)/shard_map/ppermute | solution.py:548
  27.0 1.3 collective-permute-start.11
  28.2 3.6 %collective-permute-done.2 = bf16[9,48,384]{2,1,0:T(8,128)(2,1)S(1)} collective-permute-done((bf16[9,48,384]{2,1,0:T(8,128)(2,1)S(1)}, bf16[9,48,384]{2,1,0:T(8,128)(2,1)S(1)}, u32[]{:S(2)}, u32[]{:S(2)}) %collective-permute-start.2) | collective-permute-done | bytes 331808 | tf_op jit(solution)/shard_map/ppermute | solution.py:548
  32.1 1.3 collective-permute-start.10
  34.0 4.8 %collective-permute-done.10.refs_5_ = bf16[2,160,384]{2,1,0:T(8,128)(2,1)S(1)} collective-permute-done((bf16[2,160,384]{2,1,0:T(8,128)(2,1)S(1)}, bf16[2,160,384]{2,1,0:T(8,128)(2,1)S(1)}, u32[]{:S(2)}, u32[]{:S(2)}) %collective-permute-start.10) | collective-permute-done | bytes 245792 | tf_op jit(solution)/shard_map/ppermute | solution.py:548
  39.7 1.6 collective-permute-start.13
  44.2 5.8 %collective-permute-done.12.refs_2_ = bf16[2,5,48,384]{3,2,1,0:T(8,128)(2,1)S(1)} collective-permute-done((bf16[2,5,48,384]{3,2,1,0:T(8,128)(2,1)S(1)}, bf16[2,5,48,384]{3,2,1,0:T(8,128)(2,1)S(1)}, u32[]{:S(2)}, u32[]{:S(2)}) %collective-permute-start.12) | collective-permute-done | bytes 368672 | tf_op jit(solution)/shard_map/ppermute | solution.py:548
  50.6 9.7 %collective-permute-done.19.refs_7_ = bf16[2,160,384]{2,1,0:T(8,128)(2,1)} collective-permute-done((bf16[2,160,384]{2,1,0:T(8,128)(2,1)S(1)}, bf16[2,160,384]{2,1,0:T(8,128)(2,1)}, u32[]{:S(2)}, u32[]{:S(2)}) %collective-permute-start.19) | collective-permute-done | bytes 245792 | tf_op jit(solution)/shard_map/ppermute | solution.py:548
  61.8 1.4 collective-permute-start.16
  64.1 1.5 collective-permute-start.14
  65.6 1.4 collective-permute-done.17.refs_6_
  68.3 10.7 %attn_forward.1 = (f32[16,768]{1,0:T(8,128)S(1)}, bf16[512,768]{1,0:T(8,128)(2,1)S(1)}, bf16[512,2304]{1,0:T(8,128)(2,1)S(1)}, bf16[24,256,256]{2,1,0:T(8,128)(2...) custom-call(s32[2]{0:T(128)S(1)} %pad_add_fusion.pos_ref, s32[2,1,256]{2,1,0:T(1,128)S(1)} %reshape.123.segr_ref, ...), custom_call_target="tpu_custom_call" | custom-call | flops 2617245696 | bytes 15388680 | tf_op jit(solution)/shard_map/attn_forward/pallas_call | solution.py:523
  79.1 1.5 collective-permute-done.7.refs_7_
  85.9 1.5 collective-permute-start.28
  88.2 9.4 %mlp_up.1 = (f32[8,768]{1,0:T(8,128)S(1)}, bf16[512,768]{1,0:T(8,128)(2,1)S(1)}, f32[512,768]{1,0:T(8,128)S(1)}, bf16[512,3072]{1,0:T(8,128)(2,1)S(1)}, bf16[512...) custom-call(s32[2]{0:T(128)S(1)} %pad_add_fusion.pos_ref, ...), custom_call_target="tpu_custom_call" | custom-call | flops 3019898880 | bytes 23668744 | tf_op jit(solution)/shard_map/mlp_up/pallas_call | solution.py:523
  97.7 1.7 collective-permute-done.30.refs_6_
  99.4 1.6 collective-permute-start.39
  102.0 4.3 %down_grad.1 = (bf16[16,192,384]{2,1,0:T(8,128)(2,1)}, bf16[16,192,384]{2,1,0:T(8,128)(2,1)}) custom-call(s32[2]{0:T(128)S(1)} %pad_add_fusion.pos_ref, bf16[512,3072]{1,0:T(8,128)(2,1)S(1)} %get-tuple-element.149.act_ref, bf16[512,768]{1,0:T(8,128)(2,1)S(1)} %get-tuple-element.150.gout_ref), custom_call_target="tpu_custom_call" | custom-call | flops 2415919104 | bytes 8650760 | tf_op jit(solution)/shard_map/down_grad/pallas_call | solution.py:523
  106.4 1.4 collective-permute-done.39.refs_7_
  111.3 9.9 %mlp_down.1 = (f32[8,768]{1,0:T(8,128)S(1)}, bf16[512,3072]{1,0:T(8,128)(2,1)S(1)}, bf16[3072,768]{1,0:T(8,128)(2,1)S(1)}, bf16[16,5,48,384]{3,2,1,0:T(8,128)(2,1)}, bf16[16,5,48,384]{3,2,1,0:T(8,128)(2,1)}) custom-call(s32[2]{0:T(128)S(1)} %pad_add_fusion.pos_ref, bf16[512,768]{1,0:T(8,128)(2,1)S(1)} %get-tuple-element.150.gout_ref, ...), custom_call_target="tpu_custom_call" | custom-call | flops 4831838208 | bytes 23224328 | tf_op jit(solution)/shard_map/mlp_down/pallas_call | solution.py:523
  121.4 1.3 collective-permute-start.50
  123.5 8.4 %mid_backward.1 = (f32[16,768]{1,0:T(8,128)S(1)}, f32[512,768]{1,0:T(8,128)S(1)}, bf16[512,768]{1,0:T(8,128)(2,1)S(1)}, bf16[16,5,48,384]{3,2,1,0:T(8,128)(2,1)}, bf16[16,5,48,384]{3,2,1,0:T(8,128)(2,1)}) custom-call(s32[2]{0:T(128)S(1)} %pad_add_fusion.pos_ref, ...), custom_call_target="tpu_custom_call", output_to_operand_aliasing={{3}: (10, {}), {4}: (11, {})} | custom-call | flops 3623878656 | bytes 26492936 | tf_op jit(solution)/shard_map/mid_backward/pallas_call | solution.py:523
  132.5 1.6 collective-permute-start.53
  134.8 7.0 %attn_backward.1 = (f32[8,768]{1,0:T(8,128)S(1)}, bf16[512,2304]{1,0:T(8,128)(2,1)S(1)}, bf16[512,1152]{1,0:T(8,128)(2,1)S(1)}) custom-call(s32[2]{0:T(128)S(1)} %pad_add_fusion.pos_ref, bf16[512,768]{1,0:T(8,128)(2,1)S(1)} %get-tuple-element.173.gmixed, bf16[512,2304]{1,0:T(8,128)(2,1)S(1)} %get-tuple-element.174.qkv_ref, ...), custom_call_target="tpu_custom_call" | custom-call | flops 2013265920 | bytes 9854984 | tf_op jit(solution)/shard_map/attn_backward/pallas_call | solution.py:523
  149.2 7.8 %qkv_grad.1 = (bf16[512,768]{1,0:T(8,128)(2,1)}, bf16[16,160,384]{2,1,0:T(8,128)(2,1)}) custom-call(s32[2]{0:T(128)S(1)} %pad_add_fusion.pos_ref, f32[16,768]{1,0:T(8,128)S(1)} %get-tuple-element.135.vec_ref, f32[16,768]{1,0:T(8,128)S(1)} %get-tuple-element.168.sums_ref, f32[8,768]{1,0:T(8,128)S(1)} %get-tuple-element.176.gbq_ref, ...), custom_call_target="tpu_custom_call" | custom-call | flops 3623878656 | bytes 13885448 | tf_op jit(solution)/shard_map/qkv_grad/pallas_call | solution.py:523
  157.3 1.3 copy-done.1
  161.8 5.4 %collective-permute-start.65 = (bf16[192,384]{1,0:T(8,128)(2,1)S(1)}, bf16[192,384]{1,0:T(8,128)(2,1)S(1)}, u32[]{:S(2)}, u32[]{:S(2)}) collective-permute-start(bf16[192,384]{1,0:T(8,128)(2,1)S(1)} %fusion.1), channel_id=1, source_target_pairs={{0,16},{1,17},{2,18},{3,19},{4,20},{5,21},{6,22},{7,23},{8,24},{9,... | collective-permute-start | bytes 442376 | tf_op jit(solution)/shard_map/ppermute | solution.py:548
  169.2 4.0 %layer_out.1 = bf16[512,768]{1,0:T(8,128)(2,1)} custom-call(s32[2]{0:T(128)S(1)} %pad_add_fusion.pos_ref, f32[16,768]{1,0:T(8,128)S(1)} %get-tuple-element.135.vec_ref, bf16[512,3072]{1,0:T(8,128)(2,1)S(1)} %get-tuple-element.149.act_ref, f32[512,768]{1,0:T(8,128)S(1)} %get-tuple-element.161.mid_ref, bf16[3072,768]{1,0:T(8,128)(2,1)S(1)} %get-tuple-element.196.w_down), custom_call_target="tpu_custom_call" | custom-call | flops 2415919104 | bytes 10272776 | tf_op jit(solution)/shard_map/layer_out/pallas_call | solution.py:523
  174.8 1.3 collective-permute-start.70
  177.2 1.3 add_convert_fusion
  178.5 1.6 collective-permute-start.68
  180.1 2.5 %collective-permute-start.66 = (bf16[2,5,48,384]{3,2,1,0:T(8,128)(2,1)}, bf16[2,5,48,384]{3,2,1,0:T(8,128)(2,1)}, u32[]{:S(2)}, u32[]{:S(2)}) collective-permute-start(bf16[2,5,48,384]{3,2,1,0:T(8,128)(2,1)} %get-tuple-element.202), channel_id=1, source_target_pairs={{0,2},{1,3},{2,0},{3,1},{4,6},{5,7},{6,4},{7,5},{8,10},{9,11},{10,... | collective-permute-start | bytes 1105928 | tf_op jit(solution)/shard_map/ppermute | solution.py:548
  185.0 2.5 %collective-permute-start.73 = (bf16[2,160,384]{2,1,0:T(8,128)(2,1)}, bf16[2,160,384]{2,1,0:T(8,128)(2,1)S(1)}, u32[]{:S(2)}, u32[]{:S(2)}) collective-permute-start(bf16[2,160,384]{2,1,0:T(8,128)(2,1)} %get-tuple-element.208), channel_id=1, source_target_pairs={{0,2},{1,3},{2,0},{3,1},{4,6},{5,7},{6,4},{7,5},{8,10},{9,11},{10,... | collective-permute-start | bytes 737288 | tf_op jit(solution)/shard_map/ppermute | solution.py:548
  187.4 1.9 collective-permute-done.68
  189.3 1.8 collective-permute-start.74
  193.0 1.3 fusion
  194.4 3.6 %collective-permute-start.72 = (bf16[5,48,384]{2,1,0:T(8,128)(2,1)S(1)}, bf16[5,48,384]{2,1,0:T(8,128)(2,1)S(1)}, u32[]{:S(2)}, u32[]{:S(2)}) collective-permute-start(bf16[5,48,384]{2,1,0:T(8,128)(2,1)S(1)} %fusion), channel_id=1, source_target_pairs={{0,16},{1,17},{2,18},{3,19},{4,20},{5,21},{6,22},{7,23},{8,24},{9,... | collective-permute-start | bytes 552968 | tf_op jit(solution)/shard_map/ppermute | solution.py:548
  199.1 2.3 %collective-permute-start.75 = (bf16[160,384]{1,0:T(8,128)(2,1)S(1)}, bf16[160,384]{1,0:T(8,128)(2,1)S(1)}, u32[]{:S(2)}, u32[]{:S(2)}) collective-permute-start(bf16[160,384]{1,0:T(8,128)(2,1)S(1)} %fusion.2), channel_id=1, source_target_pairs={{0,16},{1,17},{2,18},{3,19},{4,20},{5,21},{6,22},{7,23},{8,24},{9,... | collective-permute-start | bytes 368648 | tf_op jit(solution)/shard_map/ppermute | solution.py:548
  201.5 6.0 %collective-permute-done.72 = bf16[5,48,384]{2,1,0:T(8,128)(2,1)S(1)} collective-permute-done((bf16[5,48,384]{2,1,0:T(8,128)(2,1)S(1)}, bf16[5,48,384]{2,1,0:T(8,128)(2,1)S(1)}, u32[]{:S(2)}, u32[]{:S(2)}) %collective-permute-start.72) | collective-permute-done | bytes 184352 | tf_op jit(solution)/shard_map/ppermute | solution.py:548
  207.5 1.3 convert_add_fusion
  208.8 1.7 finish.1
  215.0 1.3 spread_up.1
  (270 shorter events, 51.1 us)
Async XLA Ops:
  4.3 10.3 %collective-permute-start.1 = (bf16[160,384]{1,0:T(8,128)(2,1)S(1)}, bf16[160,384]{1,0:T(8,128)(2,1)S(1)}, u32[]{:S(2)}, u32[]{:S(2)}) collective-permute-start(bf16[160,384]{1,0:T(8,128)(2,1)S(1)} %get-tuple-element.121), channel_id=1, source_target_pairs={{0,16},{1,17},{2,18},{3,19},{4,20},{5,21},{6,22},{7,23},{8,24},{9,... | collective-permute-start | bytes 368648 | tf_op jit(solution)/shard_map/ppermute | solution.py:548
  14.6 17.3 %collective-permute-start.2 = (bf16[9,48,384]{2,1,0:T(8,128)(2,1)S(1)}, bf16[9,48,384]{2,1,0:T(8,128)(2,1)S(1)}, u32[]{:S(2)}, u32[]{:S(2)}) collective-permute-start(bf16[9,48,384]{2,1,0:T(8,128)(2,1)S(1)} %get-tuple-element.122), channel_id=1, source_target_pairs={{0,16},{1,17},{2,18},{3,19},{4,20},{5,21},{6,22},{7,23},{8,24},{9,... | collective-permute-start | bytes 995336 | tf_op jit(solution)/shard_map/ppermute | solution.py:548
  14.7 7.5 %collective-permute-start.8 = (bf16[2,160,384]{2,1,0:T(8,128)(2,1)S(1)}, bf16[2,160,384]{2,1,0:T(8,128)(2,1)S(1)}, u32[]{:S(2)}, u32[]{:S(2)}) collective-permute-start(bf16[2,160,384]{2,1,0:T(8,128)(2,1)S(1)} %pad_maximum_fusion.3.refs_0_), channel_id=1, source_target_pairs={{0,2},{1,3},{2,0},{3,1},{4,6},{5,7},{6,4},{7,5},{8,10},{9,11},{10,... | collective-permute-start | bytes 737288 | tf_op jit(solution)/shard_map/ppermute | solution.py:548
  16.3 10.7 %collective-permute-start.3 = (bf16[2,160,384]{2,1,0:T(8,128)(2,1)S(1)}, bf16[2,160,384]{2,1,0:T(8,128)(2,1)S(1)}, u32[]{:S(2)}, u32[]{:S(2)}) collective-permute-start(bf16[2,160,384]{2,1,0:T(8,128)(2,1)S(1)} %pad_maximum_fusion.3.refs_0_), channel_id=1, source_target_pairs={{0,8},{1,9},{2,10},{3,11},{4,12},{5,13},{6,14},{7,15},{8,0},{9,1},... | collective-permute-start | bytes 737288 | tf_op jit(solution)/shard_map/ppermute | solution.py:548
  20.3 13.0 %collective-permute-start.18 = (bf16[2,160,384]{2,1,0:T(8,128)(2,1)S(1)}, bf16[2,160,384]{2,1,0:T(8,128)(2,1)S(1)}, u32[]{:S(2)}, u32[]{:S(2)}) collective-permute-start(bf16[2,160,384]{2,1,0:T(8,128)(2,1)S(1)} %pad_maximum_fusion.3.refs_0_), channel_id=1, source_target_pairs={{0,4},{1,5},{2,6},{3,7},{4,0},{5,1},{6,2},{7,3},{8,12},{9,13},{10,... | collective-permute-start | bytes 737288 | tf_op jit(solution)/shard_map/ppermute | solution.py:548
  22.2 11.2 %collective-permute-start.9 = (bf16[2,160,384]{2,1,0:T(8,128)(2,1)S(1)}, bf16[2,160,384]{2,1,0:T(8,128)(2,1)S(1)}, u32[]{:S(2)}, u32[]{:S(2)}) collective-permute-start(bf16[2,160,384]{2,1,0:T(8,128)(2,1)S(1)} %collective-permute-done.8.refs_2_), channel_id=1, source_target_pairs={{0,4},{1,5},{2,6},{3,7},{4,0},{5,1},{6,2},{7,3},{8,12},{9,13},{10,... | collective-permute-start | bytes 737288 | tf_op jit(solution)/shard_map/ppermute | solution.py:548
  32.0 9.3 %collective-permute-start.4 = (bf16[2,5,48,384]{3,2,1,0:T(8,128)(2,1)S(1)}, bf16[2,5,48,384]{3,2,1,0:T(8,128)(2,1)S(1)}, u32[]{:S(2)}, u32[]{:S(2)}) collective-permute-start(bf16[2,5,48,384]{3,2,1,0:T(8,128)(2,1)S(1)} %pad_maximum_fusion.refs_0_), channel_id=1, source_target_pairs={{0,8},{1,9},{2,10},{3,11},{4,12},{5,13},{6,14},{7,15},{8,0},{9,1},... | collective-permute-start | bytes 1105928 | tf_op jit(solution)/shard_map/ppermute | solution.py:548
  33.9 8.3 %collective-permute-start.22 = (bf16[2,160,384]{2,1,0:T(8,128)(2,1)S(1)}, bf16[2,160,384]{2,1,0:T(8,128)(2,1)S(1)}, u32[]{:S(2)}, u32[]{:S(2)}) collective-permute-start(bf16[2,160,384]{2,1,0:T(8,128)(2,1)S(1)} %collective-permute-done.8.refs_2_), channel_id=1, source_target_pairs={{0,1},{1,0},{2,3},{3,2},{4,5},{5,4},{6,7},{7,6},{8,9},{9,8},{10,11... | collective-permute-start | bytes 737288 | tf_op jit(solution)/shard_map/ppermute | solution.py:548
  38.7 11.3 %collective-permute-start.12 = (bf16[2,5,48,384]{3,2,1,0:T(8,128)(2,1)S(1)}, bf16[2,5,48,384]{3,2,1,0:T(8,128)(2,1)S(1)}, u32[]{:S(2)}, u32[]{:S(2)}) collective-permute-start(bf16[2,5,48,384]{3,2,1,0:T(8,128)(2,1)S(1)} %pad_maximum_fusion.refs_0_), channel_id=1, source_target_pairs={{0,2},{1,3},{2,0},{3,1},{4,6},{5,7},{6,4},{7,5},{8,10},{9,11},{10,... | collective-permute-start | bytes 1105928 | tf_op jit(solution)/shard_map/ppermute | solution.py:548
  39.7 20.6 %collective-permute-start.13 = (bf16[2,5,48,384]{3,2,1,0:T(8,128)(2,1)S(1)}, bf16[2,5,48,384]{3,2,1,0:T(8,128)(2,1)S(1)}, u32[]{:S(2)}, u32[]{:S(2)}) collective-permute-start(bf16[2,5,48,384]{3,2,1,0:T(8,128)(2,1)S(1)} %pad_maximum_fusion.refs_0_), channel_id=1, source_target_pairs={{0,4},{1,5},{2,6},{3,7},{4,0},{5,1},{6,2},{7,3},{8,12},{9,13},{10,... | collective-permute-start | bytes 1105928 | tf_op jit(solution)/shard_map/ppermute | solution.py:548
  41.3 19.5 %collective-permute-start.6 = (bf16[2,5,48,384]{3,2,1,0:T(8,128)(2,1)S(1)}, bf16[2,5,48,384]{3,2,1,0:T(8,128)(2,1)S(1)}, u32[]{:S(2)}, u32[]{:S(2)}) collective-permute-start(bf16[2,5,48,384]{3,2,1,0:T(8,128)(2,1)S(1)} %collective-permute-done.4.refs_1_), channel_id=1, source_target_pairs={{0,2},{1,3},{2,0},{3,1},{4,6},{5,7},{6,4},{7,5},{8,10},{9,11},{10,... | collective-permute-start | bytes 1105928 | tf_op jit(solution)/shard_map/ppermute | solution.py:548
  42.2 18.1 %collective-permute-start.19 = (bf16[2,160,384]{2,1,0:T(8,128)(2,1)S(1)}, bf16[2,160,384]{2,1,0:T(8,128)(2,1)}, u32[]{:S(2)}, u32[]{:S(2)}) collective-permute-start(bf16[2,160,384]{2,1,0:T(8,128)(2,1)S(1)} %collective-permute-done.10.refs_5_), channel_id=1, source_target_pairs={{0,2},{1,3},{2,0},{3,1},{4,6},{5,7},{6,4},{7,5},{8,10},{9,11},{10,... | collective-permute-start | bytes 737288 | tf_op jit(solution)/shard_map/ppermute | solution.py:548
  43.3 17.7 %collective-permute-start.5 = (bf16[2,5,48,384]{3,2,1,0:T(8,128)(2,1)S(1)}, bf16[2,5,48,384]{3,2,1,0:T(8,128)(2,1)S(1)}, u32[]{:S(2)}, u32[]{:S(2)}) collective-permute-start(bf16[2,5,48,384]{3,2,1,0:T(8,128)(2,1)S(1)} %collective-permute-done.4.refs_1_), channel_id=1, source_target_pairs={{0,4},{1,5},{2,6},{3,7},{4,0},{5,1},{6,2},{7,3},{8,12},{9,13},{10,... | collective-permute-start | bytes 1105928 | tf_op jit(solution)/shard_map/ppermute | solution.py:548
  50.0 16.9 %collective-permute-start.17 = (bf16[2,5,48,384]{3,2,1,0:T(8,128)(2,1)S(1)}, bf16[2,5,48,384]{3,2,1,0:T(8,128)(2,1)S(1)}, u32[]{:S(2)}, u32[]{:S(2)}) collective-permute-start(bf16[2,5,48,384]{3,2,1,0:T(8,128)(2,1)S(1)} %collective-permute-done.12.refs_2_), channel_id=1, source_target_pairs={{0,4},{1,5},{2,6},{3,7},{4,0},{5,1},{6,2},{7,3},{8,12},{9,13},{10,... | collective-permute-start | bytes 1105928 | tf_op jit(solution)/shard_map/ppermute | solution.py:548
  61.8 17.2 %collective-permute-start.16 = (bf16[2,192,384]{2,1,0:T(8,128)(2,1)S(1)}, bf16[2,192,384]{2,1,0:T(8,128)(2,1)}, u32[]{:S(2)}, u32[]{:S(2)}) collective-permute-start(bf16[2,192,384]{2,1,0:T(8,128)(2,1)S(1)} %pad_maximum_fusion.1.refs_0_), channel_id=1, source_target_pairs={{0,8},{1,9},{2,10},{3,11},{4,12},{5,13},{6,14},{7,15},{8,0},{9,1},... | collective-permute-start | bytes 884744 | tf_op jit(solution)/shard_map/ppermute | solution.py:548
  63.2 15.9 %collective-permute-start.15 = (bf16[2,192,384]{2,1,0:T(8,128)(2,1)S(1)}, bf16[2,192,384]{2,1,0:T(8,128)(2,1)}, u32[]{:S(2)}, u32[]{:S(2)}) collective-permute-start(bf16[2,192,384]{2,1,0:T(8,128)(2,1)S(1)} %pad_maximum_fusion.1.refs_0_), channel_id=1, source_target_pairs={{0,4},{1,5},{2,6},{3,7},{4,0},{5,1},{6,2},{7,3},{8,12},{9,13},{10,... | collective-permute-start | bytes 884744 | tf_op jit(solution)/shard_map/ppermute | solution.py:548
  64.1 15.0 %collective-permute-start.14 = (bf16[2,192,384]{2,1,0:T(8,128)(2,1)S(1)}, bf16[2,192,384]{2,1,0:T(8,128)(2,1)}, u32[]{:S(2)}, u32[]{:S(2)}) collective-permute-start(bf16[2,192,384]{2,1,0:T(8,128)(2,1)S(1)} %pad_maximum_fusion.1.refs_0_), channel_id=1, source_target_pairs={{0,2},{1,3},{2,0},{3,1},{4,6},{5,7},{6,4},{7,5},{8,10},{9,11},{10,... | collective-permute-start | bytes 884744 | tf_op jit(solution)/shard_map/ppermute | solution.py:548
  66.9 13.6 %collective-permute-start.7 = (bf16[2,5,48,384]{3,2,1,0:T(8,128)(2,1)S(1)}, bf16[2,5,48,384]{3,2,1,0:T(8,128)(2,1)}, u32[]{:S(2)}, u32[]{:S(2)}) collective-permute-start(bf16[2,5,48,384]{3,2,1,0:T(8,128)(2,1)S(1)} %collective-permute-done.5.refs_5_), channel_id=1, source_target_pairs={{0,2},{1,3},{2,0},{3,1},{4,6},{5,7},{6,4},{7,5},{8,10},{9,11},{10,... | collective-permute-start | bytes 1105928 | tf_op jit(solution)/shard_map/ppermute | solution.py:548
  83.8 15.6 %collective-permute-start.29 = (bf16[2,192,384]{2,1,0:T(8,128)(2,1)}, bf16[2,192,384]{2,1,0:T(8,128)(2,1)S(1)}, u32[]{:S(2)}, u32[]{:S(2)}) collective-permute-start(bf16[2,192,384]{2,1,0:T(8,128)(2,1)} %collective-permute-done.16.refs_1_), channel_id=1, source_target_pairs={{0,4},{1,5},{2,6},{3,7},{4,0},{5,1},{6,2},{7,3},{8,12},{9,13},{10,... | collective-permute-start | bytes 884744 | tf_op jit(solution)/shard_map/ppermute | solution.py:548
  85.0 14.4 %collective-permute-start.30 = (bf16[2,192,384]{2,1,0:T(8,128)(2,1)}, bf16[2,192,384]{2,1,0:T(8,128)(2,1)S(1)}, u32[]{:S(2)}, u32[]{:S(2)}) collective-permute-start(bf16[2,192,384]{2,1,0:T(8,128)(2,1)} %collective-permute-done.14.refs_2_), channel_id=1, source_target_pairs={{0,4},{1,5},{2,6},{3,7},{4,0},{5,1},{6,2},{7,3},{8,12},{9,13},{10,... | collective-permute-start | bytes 884744 | tf_op jit(solution)/shard_map/ppermute | solution.py:548
  85.9 13.6 %collective-permute-start.28 = (bf16[2,192,384]{2,1,0:T(8,128)(2,1)}, bf16[2,192,384]{2,1,0:T(8,128)(2,1)S(1)}, u32[]{:S(2)}, u32[]{:S(2)}) collective-permute-start(bf16[2,192,384]{2,1,0:T(8,128)(2,1)} %collective-permute-done.16.refs_1_), channel_id=1, source_target_pairs={{0,2},{1,3},{2,0},{3,1},{4,6},{5,7},{6,4},{7,5},{8,10},{9,11},{10,... | collective-permute-start | bytes 884744 | tf_op jit(solution)/shard_map/ppermute | solution.py:548
  99.4 8.3 %collective-permute-start.39 = (bf16[2,192,384]{2,1,0:T(8,128)(2,1)S(1)}, bf16[2,192,384]{2,1,0:T(8,128)(2,1)S(1)}, u32[]{:S(2)}, u32[]{:S(2)}) collective-permute-start(bf16[2,192,384]{2,1,0:T(8,128)(2,1)S(1)} %collective-permute-done.29.refs_5_), channel_id=1, source_target_pairs={{0,2},{1,3},{2,0},{3,1},{4,6},{5,7},{6,4},{7,5},{8,10},{9,11},{10,... | collective-permute-start | bytes 884744 | tf_op jit(solution)/shard_map/ppermute | solution.py:548
  110.6 10.6 %collective-permute-start.48 = (bf16[16,192,384]{2,1,0:T(8,128)(2,1)}, bf16[16,192,384]{2,1,0:T(8,128)(2,1)S(1)}, u32[]{:S(2)}, u32[]{:S(2)}) collective-permute-start(bf16[16,192,384]{2,1,0:T(8,128)(2,1)} %get-tuple-element.154), channel_id=1, source_target_pairs={{0,1},{1,0},{2,3},{3,2},{4,5},{5,4},{6,7},{7,6},{8,9},{9,8},{10,11... | collective-permute-start | bytes 7077896 | tf_op jit(solution)/shard_map/ppermute | solution.py:548
  121.4 10.5 %collective-permute-start.50 = (bf16[2,192,384]{2,1,0:T(8,128)(2,1)S(1)}, bf16[2,192,384]{2,1,0:T(8,128)(2,1)S(1)}, u32[]{:S(2)}, u32[]{:S(2)}) collective-permute-start(bf16[2,192,384]{2,1,0:T(8,128)(2,1)S(1)} %get-tuple-element.233), channel_id=1, source_target_pairs={{0,4},{1,5},{2,6},{3,7},{4,0},{5,1},{6,2},{7,3},{8,12},{9,13},{10,... | collective-permute-start | bytes 884744 | tf_op jit(solution)/shard_map/ppermute | solution.py:548
  122.6 9.5 %collective-permute-start.49 = (bf16[2,192,384]{2,1,0:T(8,128)(2,1)S(1)}, bf16[2,192,384]{2,1,0:T(8,128)(2,1)S(1)}, u32[]{:S(2)}, u32[]{:S(2)}) collective-permute-start(bf16[2,192,384]{2,1,0:T(8,128)(2,1)S(1)} %get-tuple-element.234), channel_id=1, source_target_pairs={{0,2},{1,3},{2,0},{3,1},{4,6},{5,7},{6,4},{7,5},{8,10},{9,11},{10,... | collective-permute-start | bytes 884744 | tf_op jit(solution)/shard_map/ppermute | solution.py:548
  132.1 11.7 %collective-permute-start.51 = (bf16[16,5,48,384]{3,2,1,0:T(8,128)(2,1)}, bf16[16,5,48,384]{3,2,1,0:T(8,128)(2,1)S(1)}, u32[]{:S(2)}, u32[]{:S(2)}) collective-permute-start(bf16[16,5,48,384]{3,2,1,0:T(8,128)(2,1)} %get-tuple-element.170), channel_id=1, source_target_pairs={{0,1},{1,0},{2,3},{3,2},{4,5},{5,4},{6,7},{7,6},{8,9},{9,8},{10,11... | collective-permute-start | bytes 8847368 | tf_op jit(solution)/shard_map/ppermute | solution.py:548
  132.5 9.4 %collective-permute-start.53 = (bf16[2,192,384]{2,1,0:T(8,128)(2,1)S(1)}, bf16[2,192,384]{2,1,0:T(8,128)(2,1)S(1)}, u32[]{:S(2)}, u32[]{:S(2)}) collective-permute-start(bf16[2,192,384]{2,1,0:T(8,128)(2,1)S(1)} %get-tuple-element.231), channel_id=1, source_target_pairs={{0,4},{1,5},{2,6},{3,7},{4,0},{5,1},{6,2},{7,3},{8,12},{9,13},{10,... | collective-permute-start | bytes 884744 | tf_op jit(solution)/shard_map/ppermute | solution.py:548
  134.0 8.8 %collective-permute-start.52 = (bf16[2,192,384]{2,1,0:T(8,128)(2,1)S(1)}, bf16[2,192,384]{2,1,0:T(8,128)(2,1)S(1)}, u32[]{:S(2)}, u32[]{:S(2)}) collective-permute-start(bf16[2,192,384]{2,1,0:T(8,128)(2,1)S(1)} %get-tuple-element.232), channel_id=1, source_target_pairs={{0,2},{1,3},{2,0},{3,1},{4,6},{5,7},{6,4},{7,5},{8,10},{9,11},{10,... | collective-permute-start | bytes 884744 | tf_op jit(solution)/shard_map/ppermute | solution.py:548
  144.0 13.0 %collective-permute-start.57 = (bf16[2,5,48,384]{3,2,1,0:T(8,128)(2,1)S(1)}, bf16[2,5,48,384]{3,2,1,0:T(8,128)(2,1)S(1)}, u32[]{:S(2)}, u32[]{:S(2)}) collective-permute-start(bf16[2,5,48,384]{3,2,1,0:T(8,128)(2,1)S(1)} %get-tuple-element.226), channel_id=1, source_target_pairs={{0,4},{1,5},{2,6},{3,7},{4,0},{5,1},{6,2},{7,3},{8,12},{9,13},{10,... | collective-permute-start | bytes 1105928 | tf_op jit(solution)/shard_map/ppermute | solution.py:548
  144.8 12.2 %collective-permute-start.56 = (bf16[2,5,48,384]{3,2,1,0:T(8,128)(2,1)S(1)}, bf16[2,5,48,384]{3,2,1,0:T(8,128)(2,1)S(1)}, u32[]{:S(2)}, u32[]{:S(2)}) collective-permute-start(bf16[2,5,48,384]{3,2,1,0:T(8,128)(2,1)S(1)} %get-tuple-element.227), channel_id=1, source_target_pairs={{0,2},{1,3},{2,0},{3,1},{4,6},{5,7},{6,4},{7,5},{8,10},{9,11},{10,... | collective-permute-start | bytes 1105928 | tf_op jit(solution)/shard_map/ppermute | solution.py:548
  145.8 15.9 %collective-permute-start.58 = (bf16[2,192,384]{2,1,0:T(8,128)(2,1)S(1)}, bf16[2,192,384]{2,1,0:T(8,128)(2,1)S(1)}, u32[]{:S(2)}, u32[]{:S(2)}) collective-permute-start(bf16[2,192,384]{2,1,0:T(8,128)(2,1)S(1)} %get-tuple-element.180), channel_id=1, source_target_pairs={{0,2},{1,3},{2,0},{3,1},{4,6},{5,7},{6,4},{7,5},{8,10},{9,11},{10,... | collective-permute-start | bytes 884744 | tf_op jit(solution)/shard_map/ppermute | solution.py:548
  147.3 14.4 %collective-permute-start.59 = (bf16[2,192,384]{2,1,0:T(8,128)(2,1)S(1)}, bf16[2,192,384]{2,1,0:T(8,128)(2,1)S(1)}, u32[]{:S(2)}, u32[]{:S(2)}) collective-permute-start(bf16[2,192,384]{2,1,0:T(8,128)(2,1)S(1)} %get-tuple-element.181), channel_id=1, source_target_pairs={{0,4},{1,5},{2,6},{3,7},{4,0},{5,1},{6,2},{7,3},{8,12},{9,13},{10,... | collective-permute-start | bytes 884744 | tf_op jit(solution)/shard_map/ppermute | solution.py:548
  148.1 8.9 %collective-permute-start.60 = (bf16[2,192,384]{2,1,0:T(8,128)(2,1)S(1)}, bf16[2,192,384]{2,1,0:T(8,128)(2,1)S(1)}, u32[]{:S(2)}, u32[]{:S(2)}) collective-permute-start(bf16[2,192,384]{2,1,0:T(8,128)(2,1)S(1)} %get-tuple-element.230), channel_id=1, source_target_pairs={{0,8},{1,9},{2,10},{3,11},{4,12},{5,13},{6,14},{7,15},{8,0},{9,1},... | collective-permute-start | bytes 884744 | tf_op jit(solution)/shard_map/ppermute | solution.py:548
  159.4 15.3 %collective-permute-start.64 = (bf16[2,160,384]{2,1,0:T(8,128)(2,1)S(1)}, bf16[2,160,384]{2,1,0:T(8,128)(2,1)S(1)}, u32[]{:S(2)}, u32[]{:S(2)}) collective-permute-start(bf16[2,160,384]{2,1,0:T(8,128)(2,1)S(1)} %get-tuple-element.237), channel_id=1, source_target_pairs={{0,4},{1,5},{2,6},{3,7},{4,0},{5,1},{6,2},{7,3},{8,12},{9,13},{10,... | collective-permute-start | bytes 737288 | tf_op jit(solution)/shard_map/ppermute | solution.py:548
  160.6 14.1 %collective-permute-start.63 = (bf16[2,160,384]{2,1,0:T(8,128)(2,1)S(1)}, bf16[2,160,384]{2,1,0:T(8,128)(2,1)S(1)}, u32[]{:S(2)}, u32[]{:S(2)}) collective-permute-start(bf16[2,160,384]{2,1,0:T(8,128)(2,1)S(1)} %get-tuple-element.238), channel_id=1, source_target_pairs={{0,2},{1,3},{2,0},{3,1},{4,6},{5,7},{6,4},{7,5},{8,10},{9,11},{10,... | collective-permute-start | bytes 737288 | tf_op jit(solution)/shard_map/ppermute | solution.py:548
  161.8 11.6 %collective-permute-start.65 = (bf16[192,384]{1,0:T(8,128)(2,1)S(1)}, bf16[192,384]{1,0:T(8,128)(2,1)S(1)}, u32[]{:S(2)}, u32[]{:S(2)}) collective-permute-start(bf16[192,384]{1,0:T(8,128)(2,1)S(1)} %fusion.1), channel_id=1, source_target_pairs={{0,16},{1,17},{2,18},{3,19},{4,20},{5,21},{6,22},{7,23},{8,24},{9,... | collective-permute-start | bytes 442376 | tf_op jit(solution)/shard_map/ppermute | solution.py:548
  167.1 9.2 %collective-permute-start.62 = (bf16[2,5,48,384]{3,2,1,0:T(8,128)(2,1)S(1)}, bf16[2,5,48,384]{3,2,1,0:T(8,128)(2,1)S(1)}, u32[]{:S(2)}, u32[]{:S(2)}) collective-permute-start(bf16[2,5,48,384]{3,2,1,0:T(8,128)(2,1)S(1)} %get-tuple-element.224), channel_id=1, source_target_pairs={{0,4},{1,5},{2,6},{3,7},{4,0},{5,1},{6,2},{7,3},{8,12},{9,13},{10,... | collective-permute-start | bytes 1105928 | tf_op jit(solution)/shard_map/ppermute | solution.py:548
  168.0 9.2 %collective-permute-start.61 = (bf16[2,5,48,384]{3,2,1,0:T(8,128)(2,1)S(1)}, bf16[2,5,48,384]{3,2,1,0:T(8,128)(2,1)S(1)}, u32[]{:S(2)}, u32[]{:S(2)}) collective-permute-start(bf16[2,5,48,384]{3,2,1,0:T(8,128)(2,1)S(1)} %get-tuple-element.225), channel_id=1, source_target_pairs={{0,2},{1,3},{2,0},{3,1},{4,6},{5,7},{6,4},{7,5},{8,10},{9,11},{10,... | collective-permute-start | bytes 1105928 | tf_op jit(solution)/shard_map/ppermute | solution.py:548
  174.0 8.9 %collective-permute-start.69 = (bf16[2,160,384]{2,1,0:T(8,128)(2,1)S(1)}, bf16[2,160,384]{2,1,0:T(8,128)(2,1)S(1)}, u32[]{:S(2)}, u32[]{:S(2)}) collective-permute-start(bf16[2,160,384]{2,1,0:T(8,128)(2,1)S(1)} %get-tuple-element.236), channel_id=1, source_target_pairs={{0,2},{1,3},{2,0},{3,1},{4,6},{5,7},{6,4},{7,5},{8,10},{9,11},{10,... | collective-permute-start | bytes 737288 | tf_op jit(solution)/shard_map/ppermute | solution.py:548
  174.8 8.5 %collective-permute-start.70 = (bf16[2,160,384]{2,1,0:T(8,128)(2,1)S(1)}, bf16[2,160,384]{2,1,0:T(8,128)(2,1)S(1)}, u32[]{:S(2)}, u32[]{:S(2)}) collective-permute-start(bf16[2,160,384]{2,1,0:T(8,128)(2,1)S(1)} %add_convert_fusion.16), channel_id=1, source_target_pairs={{0,4},{1,5},{2,6},{3,7},{4,0},{5,1},{6,2},{7,3},{8,12},{9,13},{10,... | collective-permute-start | bytes 737288 | tf_op jit(solution)/shard_map/ppermute | solution.py:548
  178.5 10.8 %collective-permute-start.68 = (bf16[2,5,48,384]{3,2,1,0:T(8,128)(2,1)}, bf16[2,5,48,384]{3,2,1,0:T(8,128)(2,1)}, u32[]{:S(2)}, u32[]{:S(2)}) collective-permute-start(bf16[2,5,48,384]{3,2,1,0:T(8,128)(2,1)} %get-tuple-element.221), channel_id=1, source_target_pairs={{0,8},{1,9},{2,10},{3,11},{4,12},{5,13},{6,14},{7,15},{8,0},{9,1},... | collective-permute-start | bytes 1105928 | tf_op jit(solution)/shard_map/ppermute | solution.py:548
  180.1 12.3 %collective-permute-start.66 = (bf16[2,5,48,384]{3,2,1,0:T(8,128)(2,1)}, bf16[2,5,48,384]{3,2,1,0:T(8,128)(2,1)}, u32[]{:S(2)}, u32[]{:S(2)}) collective-permute-start(bf16[2,5,48,384]{3,2,1,0:T(8,128)(2,1)} %get-tuple-element.202), channel_id=1, source_target_pairs={{0,2},{1,3},{2,0},{3,1},{4,6},{5,7},{6,4},{7,5},{8,10},{9,11},{10,... | collective-permute-start | bytes 1105928 | tf_op jit(solution)/shard_map/ppermute | solution.py:548
  182.5 10.5 %collective-permute-start.67 = (bf16[2,5,48,384]{3,2,1,0:T(8,128)(2,1)}, bf16[2,5,48,384]{3,2,1,0:T(8,128)(2,1)}, u32[]{:S(2)}, u32[]{:S(2)}) collective-permute-start(bf16[2,5,48,384]{3,2,1,0:T(8,128)(2,1)} %get-tuple-element.203), channel_id=1, source_target_pairs={{0,4},{1,5},{2,6},{3,7},{4,0},{5,1},{6,2},{7,3},{8,12},{9,13},{10,... | collective-permute-start | bytes 1105928 | tf_op jit(solution)/shard_map/ppermute | solution.py:548
  184.3 8.1 %collective-permute-start.71 = (bf16[2,160,384]{2,1,0:T(8,128)(2,1)}, bf16[2,160,384]{2,1,0:T(8,128)(2,1)S(1)}, u32[]{:S(2)}, u32[]{:S(2)}) collective-permute-start(bf16[2,160,384]{2,1,0:T(8,128)(2,1)} %get-tuple-element.240), channel_id=1, source_target_pairs={{0,8},{1,9},{2,10},{3,11},{4,12},{5,13},{6,14},{7,15},{8,0},{9,1},... | collective-permute-start | bytes 737288 | tf_op jit(solution)/shard_map/ppermute | solution.py:548
  185.0 13.0 %collective-permute-start.73 = (bf16[2,160,384]{2,1,0:T(8,128)(2,1)}, bf16[2,160,384]{2,1,0:T(8,128)(2,1)S(1)}, u32[]{:S(2)}, u32[]{:S(2)}) collective-permute-start(bf16[2,160,384]{2,1,0:T(8,128)(2,1)} %get-tuple-element.208), channel_id=1, source_target_pairs={{0,2},{1,3},{2,0},{3,1},{4,6},{5,7},{6,4},{7,5},{8,10},{9,11},{10,... | collective-permute-start | bytes 737288 | tf_op jit(solution)/shard_map/ppermute | solution.py:548
  189.3 8.6 %collective-permute-start.74 = (bf16[2,160,384]{2,1,0:T(8,128)(2,1)}, bf16[2,160,384]{2,1,0:T(8,128)(2,1)S(1)}, u32[]{:S(2)}, u32[]{:S(2)}) collective-permute-start(bf16[2,160,384]{2,1,0:T(8,128)(2,1)} %get-tuple-element.209), channel_id=1, source_target_pairs={{0,4},{1,5},{2,6},{3,7},{4,0},{5,1},{6,2},{7,3},{8,12},{9,13},{10,... | collective-permute-start | bytes 737288 | tf_op jit(solution)/shard_map/ppermute | solution.py:548
  194.4 13.1 %collective-permute-start.72 = (bf16[5,48,384]{2,1,0:T(8,128)(2,1)S(1)}, bf16[5,48,384]{2,1,0:T(8,128)(2,1)S(1)}, u32[]{:S(2)}, u32[]{:S(2)}) collective-permute-start(bf16[5,48,384]{2,1,0:T(8,128)(2,1)S(1)} %fusion), channel_id=1, source_target_pairs={{0,16},{1,17},{2,18},{3,19},{4,20},{5,21},{6,22},{7,23},{8,24},{9,... | collective-permute-start | bytes 552968 | tf_op jit(solution)/shard_map/ppermute | solution.py:548
  199.1 9.7 %collective-permute-start.75 = (bf16[160,384]{1,0:T(8,128)(2,1)S(1)}, bf16[160,384]{1,0:T(8,128)(2,1)S(1)}, u32[]{:S(2)}, u32[]{:S(2)}) collective-permute-start(bf16[160,384]{1,0:T(8,128)(2,1)S(1)} %fusion.2), channel_id=1, source_target_pairs={{0,16},{1,17},{2,18},{3,19},{4,20},{5,21},{6,22},{7,23},{8,24},{9,... | collective-permute-start | bytes 368648 | tf_op jit(solution)/shard_map/ppermute | solution.py:548
  (88 other events, 1052.2 us)
